TPU v7x, 32 devices: a whole 2x2x4 slice. The times are simulated.
32 devices in a mesh: dp: 4 (over y, x), row: 2 (over core), col: 4 (over z).
Axes of the slice: x: 2, y: 2, z: 4, core: 2. Of those that a mesh axis runs over, the one named last changes fastest.
Arguments:
- tokens: bfloat16 [16384, 2048], P('dp', ('row', 'col')), may hold values from -6 to 6
- cotangent: bfloat16 [16384, 2048], P('dp', ('row', 'col')), may hold values from -6 to 6
- doc_lengths: int32 [8, 4], P(('dp', 'row')), may hold values from 1 to 1024, 2048 in all within a row
- qkv_weight: float32 [2048, 3, 2048], P('row', None, 'col'), may hold values from -0.198873782 to 0.198873782
- out_weight: float32 [2048, 2048], P('col', 'row'), may hold values from -0.198873782 to 0.198873782
- gate_weight: float32 [2048, 8192], P('row', 'col'), may hold values from -0.125 to 0.125
- up_weight: float32 [2048, 8192], P('row', 'col'), may hold values from -0.125 to 0.125
- down_weight: float32 [8192, 2048], P('col', 'row'), may hold values from -0.099436891 to 0.099436891
- head_gains: float32 [2, 2048], P(None, 'col'), may hold values from 0.5 to 1.5
- post_gains: float32 [2048, 2], P(('row', 'col')), may hold values from 0.5 to 1.5
- qkv_first: float32 [2048, 3, 2048], P(('row', 'dp'), None, 'col'), may hold values from -80 to 80
- qkv_second: float32 [2048, 3, 2048], P(('row', 'dp'), None, 'col'), may hold values from 491.52 to 6553.6
- out_first: float32 [2048, 2048], P(('col', 'dp'), 'row'), may hold values from -80 to 80
- out_second: float32 [2048, 2048], P(('col', 'dp'), 'row'), may hold values from 491.52 to 6553.6
- gate_first: float32 [2048, 8192], P(('row', 'dp'), 'col'), may hold values from -80 to 80
- gate_second: float32 [2048, 8192], P(('row', 'dp'), 'col'), may hold values from 491.52 to 6553.6
- up_first: float32 [2048, 8192], P(('row', 'dp'), 'col'), may hold values from -80 to 80
- up_second: float32 [2048, 8192], P(('row', 'dp'), 'col'), may hold values from 491.52 to 6553.6
- down_first: float32 [8192, 2048], P(('col', 'dp'), 'row'), may hold values from -80 to 80
- down_second: float32 [8192, 2048], P(('col', 'dp'), 'row'), may hold values from 491.52 to 6553.6
- head_first: float32 [2, 2048], P(None, 'col'), may hold values from -80 to 80
- head_second: float32 [2, 2048], P(None, 'col'), may hold values from 491.52 to 6553.6
- post_first: float32 [2048, 2], P(('row', 'col', 'dp')), may hold values from -80 to 80
- post_second: float32 [2048, 2], P(('row', 'col', 'dp')), may hold values from 491.52 to 6553.6
Outputs:
- mixed: bfloat16 [16384, 2048], P('dp', ('row', 'col'))
- dtokens: float32 [16384, 2048], P('dp', ('row', 'col'))
- qkv_first_new: float32 [2048, 3, 2048], P(('row', 'dp'), None, 'col')
- qkv_second_new: float32 [2048, 3, 2048], P(('row', 'dp'), None, 'col')
- qkv_weight_new: float32 [2048, 3, 2048], P(('row', 'dp'), None, 'col')
- out_first_new: float32 [2048, 2048], P(('col', 'dp'), 'row')
- out_second_new: float32 [2048, 2048], P(('col', 'dp'), 'row')
- out_weight_new: float32 [2048, 2048], P(('col', 'dp'), 'row')
- gate_first_new: float32 [2048, 8192], P(('row', 'dp'), 'col')
- gate_second_new: float32 [2048, 8192], P(('row', 'dp'), 'col')
- gate_weight_new: float32 [2048, 8192], P(('row', 'dp'), 'col')
- up_first_new: float32 [2048, 8192], P(('row', 'dp'), 'col')
- up_second_new: float32 [2048, 8192], P(('row', 'dp'), 'col')
- up_weight_new: float32 [2048, 8192], P(('row', 'dp'), 'col')
- down_first_new: float32 [8192, 2048], P(('col', 'dp'), 'row')
- down_second_new: float32 [8192, 2048], P(('col', 'dp'), 'row')
- down_weight_new: float32 [8192, 2048], P(('col', 'dp'), 'row')
- head_first_new: float32 [2, 2048], P(None, 'col')
- head_second_new: float32 [2, 2048], P(None, 'col')
- head_gains_new: float32 [2, 2048], P(None, 'col')
- post_first_new: float32 [2048, 2], P(('row', 'col', 'dp'))
- post_second_new: float32 [2048, 2], P(('row', 'col', 'dp'))
- post_gains_new: float32 [2048, 2], P(('row', 'col', 'dp'))
Inputs may be any that keep to these rules, and one draw needn't show every extreme that they name: `doc_lengths`: each row holds the lengths of its sequence's documents in order and sums to 2048.
All inputs are finite; a program needn't handle non-finite values.
Results may differ from a plain program's by a relative error of at most 0.023.
Values may be sent and summed in bfloat16 or wider, within the bound.
A program may use at most 512 MiB of HBM per device.

v0:
```python
import jax
import jax.numpy as jnp
from jax import lax
from jax.sharding import PartitionSpec as P

HD = 128
STEP = 10


norm_eps = 1e-06
rope_base = 500000.0
beta_one = 0.9
beta_two = 0.95
adam_eps = 1e-08
weight_decay = 0.1
rate_matrix = 0.02
rate_gain = 0.6
big_negative = -1e30


def segments(lengths, seq_len):
    doc_ends = jnp.cumsum(lengths, axis=1)
    places = jnp.arange(seq_len, dtype=jnp.int32)
    return jnp.sum((doc_ends[:, None, :] <= places[None, :, None]).astype(jnp.int32), axis=2)


def rotary(seq_len, head_size):
    half_width = head_size // 2
    freqs = rope_base ** (-(jnp.arange(half_width, dtype=jnp.float32) * 2.0) / head_size)
    angles = jnp.arange(seq_len, dtype=jnp.float32)[:, None] * freqs[None, :]
    return (jnp.cos(angles), jnp.sin(angles))


def rotate(values, cos_table, sin_table):
    half_width = values.shape[-1] // 2
    cos_part = cos_table[:, None, :]
    sin_part = sin_table[:, None, :]
    first_half = values[..., :half_width]
    second_half = values[..., half_width:]
    return jnp.concatenate(
        [
            first_half * cos_part - second_half * sin_part,
            second_half * cos_part + first_half * sin_part,
        ],
        axis=-1,
    )


def unrotate(gradient, cos_table, sin_table):
    half_width = gradient.shape[-1] // 2
    cos_part = cos_table[:, None, :]
    sin_part = sin_table[:, None, :]
    first_half = gradient[..., :half_width]
    second_half = gradient[..., half_width:]
    return jnp.concatenate(
        [
            first_half * cos_part + second_half * sin_part,
            second_half * cos_part - first_half * sin_part,
        ],
        axis=-1,
    )


def widen_cols(piece):
    return lax.all_gather(piece, "col", axis=1, tiled=True)


def narrow(partial_value):
    return lax.psum_scatter(partial_value, "col", scatter_dimension=1, tiled=True)


def row_total(partial_value):
    return lax.psum_scatter(partial_value, "row", scatter_dimension=0, tiled=True)


def row_join(piece):
    return lax.all_gather(piece, "row", axis=0, tiled=True)


def token_total(values):
    return lax.psum(values, ("row", "col"))


def head_total(values):
    return lax.psum(values, "col")


def post_norm(pre_vals, gains, model_width):
    scale = lax.rsqrt(token_total(jnp.sum(pre_vals * pre_vals, axis=1)) / model_width + norm_eps)
    return (pre_vals * scale[:, None] * gains[None, :], scale)


def post_norm_back(pre_vals, scale, gains, gradient, model_width):
    weighted = gradient * gains[None, :]
    inner = token_total(jnp.sum(weighted * pre_vals, axis=1)) / model_width
    grad_pre = scale[:, None] * weighted - pre_vals * (scale * scale * scale * inner)[:, None]
    grad_gain = jnp.sum(gradient * pre_vals * scale[:, None], axis=0)
    return (grad_pre, grad_gain)


def mask_rows(seg_ids, first_row, last_row):
    places = jnp.arange(last_row, dtype=jnp.int32)
    allowed = places[None, :] <= places[first_row:last_row, None]
    return allowed & (seg_ids[None, :last_row] == seg_ids[first_row:last_row, None])


def attend(query, key_rows, value_rows, seg_ids):
    seq_len = query.shape[0]
    block = min(512, seq_len)
    scale_attn = HD ** (-0.5)
    outs_list = []
    lse_list = []
    for block_idx in range(seq_len // block):
        first_row = block_idx * block
        last_row = first_row + block
        scores = (
            jnp.einsum(
                "qhd,khd->hqk",
                query[first_row:last_row],
                key_rows[:last_row],
                preferred_element_type=jnp.float32,
            )
            * scale_attn
        )
        scores = jnp.where(mask_rows(seg_ids, first_row, last_row)[None], scores, big_negative)
        row_max = jnp.max(scores, axis=-1, keepdims=True)
        exp_score = jnp.exp(scores - row_max)
        denom_sum = jnp.sum(exp_score, axis=-1, keepdims=True)
        attn_prob = (exp_score / denom_sum).astype(jnp.bfloat16)
        outs_list.append(
            jnp.einsum(
                "hqk,khd->qhd", attn_prob, value_rows[:last_row], preferred_element_type=jnp.float32
            )
        )
        lse_list.append((row_max + jnp.log(denom_sum))[..., 0])
    return (jnp.concatenate(outs_list, axis=0), jnp.concatenate(lse_list, axis=1))


def attend_back(query, key_rows, value_rows, seg_ids, grad_out, log_total):
    seq_len = query.shape[0]
    block = min(512, seq_len)
    scale_attn = HD ** (-0.5)
    grad_query = []
    grad_key = jnp.zeros(query.shape, jnp.float32)
    grad_value = jnp.zeros(query.shape, jnp.float32)
    for block_idx in range(seq_len // block):
        first_row = block_idx * block
        last_row = first_row + block
        scores = (
            jnp.einsum(
                "qhd,khd->hqk",
                query[first_row:last_row],
                key_rows[:last_row],
                preferred_element_type=jnp.float32,
            )
            * scale_attn
        )
        scores = jnp.where(mask_rows(seg_ids, first_row, last_row)[None], scores, big_negative)
        attn_prob = jnp.exp(scores - log_total[:, first_row:last_row, None])
        prob_low = attn_prob.astype(jnp.bfloat16)
        grad_prob = jnp.einsum(
            "qhd,khd->hqk",
            grad_out[first_row:last_row],
            value_rows[:last_row],
            preferred_element_type=jnp.float32,
        )
        delta = jnp.sum(attn_prob * grad_prob, axis=-1, keepdims=True)
        grad_score = (attn_prob * (grad_prob - delta)).astype(jnp.bfloat16)
        grad_query.append(
            jnp.einsum(
                "hqk,khd->qhd", grad_score, key_rows[:last_row], preferred_element_type=jnp.float32
            )
            * scale_attn
        )
        pad_rows = ((0, seq_len - last_row), (0, 0), (0, 0))
        key_part = (
            jnp.einsum(
                "hqk,qhd->khd",
                grad_score,
                query[first_row:last_row],
                preferred_element_type=jnp.float32,
            )
            * scale_attn
        )
        value_part = jnp.einsum(
            "hqk,qhd->khd",
            prob_low,
            grad_out[first_row:last_row],
            preferred_element_type=jnp.float32,
        )
        grad_key = grad_key + jnp.pad(key_part, pad_rows)
        grad_value = grad_value + jnp.pad(value_part, pad_rows)
    return (jnp.concatenate(grad_query, axis=0), grad_key, grad_value)


def adamw_step(weight, gradient, first_mom, second_mom, step_rate, decay_rate):
    first_new = beta_one * first_mom + (1.0 - beta_one) * gradient
    second_new = beta_two * second_mom + (1.0 - beta_two) * gradient * gradient
    fix_one = 1.0 - beta_one**STEP
    fix_two = 1.0 - beta_two**STEP
    direction = first_new / fix_one / (jnp.sqrt(second_new / fix_two) + adam_eps)
    return (first_new, second_new, weight - step_rate * (direction + decay_rate * weight))


def shards(
    tokens,
    cotangent,
    doc_lengths,
    qkv_weight,
    out_weight,
    gate_weight,
    up_weight,
    down_weight,
    head_gains,
    post_gains,
    qkv_first,
    qkv_second,
    out_first,
    out_second,
    gate_first,
    gate_second,
    up_first,
    up_second,
    down_first,
    down_second,
    head_first,
    head_second,
    post_first,
    post_second,
):
    n_row = lax.axis_size("row")
    n_col = lax.axis_size("col")
    model_width = tokens.shape[1] * n_row * n_col
    rows_dev = tokens.shape[0]
    half_rows = rows_dev // n_row
    n_seq = doc_lengths.shape[0]
    seq_len = half_rows // n_seq
    col_width = qkv_weight.shape[2]
    heads_dev = col_width // HD
    ff_dev = gate_weight.shape[1]
    seg_ids = segments(doc_lengths, seq_len)
    cos_table, sin_table = rotary(seq_len, HD)
    cos_all = jnp.tile(cos_table, (n_seq, 1))
    sin_all = jnp.tile(sin_table, (n_seq, 1))
    qkv_low = qkv_weight.astype(jnp.bfloat16).reshape(qkv_weight.shape[0], 3 * col_width)
    out_low = out_weight.astype(jnp.bfloat16)
    gate_up_low = jnp.concatenate(
        [gate_weight.astype(jnp.bfloat16), up_weight.astype(jnp.bfloat16)], axis=1
    )
    down_low = down_weight.astype(jnp.bfloat16)
    heads_shape = (n_seq, seq_len, heads_dev, HD)
    tok_cols = widen_cols(tokens)
    qkv = row_total(jnp.dot(tok_cols, qkv_low, preferred_element_type=jnp.float32))
    query_pre = qkv[:, :col_width]
    key_pre = qkv[:, col_width : 2 * col_width]
    value_val = qkv[:, 2 * col_width :]
    head_sums = head_total(
        jnp.stack(
            [jnp.sum(query_pre * query_pre, axis=1), jnp.sum(key_pre * key_pre, axis=1)], axis=1
        )
    )
    inv_scale = lax.rsqrt(head_sums / model_width + norm_eps)
    query_hat = query_pre * inv_scale[:, 0:1]
    key_hat = key_pre * inv_scale[:, 1:2]
    query_rot = rotate(
        (query_hat * head_gains[0][None, :]).reshape(half_rows, heads_dev, HD), cos_all, sin_all
    )
    key_rot = rotate(
        (key_hat * head_gains[1][None, :]).reshape(half_rows, heads_dev, HD), cos_all, sin_all
    )
    query_low = query_rot.astype(jnp.bfloat16).reshape(heads_shape)
    key_low = key_rot.astype(jnp.bfloat16).reshape(heads_shape)
    value_low = value_val.astype(jnp.bfloat16).reshape(heads_shape)
    att_out, log_total = lax.map(
        lambda packed: attend(*packed), (query_low, key_low, value_low, seg_ids)
    )
    att_low = att_out.reshape(half_rows, col_width).astype(jnp.bfloat16)
    att_full = row_join(att_low)
    a_pre = narrow(jnp.dot(att_full, out_low, preferred_element_type=jnp.float32))
    a_val, a_scale = post_norm(a_pre, post_gains[:, 0], model_width)
    h_val = tokens.astype(jnp.float32) + a_val
    h_cols = widen_cols(h_val.astype(jnp.bfloat16))
    gate_up_part = jnp.dot(h_cols, gate_up_low, preferred_element_type=jnp.float32)
    gate_up_all = lax.psum(gate_up_part, "row")
    hidden_full = (jax.nn.silu(gate_up_all[:, :ff_dev]) * gate_up_all[:, ff_dev:]).astype(
        jnp.bfloat16
    )
    gate_up_own = lax.dynamic_slice_in_dim(
        gate_up_all, lax.axis_index("row") * half_rows, half_rows, 0
    )
    m_pre = narrow(jnp.dot(hidden_full, down_low, preferred_element_type=jnp.float32))
    m_val, m_scale = post_norm(m_pre, post_gains[:, 1], model_width)
    mixed = (h_val + m_val).astype(jnp.bfloat16)
    back_vals = cotangent.astype(jnp.float32)
    grad_m_pre, grad_gain_mlp = post_norm_back(
        m_pre, m_scale, post_gains[:, 1], back_vals, model_width
    )
    grad_m_cols = widen_cols(grad_m_pre.astype(jnp.bfloat16))
    grad_down = jnp.einsum(
        "tf,td->fd", hidden_full, grad_m_cols, preferred_element_type=jnp.float32
    )
    grad_hidden = row_total(
        jnp.einsum("td,fd->tf", grad_m_cols, down_low, preferred_element_type=jnp.float32)
    )
    grad_hidden = lax.optimization_barrier(grad_hidden.astype(jnp.bfloat16)).astype(jnp.float32)
    gate_own = gate_up_own[:, :ff_dev]
    up_own = gate_up_own[:, ff_dev:]
    sigmoid_gate = jax.nn.sigmoid(gate_own)
    grad_gate = grad_hidden * up_own * sigmoid_gate * (1.0 + gate_own * (1.0 - sigmoid_gate))
    grad_up = grad_hidden * gate_own * sigmoid_gate
    grad_gate_up = row_join(jnp.concatenate([grad_gate, grad_up], axis=1).astype(jnp.bfloat16))
    grad_gate_up_w = jnp.einsum(
        "td,tf->df", h_cols, grad_gate_up, preferred_element_type=jnp.float32
    )
    grad_h = back_vals + narrow(
        jnp.einsum("tf,df->td", grad_gate_up, gate_up_low, preferred_element_type=jnp.float32)
    )
    grad_a_pre, grad_gain_attn = post_norm_back(
        a_pre, a_scale, post_gains[:, 0], grad_h, model_width
    )
    grad_a_cols = widen_cols(grad_a_pre.astype(jnp.bfloat16))
    grad_out_w = jnp.einsum("tc,td->cd", att_full, grad_a_cols, preferred_element_type=jnp.float32)
    grad_att = row_total(
        jnp.einsum("td,cd->tc", grad_a_cols, out_low, preferred_element_type=jnp.float32)
    )
    grad_att_low = grad_att.astype(jnp.bfloat16).reshape(heads_shape)
    grad_query, grad_key, grad_value = lax.map(
        lambda packed: attend_back(*packed),
        (query_low, key_low, value_low, seg_ids, grad_att_low, log_total),
    )
    grad_query_hat = unrotate(
        grad_query.reshape(half_rows, heads_dev, HD), cos_all, sin_all
    ).reshape(half_rows, col_width)
    grad_key_hat = unrotate(grad_key.reshape(half_rows, heads_dev, HD), cos_all, sin_all).reshape(
        half_rows, col_width
    )
    grad_head = jnp.stack(
        [jnp.sum(grad_query_hat * query_hat, axis=0), jnp.sum(grad_key_hat * key_hat, axis=0)],
        axis=0,
    )
    weighted_query = grad_query_hat * head_gains[0][None, :]
    weighted_key = grad_key_hat * head_gains[1][None, :]
    inner_sums = (
        head_total(
            jnp.stack(
                [
                    jnp.sum(weighted_query * query_pre, axis=1),
                    jnp.sum(weighted_key * key_pre, axis=1),
                ],
                axis=1,
            )
        )
        / model_width
    )
    cube_scale = inv_scale * inv_scale * inv_scale
    grad_query_pre = inv_scale[:, 0:1] * weighted_query - query_pre * (
        cube_scale[:, 0:1] * inner_sums[:, 0:1]
    )
    grad_key_pre = inv_scale[:, 1:2] * weighted_key - key_pre * (
        cube_scale[:, 1:2] * inner_sums[:, 1:2]
    )
    grad_qkv_own = jnp.concatenate(
        [grad_query_pre, grad_key_pre, grad_value.reshape(half_rows, col_width)], axis=1
    )
    grad_qkv = row_join(grad_qkv_own.astype(jnp.bfloat16))
    grad_qkv_w = jnp.einsum(
        "td,tc->dc", tok_cols, grad_qkv, preferred_element_type=jnp.float32
    ).reshape(qkv_weight.shape)
    dtokens = grad_h + narrow(
        jnp.einsum("tc,dc->td", grad_qkv, qkv_low, preferred_element_type=jnp.float32)
    )
    grad_post = jnp.stack([grad_gain_attn, grad_gain_mlp], axis=1)
    summed = (
        lax.psum_scatter(
            grad_qkv_w.astype(jnp.bfloat16), "dp", scatter_dimension=0, tiled=True
        ).astype(jnp.float32),
        lax.psum_scatter(
            grad_out_w.astype(jnp.bfloat16), "dp", scatter_dimension=0, tiled=True
        ).astype(jnp.float32),
        lax.psum_scatter(
            grad_gate_up_w[:, :ff_dev].astype(jnp.bfloat16), "dp", scatter_dimension=0, tiled=True
        ).astype(jnp.float32),
        lax.psum_scatter(
            grad_gate_up_w[:, ff_dev:].astype(jnp.bfloat16), "dp", scatter_dimension=0, tiled=True
        ).astype(jnp.float32),
        lax.psum_scatter(
            grad_down.astype(jnp.bfloat16), "dp", scatter_dimension=0, tiled=True
        ).astype(jnp.float32),
        lax.psum_scatter(
            grad_post.astype(jnp.bfloat16), "dp", scatter_dimension=0, tiled=True
        ).astype(jnp.float32),
    )
    head_summed = lax.psum(grad_head, ("dp", "row"))
    dp_index = lax.axis_index("dp")

    def owned_rows(weight, part_rows):
        return lax.dynamic_slice_in_dim(weight, dp_index * part_rows, part_rows, 0)

    qkv_res = adamw_step(
        owned_rows(qkv_weight, summed[0].shape[0]),
        summed[0],
        qkv_first,
        qkv_second,
        rate_matrix,
        weight_decay,
    )
    out_res = adamw_step(
        owned_rows(out_weight, summed[1].shape[0]),
        summed[1],
        out_first,
        out_second,
        rate_matrix,
        weight_decay,
    )
    gate_res = adamw_step(
        owned_rows(gate_weight, summed[2].shape[0]),
        summed[2],
        gate_first,
        gate_second,
        rate_matrix,
        weight_decay,
    )
    up_res = adamw_step(
        owned_rows(up_weight, summed[3].shape[0]),
        summed[3],
        up_first,
        up_second,
        rate_matrix,
        weight_decay,
    )
    down_res = adamw_step(
        owned_rows(down_weight, summed[4].shape[0]),
        summed[4],
        down_first,
        down_second,
        rate_matrix,
        weight_decay,
    )
    head_res = adamw_step(head_gains, head_summed, head_first, head_second, rate_gain, 0.0)
    post_res = adamw_step(
        owned_rows(post_gains, summed[5].shape[0]),
        summed[5],
        post_first,
        post_second,
        rate_gain,
        0.0,
    )
    return (
        mixed,
        dtokens,
        qkv_res[0],
        qkv_res[1],
        qkv_res[2],
        out_res[0],
        out_res[1],
        out_res[2],
        gate_res[0],
        gate_res[1],
        gate_res[2],
        up_res[0],
        up_res[1],
        up_res[2],
        down_res[0],
        down_res[1],
        down_res[2],
        head_res[0],
        head_res[1],
        head_res[2],
        post_res[0],
        post_res[1],
        post_res[2],
    )


def solution(mesh):
    in_specs = (
        P("dp", ("row", "col")),
        P("dp", ("row", "col")),
        P(("dp", "row"), None),
        P("row", None, "col"),
        P("col", "row"),
        P("row", "col"),
        P("row", "col"),
        P("col", "row"),
        P(None, "col"),
        P(("row", "col"), None),
        P(("row", "dp"), None, "col"),
        P(("row", "dp"), None, "col"),
        P(("col", "dp"), "row"),
        P(("col", "dp"), "row"),
        P(("row", "dp"), "col"),
        P(("row", "dp"), "col"),
        P(("row", "dp"), "col"),
        P(("row", "dp"), "col"),
        P(("col", "dp"), "row"),
        P(("col", "dp"), "row"),
        P(None, "col"),
        P(None, "col"),
        P(("row", "col", "dp"), None),
        P(("row", "col", "dp"), None),
    )
    out_specs = (
        P("dp", ("row", "col")),
        P("dp", ("row", "col")),
        P(("row", "dp"), None, "col"),
        P(("row", "dp"), None, "col"),
        P(("row", "dp"), None, "col"),
        P(("col", "dp"), "row"),
        P(("col", "dp"), "row"),
        P(("col", "dp"), "row"),
        P(("row", "dp"), "col"),
        P(("row", "dp"), "col"),
        P(("row", "dp"), "col"),
        P(("row", "dp"), "col"),
        P(("row", "dp"), "col"),
        P(("row", "dp"), "col"),
        P(("col", "dp"), "row"),
        P(("col", "dp"), "row"),
        P(("col", "dp"), "row"),
        P(None, "col"),
        P(None, "col"),
        P(None, "col"),
        P(("row", "col", "dp"), None),
        P(("row", "col", "dp"), None),
        P(("row", "col", "dp"), None),
    )
    return jax.shard_map(shards, mesh=mesh, in_specs=in_specs, out_specs=out_specs, check_vma=False)
```

profile of v0, /device:TPU:0, one launch (start us, length us, event | category | flops | bytes accessed | tf_op | source)
XLA Modules:
  0.0 3068.5 jit_solution(4839502244718856692)
XLA Ops:
  12.0 149.5 %all-gather.8.cloned.1.call-done = bf16[4096,1024]{1,0:T(8,128)(2,1)} async-done(((bf16[4096,256]{1,0:T(8,128)(2,1)}), bf16[4096,1024]{1,0:T(8,128)(2,1)}) %all-gather.8.cloned.1.call-update) | async-done | bytes 8388624 | tf_op jit(solution)/shard_map/all_gather | solution.py:65
  161.5 20.3 fusion.170
  192.7 22.9 reduce-scatter.16.cloned.1.call-done
  219.7 19.2 psum.56
  239.6 6.0 multiply_multiply_fusion
  278.6 8.3 convert.59
  313.2 8.3 fusion.166
  321.5 8.1 fusion.6
  330.2 8.4 fusion.96
  340.4 11.9 all-gather.10.cloned.1.call-done
  352.3 10.3 fusion.121
  363.9 280.4 %reduce-scatter.18.cloned.1.call-done = f32[4096,256]{1,0:T(8,128)} async-done(((f32[4096,1024]{1,0:T(8,128)}), f32[4096,256]{1,0:T(8,128)}) %reduce-scatter.18.cloned.1.call-update) | async-done | bytes 4194320 | tf_op jit(solution)/shard_map/reduce_scatter | solution.py:69
  647.1 28.5 psum.57
  679.9 6.2 convert_element_type.169
  686.1 6.8 convert_element_type.170
  692.9 134.7 %all-gather.12.cloned.1.call-done = bf16[4096,1024]{1,0:T(8,128)(2,1)} async-done(((bf16[4096,256]{1,0:T(8,128)(2,1)}), bf16[4096,1024]{1,0:T(8,128)(2,1)}) %all-gather.12.cloned.1.call-update) | async-done | bytes 8388624 | tf_op jit(solution)/shard_map/all_gather | solution.py:65
  827.6 45.9 %fusion.21 = f32[4096,4096]{1,0:T(8,128)} fusion(bf16[4096,1024]{1,0:T(8,128)(2,1)} %all-gather.12.cloned.1.call-done, bf16[1024,2048]{1,0:T(8,128)(2,1)} %convert_element_type.170, bf16[1024,2048]{1,0:T(8,128)(2,1)} %convert_element_type.169), kind=kOutput, calls=%fused_computation.48 | convolution fusion | flops 34376515584 | bytes 83886080 | tf_op jit(solution)/shard_map/dot_general | solution.py:283
  873.6 187.7 %all-reduce.8.cloned.1.call-done = f32[4096,4096]{1,0:T(8,128)} async-done(((f32[4096,4096]{1,0:T(8,128)}), f32[4096,4096]{1,0:T(8,128)}) %all-reduce.8.cloned.1.call-update) | async-done | bytes 67108880 | tf_op jit(solution)/shard_map/psum | solution.py:284
  1061.3 27.7 fusion
  1089.0 24.6 fusion.61
  1113.8 281.7 %reduce-scatter.20.cloned.1.call-done = f32[4096,256]{1,0:T(8,128)} async-done(((f32[4096,1024]{1,0:T(8,128)}), f32[4096,256]{1,0:T(8,128)}) %reduce-scatter.20.cloned.1.call-update) | async-done | bytes 4194320 | tf_op jit(solution)/shard_map/reduce_scatter | solution.py:69
  1398.3 28.5 psum.59
  1430.5 26.1 psum.60
  1460.5 149.0 %all-gather.14.cloned.1.call-done = bf16[4096,1024]{1,0:T(8,128)(2,1)} async-done(((bf16[4096,256]{1,0:T(8,128)(2,1)}), bf16[4096,1024]{1,0:T(8,128)(2,1)}) %all-gather.14.cloned.1.call-update) | async-done | bytes 8388624 | tf_op jit(solution)/shard_map/all_gather | solution.py:65
  1609.5 26.8 fusion.59
  1636.3 43.4 %reduce-scatter.22.cloned.1.call-done = f32[2048,2048]{1,0:T(8,128)} async-done(((f32[4096,2048]{1,0:T(8,128)}), f32[2048,2048]{1,0:T(8,128)}) %reduce-scatter.22.cloned.1.call-update) | async-done | bytes 16777232 | tf_op jit(solution)/shard_map/reduce_scatter | solution.py:73
  1679.8 6.6 convert_element_type.176
  1686.3 16.3 fusion.3
  1702.7 10.4 pad_maximum_fusion
  1713.2 52.5 %all-gather.16.cloned.1.call-done = bf16[4096,4096]{1,0:T(8,128)(2,1)} async-done(((bf16[2048,4096]{1,0:T(8,128)(2,1)}), bf16[4096,4096]{1,0:T(8,128)(2,1)}) %all-gather.16.cloned.1.call-update) | async-done | bytes 33554448 | tf_op jit(solution)/shard_map/all_gather | solution.py:77
  1765.7 43.7 %fusion.20 = f32[4096,1024]{1,0:T(8,128)} fusion(bf16[4096,4096]{1,0:T(8,128)(2,1)} %all-gather.16.cloned.1.call-done, bf16[1024,2048]{1,0:T(8,128)(2,1)} %convert_element_type.170, bf16[1024,2048]{1,0:T(8,128)(2,1)} %convert_element_type.169), kind=kOutput, calls=%fused_computation.47 | convolution fusion | flops 34376515584 | bytes 58720256 | tf_op jit(solution)/shard_map/tf,df->td/dot_general | solution.py:316
  1809.5 281.6 %reduce-scatter.24.cloned.1.call-done = f32[4096,256]{1,0:T(8,128)} async-done(((f32[4096,1024]{1,0:T(8,128)}), f32[4096,256]{1,0:T(8,128)}) %reduce-scatter.24.cloned.1.call-update) | async-done | bytes 4194320 | tf_op jit(solution)/shard_map/reduce_scatter | solution.py:69
  2095.8 28.5 psum.61
  2124.3 8.7 subtract_convert_fusion.2
  2133.3 147.5 %all-gather.18.cloned.1.call-done = bf16[4096,1024]{1,0:T(8,128)(2,1)} async-done(((bf16[4096,256]{1,0:T(8,128)(2,1)}), bf16[4096,1024]{1,0:T(8,128)(2,1)}) %all-gather.18.cloned.1.call-update) | async-done | bytes 8388624 | tf_op jit(solution)/shard_map/all_gather | solution.py:65
  2280.8 11.8 fusion.119
  2293.4 14.4 reduce-scatter.26.cloned.1.call-done
  2323.9 6.5 fusion.67
  2345.0 8.7 fusion.41
  2353.7 9.5 multiply_reduce_fusion.1
  2363.2 6.9 multiply_convert_fusion.1
  2377.5 12.7 multiply_reduce_fusion
  2390.3 7.5 fusion.33
  2400.3 12.4 multiply_convert_fusion
  2424.3 10.3 multiply_add_fusion.1
  2434.7 8.2 fusion.32
  2442.9 19.0 psum.62
  2462.0 10.1 subtract_convert_fusion.1
  2475.2 24.8 convolution_convert_fusion.1
  2500.1 41.9 %convolution_convert_fusion = bf16[1024,4096]{1,0:T(8,128)(2,1)S(1)} fusion(bf16[4096,1024]{1,0:T(8,128)(2,1)} %all-gather.12.cloned.1.call-done, bf16[4096,4096]{1,0:T(8,128)(2,1)} %all-gather.16.cloned.1.call-done), kind=kOutput, calls=%fused_computation.37 | convolution fusion | flops 34363932672 | bytes 50331648 | tf_op jit(solution)/shard_map/td,tf->df/dot_general | solution.py:312
  2547.4 10.2 convolution_convert_fusion.3
  2557.7 18.2 convolution_convert_fusion.2
  2579.0 19.4 fusion.171
  2600.0 6.4 multiply_subtract_fusion.2
  2610.9 7.1 multiply_subtract_fusion.4
  2618.0 48.9 %reduce-scatter.36.cloned.1.call-done = bf16[256,2048]{1,0:T(8,128)(2,1)} async-done(((bf16[1024,2048]{1,0:T(8,128)(2,1)}), bf16[256,2048]{1,0:T(8,128)(2,1)}) %reduce-scatter.36.cloned.1.call-update) | async-done | bytes 1048592 | tf_op jit(solution)/shard_map/reduce_scatter | solution.py:383
  2667.0 6.4 multiply_subtract_fusion.3
  2673.4 20.7 reduce-scatter.40.cloned.1.call-done
  2695.5 29.8 reduce-scatter.32.cloned.1.call-done
  2727.8 12.9 psum.63
  2741.4 31.1 %reduce-scatter.30.cloned.1.call-done = bf16[256,3,512]{2,0,1:T(8,128)(2,1)} async-done(((bf16[1024,3,512]{2,0,1:T(8,128)(2,1)}), bf16[256,3,512]{2,0,1:T(8,128)(2,1)}) %reduce-scatter.30.cloned.1.call-update) | async-done | bytes 786448 | tf_op jit(solution)/shard_map/reduce_scatter | solution.py:374
  2772.5 5.6 multiply_subtract_fusion.5
  2778.1 277.2 %reduce-scatter.28.cloned.1.call-done = f32[4096,256]{1,0:T(8,128)} async-done(((f32[4096,1024]{1,0:T(8,128)}), f32[4096,256]{1,0:T(8,128)}) %reduce-scatter.28.cloned.1.call-update) | async-done | bytes 4194320 | tf_op jit(solution)/shard_map/reduce_scatter | solution.py:69
  3055.3 6.2 fusion.125
  (343 shorter events, 180.7 us)
Async XLA Ops:
  7.2 154.3 %all-gather.8.cloned.1.call-start = ((), (), s32[]{:S(2)}) async-start(), calls=%async_computation.13 | async-start | bytes 10485760 | tf_op jit(solution)/shard_map/all_gather | solution.py:65
  7.9 207.6 %reduce-scatter.16.cloned.1.call-start = ((), (), s32[]{:S(2)}) async-start(), calls=%async_computation.14 | async-start | bytes 37748736 | tf_op jit(solution)/shard_map/reduce_scatter | solution.py:73
  12.0 169.7 %copy-start.40 = (bf16[1024,3,512]{0,2,1:T(8,128)(2,1)}, bf16[1024,3,512]{0,2,1:T(8,128)(2,1)S(1)}, u32[]{:S(2)}) copy-start(bf16[1024,3,512]{0,2,1:T(8,128)(2,1)S(1)} %copy.181) | copy-start | bytes 9437188
  181.7 170.6 %all-gather.10.cloned.1.call-start = ((), (), s32[]{:S(2)}) async-start(), calls=%async_computation.15 | async-start | bytes 6291456 | tf_op jit(solution)/shard_map/all_gather | solution.py:77
  182.7 56.8 %copy-start.75 = (f32[1,512]{1,0:T(1,128)}, f32[1,512]{1,0:T(1,128)S(1)}, u32[]{:S(2)}) copy-start(f32[1,512]{1,0:T(1,128)S(1)} %get-tuple-element.147) | copy-start | bytes 6148
  182.8 56.8 %copy-start.77 = (f32[1,512]{1,0:T(1,128)}, f32[1,512]{1,0:T(1,128)S(1)}, u32[]{:S(2)}) copy-start(f32[1,512]{1,0:T(1,128)S(1)} %get-tuple-element.148) | copy-start | bytes 6148
  267.9 32.1 %copy-start.1 = (bf16[2048,4,64]{2,0,1:T(8,128)(2,1)}, bf16[2048,4,64]{2,0,1:T(8,128)(2,1)S(1)}, u32[]{:S(2)}) copy-start(bf16[2048,4,64]{2,0,1:T(8,128)(2,1)S(1)} %get-tuple-element.135) | copy-start | bytes 3145732
  274.8 20.8 copy-start.60
  276.0 10.9 copy-start.62
  278.6 17.0 slice-start.3
  338.7 13.6 copy-start.57
  340.4 304.0 %reduce-scatter.18.cloned.1.call-start = ((), (), s32[]{:S(2)}) async-start(), calls=%async_computation.16 | async-start | bytes 20971520 | tf_op jit(solution)/shard_map/reduce_scatter | solution.py:69
  362.7 313.6 %copy-start.25 = (bf16[4096,256]{1,0:T(8,128)(2,1)S(1)}, bf16[4096,256]{1,0:T(8,128)(2,1)}, u32[]{:S(2)}) copy-start(bf16[4096,256]{1,0:T(8,128)(2,1)} %param.24) | copy-start | bytes 6291460
  362.7 464.9 %all-gather.12.cloned.1.call-start = ((), (), s32[]{:S(2)}) async-start(), calls=%async_computation.17 | async-start | bytes 10485760 | tf_op jit(solution)/shard_map/all_gather | solution.py:65
  363.9 315.9 %copy-start.79 = (f32[256,1]{0,1:T(1,128)}, f32[256,1]{0,1:T(1,128)S(1)}, u32[]{:S(2)}) copy-start(f32[256,1]{0,1:T(1,128)S(1)} %get-tuple-element.150) | copy-start | bytes 3076
  679.9 381.4 %all-reduce.8.cloned.1.call-start = ((), (), s32[]{:S(2)}) async-start(), calls=%async_computation.18 | async-start | bytes 134217728 | tf_op jit(solution)/shard_map/psum | solution.py:284
  873.6 521.9 %reduce-scatter.20.cloned.1.call-start = ((), (), s32[]{:S(2)}) async-start(), calls=%async_computation.19 | async-start | bytes 20971520 | tf_op jit(solution)/shard_map/reduce_scatter | solution.py:69
  1113.7 313.1 %copy-start.10 = (bf16[4096,256]{1,0:T(8,128)(2,1)S(1)}, bf16[4096,256]{1,0:T(8,128)(2,1)}, u32[]{:S(2)}) copy-start(bf16[4096,256]{1,0:T(8,128)(2,1)} %param.25) | copy-start | bytes 6291460
  1113.7 313.1 %copy-start.83 = (f32[256,1]{0,1:T(1,128)S(1)}, f32[256,1]{0,1:T(1,128)}, u32[]{:S(2)}) copy-start(f32[256,1]{0,1:T(1,128)} %get-tuple-element.149) | copy-start | bytes 3076
  1113.7 495.8 %all-gather.14.cloned.1.call-start = ((), (), s32[]{:S(2)}) async-start(), calls=%async_computation.20 | async-start | bytes 10485760 | tf_op jit(solution)/shard_map/all_gather | solution.py:65
  1460.5 219.3 %reduce-scatter.22.cloned.1.call-start = ((), (), s32[]{:S(2)}) async-start(), calls=%async_computation.21 | async-start | bytes 50331648 | tf_op jit(solution)/shard_map/reduce_scatter | solution.py:73
  1636.2 129.5 %all-gather.16.cloned.1.call-start = ((), (), s32[]{:S(2)}) async-start(), calls=%async_computation.22 | async-start | bytes 50331648 | tf_op jit(solution)/shard_map/all_gather | solution.py:77
  1713.1 378.0 %reduce-scatter.24.cloned.1.call-start = ((), (), s32[]{:S(2)}) async-start(), calls=%async_computation.23 | async-start | bytes 20971520 | tf_op jit(solution)/shard_map/reduce_scatter | solution.py:69
  1809.4 281.7 %copy-start.50 = (f32[4096]{0:T(1024)S(1)}, f32[4096]{0:T(1024)}, u32[]{:S(2)}) copy-start(f32[4096]{0:T(1024)} %copy-done.49) | copy-start | bytes 49156
  1809.4 281.7 %copy-start.80 = (f32[256,1]{0,1:T(1,128)S(1)}, f32[256,1]{0,1:T(1,128)}, u32[]{:S(2)}) copy-start(f32[256,1]{0,1:T(1,128)} %copy-done.79) | copy-start | bytes 3076
  1809.4 314.8 %copy-start.52 = (f32[4096]{0:T(1024)S(1)}, f32[4096]{0:T(1024)}, u32[]{:S(2)}) copy-start(f32[4096]{0:T(1024)} %copy-done.51) | copy-start | bytes 49156
  1809.4 471.3 %all-gather.18.cloned.1.call-start = ((), (), s32[]{:S(2)}) async-start(), calls=%async_computation.24 | async-start | bytes 10485760 | tf_op jit(solution)/shard_map/all_gather | solution.py:65
  2133.0 174.8 %reduce-scatter.26.cloned.1.call-start = ((), (), s32[]{:S(2)}) async-start(), calls=%async_computation.25 | async-start | bytes 12582912 | tf_op jit(solution)/shard_map/reduce_scatter | solution.py:73
  2292.7 265.0 %all-gather.20.cloned.1.call-start = ((), (), s32[]{:S(2)}) async-start(), calls=%async_computation.26 | async-start | bytes 18874368 | tf_op jit(solution)/shard_map/all_gather | solution.py:77
  2323.9 12.1 slice-start.5
  2345.0 18.2 slice-start
  2345.0 18.2 slice-start.1
  2353.7 9.5 slice-start.2
  2377.5 12.7 copy-start.27
  2377.5 12.7 copy-start.31
  2377.5 12.7 copy-start.36
  2400.3 12.4 copy-start.17
  2400.3 12.5 copy-start.23
  2419.6 15.0 slice-start.7
  2424.2 10.3 slice-start.8
  2424.2 10.3 slice-start.9
  2424.3 10.3 copy-start.54
  2424.3 10.3 copy-start.56
  2424.3 10.3 copy-start.76
  2424.3 10.3 copy-start.78
  2434.7 27.3 copy-start.64
  2462.0 10.1 copy-start.32
  2475.1 123.3 %reduce-scatter.38.cloned.1.call-start = ((), (), s32[]{:S(2)}) async-start(), calls=%async_computation.32 | async-start | bytes 5242880 | tf_op jit(solution)/shard_map/reduce_scatter | solution.py:386
  2500.0 110.8 %reduce-scatter.34.cloned.1.call-start = ((), (), s32[]{:S(2)}) async-start(), calls=%async_computation.30 | async-start | bytes 5242880 | tf_op jit(solution)/shard_map/reduce_scatter | solution.py:380
  2545.7 121.3 %reduce-scatter.36.cloned.1.call-start = ((), (), s32[]{:S(2)}) async-start(), calls=%async_computation.31 | async-start | bytes 5242880 | tf_op jit(solution)/shard_map/reduce_scatter | solution.py:383
  2546.3 147.8 %reduce-scatter.40.cloned.1.call-start = ((), (), s32[]{:S(2)}) async-start(), calls=%async_computation.33 | async-start | bytes 81920
  2547.2 178.1 %reduce-scatter.32.cloned.1.call-start = ((), (), s32[]{:S(2)}) async-start(), calls=%async_computation.29 | async-start | bytes 1310720 | tf_op jit(solution)/shard_map/reduce_scatter | solution.py:377
  2557.6 214.8 %reduce-scatter.30.cloned.1.call-start = ((), (), s32[]{:S(2)}) async-start(), calls=%async_computation.28 | async-start | bytes 3932160 | tf_op jit(solution)/shard_map/reduce_scatter | solution.py:374
  2579.0 476.3 %reduce-scatter.28.cloned.1.call-start = ((), (), s32[]{:S(2)}) async-start(), calls=%async_computation.27 | async-start | bytes 20971520 | tf_op jit(solution)/shard_map/reduce_scatter | solution.py:69
  2606.4 60.6 %copy-start.43 = (f32[256,2048]{1,0:T(8,128)S(1)}, f32[256,2048]{1,0:T(8,128)}, u32[]{:S(2)}) copy-start(f32[256,2048]{1,0:T(8,128)} %param.41) | copy-start | bytes 6291460
  2618.0 76.9 %copy-start.85 = (f32[256,2]{0,1:T(2,128)S(1)}, f32[256,2]{0,1:T(2,128)}, u32[]{:S(2)}) copy-start(f32[256,2]{0,1:T(2,128)} %param.33) | copy-start | bytes 6148
  2618.0 76.9 %copy-start.88 = (f32[64,2]{0,1:T(2,128)S(1)}, f32[64,2]{0,1:T(2,128)}, u32[]{:S(2)}) copy-start(f32[64,2]{0,1:T(2,128)} %param.47) | copy-start | bytes 1540
  2618.0 76.9 %copy-start.89 = (f32[64,2]{0,1:T(2,128)S(1)}, f32[64,2]{0,1:T(2,128)}, u32[]{:S(2)}) copy-start(f32[64,2]{0,1:T(2,128)} %param.46) | copy-start | bytes 1540
  2618.0 107.3 %copy-start.45 = (f32[128,1024]{1,0:T(8,128)S(1)}, f32[128,1024]{1,0:T(8,128)}, u32[]{:S(2)}) copy-start(f32[128,1024]{1,0:T(8,128)} %param.37) | copy-start | bytes 1572868
  2618.0 107.3 %copy-start.46 = (f32[128,1024]{1,0:T(8,128)S(1)}, f32[128,1024]{1,0:T(8,128)}, u32[]{:S(2)}) copy-start(f32[128,1024]{1,0:T(8,128)} %param.36) | copy-start | bytes 1572868
  2618.0 122.7 %copy-start.82 = (f32[2,512]{1,0:T(2,128)S(1)}, f32[2,512]{1,0:T(2,128)}, u32[]{:S(2)}) copy-start(f32[2,512]{1,0:T(2,128)} %param.32) | copy-start | bytes 12292
  2618.0 122.7 %copy-start.86 = (f32[2,512]{1,0:T(2,128)S(1)}, f32[2,512]{1,0:T(2,128)}, u32[]{:S(2)}) copy-start(f32[2,512]{1,0:T(2,128)} %param.45) | copy-start | bytes 12292
  2618.0 122.7 %copy-start.87 = (f32[2,512]{1,0:T(2,128)S(1)}, f32[2,512]{1,0:T(2,128)}, u32[]{:S(2)}) copy-start(f32[2,512]{1,0:T(2,128)} %param.44) | copy-start | bytes 12292
  2741.4 313.9 %copy-start.11 = (bf16[4096,256]{1,0:T(8,128)(2,1)S(1)}, bf16[4096,256]{1,0:T(8,128)(2,1)}, u32[]{:S(2)}) copy-start(bf16[4096,256]{1,0:T(8,128)(2,1)} %param.25) | copy-start | bytes 6291460
  (60 other events, 211.7 us)
Sparse Core Ops, SparseCore 0:
  9.6 151.8 all-gather.7
  181.9 33.6 reduce-scatter.15
  340.5 11.7 all-gather.9
  362.8 281.4 reduce-scatter.17
  680.0 147.5 all-gather.11
  873.7 187.5 all-reduce.7
  1113.8 281.6 reduce-scatter.19
  1460.6 148.8 all-gather.13
  1636.4 43.3 reduce-scatter.21
  1713.2 52.4 all-gather.15
  1809.6 281.4 reduce-scatter.23
  2133.2 147.5 all-gather.17
  2292.8 14.9 reduce-scatter.25
  2475.3 23.0 all-gather.19
  2501.2 53.8 reduce-scatter.37
  2558.1 52.6 reduce-scatter.33
  2614.3 52.6 reduce-scatter.35
  2670.3 23.6 reduce-scatter.39
  2697.5 27.7 reduce-scatter.31
  2728.4 44.0 reduce-scatter.29
  2775.0 280.2 reduce-scatter.27
where the time goes:
time: 3080 us; the launch traced here: 3070 us
  waiting for transfers between devices  2170 us (70%)
  matrix products  417 us (14%)
  other arithmetic  252 us (8%)
  blocking collectives  163 us (5%)
  local copies, waits for them, and re-layouts  48.4 us (2%)
    reduce_scatter x4, waiting for transfers between devices, narrow(): lax.psum_scatter(partial_value, 'col', scatter_dimension=1, tiled=True)  1120 us
    all_gather x4, waiting for transfers between devices, widen_cols(): return lax.all_gather(piece, 'col', axis=1, tiled=True)  581 us
    psum x1, waiting for transfers between devices, shards(): gate_up_all = lax.psum(gate_up_part, 'row')  188 us
    psum x4, blocking collectives, token_total(): return lax.psum(values, ('row', 'col'))  112 us
    reduce_scatter x3, waiting for transfers between devices, row_total(): lax.psum_scatter(partial_value, 'row', scatter_dimension=0, tiled=True)  80.7 us
    all_gather x3, waiting for transfers between devices, row_join(): return lax.all_gather(piece, 'row', axis=0, tiled=True)  64.5 us
  transfers between devices with their start and end apart: 21, of which 19 were waited for; matrix products, arithmetic and copies ran while one was open for 6% of the time, Pallas kernels for 0%

commit v1 on v0

v1 whole, which is shorter than its diff:
```python
import functools

import jax
import jax.numpy as jnp
from jax import lax
from jax.experimental import pallas as pl
from jax.experimental.pallas import tpu as pltpu
from jax.sharding import Mesh
from jax.sharding import PartitionSpec as P

HD = 128
STEP = 10

norm_eps = 1e-06
rope_base = 500000.0
beta_one = 0.9
beta_two = 0.95
adam_eps = 1e-08
weight_decay = 0.1
rate_matrix = 0.02
rate_gain = 0.6
big_negative = -1e30
log2_e = 1.4426950408889634

f32 = jnp.float32
bf16 = jnp.bfloat16
NN = (((1,), (0,)), ((), ()))
NT = (((1,), (1,)), ((), ()))
TN = (((0,), (0,)), ((), ()))


def swap(piece, axis):
    return lax.ppermute(piece, axis, [(0, 1), (1, 0)])


def shift(piece, axis, step):
    size = lax.axis_size(axis)
    return lax.ppermute(piece, axis, [(i, (i + step) % size) for i in range(size)])


def swap_bit(piece, axis, bit):
    return lax.ppermute(piece, axis, [(i, i ^ bit) for i in range(lax.axis_size(axis))])


def small_sum(vals, axes):
    for axis in axes:
        bit = 1
        while bit < lax.axis_size(axis):
            vals = vals + swap_bit(vals, axis, bit)
            bit *= 2
    return vals


def tie(*vals):
    return lax.optimization_barrier(vals)


def small_sum(vals, axes):
    for axis in axes:
        bit = 1
        while bit < lax.axis_size(axis):
            vals = vals + swap_bit(vals, axis, bit)
            bit *= 2
    return vals


def gather_kernel(
    chunks, tok_ref, low_ref, post_ref, x_ref, w_ref, all_ref, ex_ref,
    own_sem, zh_send, zh_recv, t_send, t_recv, r_send, r_recv,
    wz_send, wz_recv, wd_send, wd_recv, wr_send, wr_recv, wl_sem, p_send, p_recv,
):
    n_dp = lax.axis_size("dp")
    tp = lax.axis_size("zl")
    d, r, g, t = (lax.axis_index(name) for name in ("dp", "row", "zh", "zl"))
    same = r == g
    feat = tok_ref.shape[1]
    seq_len = tok_ref.shape[0] // 2
    step = seq_len // chunks
    half = low_ref.shape[0]
    rows = half // n_dp

    def place(row, zh, zl):
        return (row * 2 + zh) * tp + zl

    def land(block, c):
        return x_ref.at[block, pl.ds(c * step, step)]

    def remote(src, dst, send, recv, dev):
        return pltpu.make_async_remote_copy(
            src_ref=src, dst_ref=dst, send_sem=send, recv_sem=recv, device_id=dev,
            device_id_type=pl.DeviceIdType.MESH,
        )

    barrier = pltpu.get_barrier_semaphore()
    count = 0
    for dd in range(n_dp):
        for rr in range(2):
            if dd or rr:
                dev = (lax.rem(d + dd, n_dp), lax.rem(r + rr, 2), g, t)
                pl.semaphore_signal(barrier, inc=1, device_id=dev, device_id_type=pl.DeviceIdType.MESH)
                count += 1
    for rr in range(2):
        for gg in range(2):
            for tt in range(tp):
                if gg or tt:
                    dev = (d, lax.rem(r + rr, 2), lax.rem(g + gg, 2), lax.rem(t + tt, tp))
                    pl.semaphore_signal(barrier, inc=1, device_id=dev, device_id_type=pl.DeviceIdType.MESH)
                    count += 1
    pl.semaphore_wait(barrier, count)

    row_dev = (d, 1 - r, g, t)
    zh_dev = (d, r, 1 - g, t)
    mine = place(r, g, t)
    pending = []

    wz = remote(low_ref.at[pl.ds(pl.multiple_of(d * rows, rows), rows)], ex_ref, wz_send, wz_recv, zh_dev)
    wz.start()

    def own_src(c):
        return tok_ref.at[pl.ds(pl.multiple_of(g * seq_len + c * step, step), step)]

    zh_copies = []
    for c in range(chunks):
        src = tok_ref.at[pl.ds(pl.multiple_of((1 - g) * seq_len + c * step, step), step)]
        zh_copies.append(remote(src, land(mine, c), zh_send.at[c], zh_recv.at[c], zh_dev))
        for s in range(1, tp):
            cp = remote(
                own_src(c), land(mine, c), t_send.at[s, 0, c], t_recv.at[s, 0, c], (d, r, g, lax.rem(t + s, tp))
            )
            cp.start()
            pending.append(cp)
    local = []
    for c in range(chunks):
        cp = pltpu.make_async_copy(own_src(c), land(mine, c), own_sem.at[c])
        cp.start()
        local.append(cp)
        cp = remote(own_src(c), land(mine, c), r_send.at[0, 0, c], r_recv.at[0, 0, c], row_dev)
        cp.start()
        pending.append(cp)

    wz.wait_send()
    lead = max(1, chunks // 4)
    for cp in zh_copies[:lead]:
        cp.start()

    half_at = pl.ds(pl.multiple_of(r * half, half), half)
    w_row = remote(low_ref, w_ref.at[half_at], wr_send, wr_recv, row_dev)
    w_loc = pltpu.make_async_copy(low_ref, w_ref.at[half_at], wl_sem.at[0])

    @pl.when(same)
    def _():
        w_loc.start()

    @pl.when(jnp.logical_not(same))
    def _():
        w_row.start()

    posts = []
    n_all = 4 * tp
    p_loc = pltpu.make_async_copy(post_ref, all_ref.at[mine], wl_sem.at[1])
    p_loc.start()
    index = 0
    for rr in range(2):
        for gg in range(2):
            for tt in range(tp):
                if rr or gg or tt:
                    dev = (d, lax.rem(r + rr, 2), lax.rem(g + gg, 2), lax.rem(t + tt, tp))
                    cp = remote(post_ref, all_ref.at[mine], p_send.at[index], p_recv.at[index], dev)
                    cp.start()
                    posts.append(cp)
                    index += 1

    def drain_zh(c):
        zh_copies[c].wait_recv()
        theirs = place(r, 1 - g, t)
        for s in range(1, tp):
            cp = remote(
                land(theirs, c), land(theirs, c), t_send.at[s, 1, c], t_recv.at[s, 1, c],
                (d, r, g, lax.rem(t + s, tp)),
            )
            cp.start()
            pending.append(cp)
        cp = remote(land(theirs, c), land(theirs, c), r_send.at[0, 1, c], r_recv.at[0, 1, c], row_dev)
        cp.start()
        pending.append(cp)

    def drain_t(z, c):
        for s in range(1, tp):
            came = place(r, g if z == 0 else 1 - g, lax.rem(t + tp - s, tp))
            remote(
                land(came, c), land(came, c), t_send.at[s, z, c], t_recv.at[s, z, c],
                (d, r, g, lax.rem(t + s, tp)),
            ).wait_recv()
            cp = remote(land(came, c), land(came, c), r_send.at[s, z, c], r_recv.at[s, z, c], row_dev)
            cp.start()
            pending.append(cp)

    wz.wait_recv()
    spot = pl.ds(pl.multiple_of(r * half + d * rows, rows), rows)
    far = []
    for dd in range(1, n_dp):
        cp = remote(
            ex_ref, w_ref.at[spot], wd_send.at[dd], wd_recv.at[dd, r], (lax.rem(d + dd, n_dp), 1 - g, g, t)
        )
        cp.start()
        far.append(cp)
        for late in zh_copies[lead:][dd - 1 : dd]:
            late.start()
    for late in zh_copies[lead:][n_dp - 1 :]:
        late.start()
    near_remote = remote(ex_ref, w_ref.at[spot], wd_send.at[0], wd_recv.at[0, r], row_dev)
    near_local = pltpu.make_async_copy(ex_ref, w_ref.at[spot], wl_sem.at[2])

    @pl.when(same)
    def _():
        near_remote.start()

    @pl.when(jnp.logical_not(same))
    def _():
        near_local.start()

    for c in range(chunks):
        drain_t(0, c)
        drain_zh(c)
        if c >= 1:
            drain_t(1, c - 1)
    drain_t(1, chunks - 1)

    for c in range(chunks):
        for z in range(2):
            for s in range(tp):
                came = place(1 - r, g if z == 0 else 1 - g, lax.rem(t + tp - s, tp))
                remote(
                    land(came, c), land(came, c), r_send.at[s, z, c], r_recv.at[s, z, c], row_dev
                ).wait_recv()
    for cp in local:
        cp.wait()
    for cp in pending:
        cp.wait_send()
    for cp in zh_copies:
        cp.wait_send()
    p_loc.wait()
    for cp in posts:
        cp.wait_send()
    index = 0
    for rr in range(2):
        for gg in range(2):
            for tt in range(tp):
                if rr or gg or tt:
                    came = place(
                        lax.rem(r + 2 - rr, 2), lax.rem(g + 2 - gg, 2), lax.rem(t + tp - tt, tp)
                    )
                    remote(
                        post_ref, all_ref.at[came], p_send.at[index], p_recv.at[index], row_dev
                    ).wait_recv()
                    index += 1
    for cp in far:
        cp.wait_send()

    @pl.when(same)
    def _():
        w_loc.wait()
        near_remote.wait_send()
        remote(
            low_ref, w_ref.at[pl.ds(pl.multiple_of((1 - r) * half, half), half)], wr_send, wr_recv, row_dev
        ).wait_recv()

    @pl.when(jnp.logical_not(same))
    def _():
        w_row.wait_send()
        near_local.wait()
        for dd in range(n_dp):
            for rr in range(2):
                src_d = lax.rem(d + n_dp - dd, n_dp)
                src_r = r if rr == 0 else 1 - r
                if dd == 0 and rr == 0:
                    continue
                at = pl.ds(pl.multiple_of(src_r * half + src_d * rows, rows), rows)
                remote(ex_ref, w_ref.at[at], wd_send.at[dd], wd_recv.at[dd, src_r], row_dev).wait_recv()


def first_gather(tokens, low, post):
    n_dp = lax.axis_size("dp")
    tp = lax.axis_size("zl")
    rows_dev, feat = tokens.shape
    seq_len = rows_dev // 2
    width = feat * 4 * tp
    chunks = 4 if tp == 2 else 1
    anywhere = pl.BlockSpec(memory_space=pl.ANY)
    dma = pltpu.SemaphoreType.DMA
    x_shape = (4 * tp, seq_len, feat)
    x_full, w_full, post_all, _ = pl.pallas_call(
        functools.partial(gather_kernel, chunks),
        in_specs=[anywhere] * 3,
        out_specs=[anywhere] * 4,
        out_shape=[
            jax.ShapeDtypeStruct(x_shape, bf16),
            jax.ShapeDtypeStruct((2 * low.shape[0], low.shape[1]), bf16),
            jax.ShapeDtypeStruct((4 * tp, *post.shape), f32),
            jax.ShapeDtypeStruct((low.shape[0] // n_dp, low.shape[1]), bf16),
        ],
        scratch_shapes=[
            dma((chunks,)),
            dma((chunks,)),
            dma((chunks,)),
            dma((tp, 2, chunks)),
            dma((tp, 2, chunks)),
            dma((tp, 2, chunks)),
            dma((tp, 2, chunks)),
            dma(()),
            dma(()),
            dma((n_dp,)),
            dma((n_dp, 2)),
            dma(()),
            dma(()),
            dma((3,)),
            dma((4 * tp,)),
            dma((4 * tp,)),
        ],
        compiler_params=pltpu.CompilerParams(collective_id=0, has_side_effects=True),
        cost_estimate=pl.CostEstimate(flops=0, bytes_accessed=6 * seq_len * width, transcendentals=0),
        name="first_gather",
    )(tokens, low, post)
    x_full = x_full.transpose(1, 0, 2).reshape(seq_len, width)
    return x_full, w_full, post_all.transpose(1, 0, 2).reshape(2, width)


def doc_start(ends_ref, docs, places):
    start = jnp.zeros_like(places)
    for i in range(docs):
        end = ends_ref[i]
        start = jnp.where(places >= end, end, start)
    return start


def attend_kernel(docs, bk, ends_ref, q_ref, k_ref, vt_ref, o_ref, lse_ref):
    bq = q_ref.shape[0]
    q0 = pl.program_id(1) * bq
    places = q0 + lax.broadcasted_iota(jnp.int32, (1, bq), 1)
    start = doc_start(ends_ref, docs, places)
    lowest = jnp.int32(0)
    for i in range(docs):
        lowest = jnp.where(ends_ref[i] <= q0, ends_ref[i], lowest)
    query = q_ref[...]
    scale = log2_e * HD ** (-0.5)

    def step(j, carry):
        top, total, acc = carry
        k0 = pl.multiple_of(j * bk, bk)
        key = k_ref[pl.ds(k0, bk), :]
        scores = lax.dot_general(key, query, NT, preferred_element_type=f32) * scale
        rows = k0 + lax.broadcasted_iota(jnp.int32, (bk, 1), 0)
        scores = jnp.where((rows <= places) & (rows >= start), scores, big_negative)
        top_new = jnp.maximum(top, jnp.max(scores, axis=0, keepdims=True))
        prob = jnp.exp2(scores - top_new)
        fade = jnp.exp2(top - top_new)
        total = total * fade + jnp.sum(prob, axis=0, keepdims=True)
        acc = acc * fade + lax.dot_general(
            vt_ref[:, pl.ds(k0, bk)], prob.astype(bf16), NN, preferred_element_type=f32
        )
        return top_new, total, acc

    first = (
        jnp.full((1, bq), big_negative, f32),
        jnp.zeros((1, bq), f32),
        jnp.zeros((HD, bq), f32),
    )
    top, total, acc = lax.fori_loop(lowest // bk, (q0 + bq - 1) // bk + 1, step, first)
    o_ref[...] = (acc * (1.0 / total)).T.astype(bf16)
    lse_ref[0] = top + jnp.log2(total)


def attend(query, key, value_t, ends):
    seq_len, width = query.shape
    heads = width // HD
    block = min(512, seq_len)
    docs = ends.shape[0]
    return pl.pallas_call(
        functools.partial(attend_kernel, docs, block),
        grid_spec=pltpu.PrefetchScalarGridSpec(
            num_scalar_prefetch=1,
            grid=(heads, seq_len // block),
            in_specs=[
                pl.BlockSpec((block, HD), lambda h, i, e: (i, h)),
                pl.BlockSpec((seq_len, HD), lambda h, i, e: (0, h)),
                pl.BlockSpec((HD, seq_len), lambda h, i, e: (h, 0)),
            ],
            out_specs=[
                pl.BlockSpec((block, HD), lambda h, i, e: (i, h)),
                pl.BlockSpec((1, 1, block), lambda h, i, e: (h, 0, i)),
            ],
        ),
        out_shape=[
            jax.ShapeDtypeStruct((seq_len, width), bf16),
            jax.ShapeDtypeStruct((heads, 1, seq_len), f32),
        ],
        compiler_params=pltpu.CompilerParams(vmem_limit_bytes=48 << 20),
        cost_estimate=pl.CostEstimate(
            flops=2 * heads * seq_len * seq_len * HD,
            bytes_accessed=8 * seq_len * width,
            transcendentals=heads * seq_len * seq_len // 2,
        ),
        name="attend",
    )(ends, query, key, value_t)


def attend_back_kernel(
    docs, bq, ends_ref, q_ref, k_ref, kt_ref, v_ref, do_ref, o_ref, lse_ref,
    dqt_ref, dk_ref, dv_ref, dk_acc, dv_acc, delta_acc
):
    bk = k_ref.shape[0]
    seq_len = q_ref.shape[0]
    j = pl.program_id(1)
    k0 = j * bk
    scale = HD ** (-0.5)
    last = jnp.int32(seq_len)
    for i in reversed(range(docs)):
        last = jnp.where(ends_ref[i] > k0 + bk - 1, ends_ref[i], last)
    rows = k0 + lax.broadcasted_iota(jnp.int32, (bk, 1), 0)

    @pl.when(j == 0)
    def _():
        dqt_ref[...] = jnp.zeros_like(dqt_ref)
        ones = jnp.ones((8, HD), bf16)
        for i in range(seq_len // bq):
            part = slice(i * bq, (i + 1) * bq)
            prod = do_ref[part, :].astype(f32) * o_ref[part, :].astype(f32)
            high = prod.astype(bf16)
            low = (prod - high.astype(f32)).astype(bf16)
            delta_acc[:, part] = lax.dot_general(
                ones, high, NT, preferred_element_type=f32
            ) + lax.dot_general(ones, low, NT, preferred_element_type=f32)

    dk_acc[...] = jnp.zeros_like(dk_acc)
    dv_acc[...] = jnp.zeros_like(dv_acc)
    key = k_ref[...]
    value = v_ref[...]
    key_t = kt_ref[...]

    def step(i, carry):
        q0 = pl.multiple_of(i * bq, bq)
        cols = pl.ds(q0, bq)
        query = q_ref[cols, :]
        grad = do_ref[cols, :]
        places = q0 + lax.broadcasted_iota(jnp.int32, (1, bq), 1)
        start = doc_start(ends_ref, docs, places)
        scores = lax.dot_general(key, query, NT, preferred_element_type=f32) * (scale * log2_e)
        allowed = (rows <= places) & (rows >= start)
        prob = jnp.where(allowed, jnp.exp2(scores - lse_ref[0, :, cols]), 0.0)
        dv_acc[...] += lax.dot_general(prob.astype(bf16), grad, NN, preferred_element_type=f32)
        grad_prob = lax.dot_general(value, grad, NT, preferred_element_type=f32)
        grad_score = (prob * (grad_prob - delta_acc[0:1, cols])).astype(bf16)
        dk_acc[...] += lax.dot_general(grad_score, query, NN, preferred_element_type=f32)
        dqt_ref[:, cols] += lax.dot_general(key_t, grad_score, NN, preferred_element_type=f32) * scale
        return carry

    lax.fori_loop(k0 // bq, (last + bq - 1) // bq, step, 0)
    dk_ref[...] = dk_acc[...] * scale
    dv_ref[...] = dv_acc[...].astype(bf16)


def attend_back(query, key, key_t, value, grad, att, log_total, ends):
    seq_len, width = query.shape
    heads = width // HD
    block = min(512, seq_len)
    docs = ends.shape[0]
    whole = pl.BlockSpec((seq_len, HD), lambda h, j, e: (0, h))
    part = pl.BlockSpec((block, HD), lambda h, j, e: (j, h))
    line = pl.BlockSpec((1, 1, seq_len), lambda h, j, e: (h, 0, 0))
    return pl.pallas_call(
        functools.partial(attend_back_kernel, docs, block),
        grid_spec=pltpu.PrefetchScalarGridSpec(
            num_scalar_prefetch=1,
            grid=(heads, seq_len // block),
            in_specs=[
                whole,
                part,
                pl.BlockSpec((HD, block), lambda h, j, e: (h, j)),
                part,
                whole,
                whole,
                line,
            ],
            out_specs=[
                pl.BlockSpec((HD, seq_len), lambda h, j, e: (h, 0)),
                part,
                part,
            ],
            scratch_shapes=[
                pltpu.VMEM((block, HD), f32),
                pltpu.VMEM((block, HD), f32),
                pltpu.VMEM((8, seq_len), f32),
            ],
        ),
        out_shape=[
            jax.ShapeDtypeStruct((width, seq_len), f32),
            jax.ShapeDtypeStruct((seq_len, width), f32),
            jax.ShapeDtypeStruct((seq_len, width), bf16),
        ],
        compiler_params=pltpu.CompilerParams(vmem_limit_bytes=48 << 20),
        cost_estimate=pl.CostEstimate(
            flops=5 * heads * seq_len * seq_len * HD,
            bytes_accessed=20 * seq_len * width,
            transcendentals=heads * seq_len * seq_len // 2,
        ),
        name="attend_back",
    )(ends, query, key, key_t, value, grad, att, log_total)


def turn(values, cos_two, sin_two):
    return values * cos_two + pltpu.roll(values, HD // 2, 1) * sin_two


def prepare_kernel(qkv_ref, scale_ref, gains_ref, cos_ref, sin_ref, q_ref, k_ref, kt_ref, v_ref, vt_ref):
    width = q_ref.shape[1]
    cos_two = cos_ref[...]
    sin_two = sin_ref[...]
    for which, out_ref in ((0, q_ref), (1, k_ref)):
        scale = scale_ref[:, which : which + 1]
        for head in range(width // HD):
            cols = slice(head * HD, (head + 1) * HD)
            vals = qkv_ref[:, which * width + head * HD : which * width + (head + 1) * HD]
            out = turn(vals * scale * gains_ref[which : which + 1, cols], cos_two, sin_two)
            out_ref[:, cols] = out.astype(bf16)
            if which == 1:
                kt_ref[cols, :] = out.T.astype(bf16)
    value = qkv_ref[:, 2 * width :]
    v_ref[...] = value.astype(bf16)
    vt_ref[...] = value.T.astype(bf16)


def prepare(qkv, inv_scale, gains, cos_two, sin_two):
    seq_len, triple = qkv.shape
    width = triple // 3
    block = min(256, seq_len)
    flat = pl.BlockSpec((block, width), lambda i: (i, 0))
    tall = pl.BlockSpec((width, block), lambda i: (0, i))
    table = pl.BlockSpec((block, HD), lambda i: (i, 0))
    return pl.pallas_call(
        prepare_kernel,
        grid=(seq_len // block,),
        in_specs=[
            pl.BlockSpec((block, triple), lambda i: (i, 0)),
            pl.BlockSpec((block, 2), lambda i: (i, 0)),
            pl.BlockSpec((2, width), lambda i: (0, 0)),
            table,
            table,
        ],
        out_specs=[flat, flat, tall, flat, tall],
        out_shape=[
            jax.ShapeDtypeStruct((seq_len, width), bf16),
            jax.ShapeDtypeStruct((seq_len, width), bf16),
            jax.ShapeDtypeStruct((width, seq_len), bf16),
            jax.ShapeDtypeStruct((seq_len, width), bf16),
            jax.ShapeDtypeStruct((width, seq_len), bf16),
        ],
        compiler_params=pltpu.CompilerParams(vmem_limit_bytes=48 << 20),
        cost_estimate=pl.CostEstimate(flops=10 * seq_len * triple, bytes_accessed=8 * seq_len * triple, transcendentals=0),
        name="prepare",
    )(qkv, inv_scale, gains, cos_two, sin_two)


def unturn_kernel(dqt_ref, dk_ref, qkv_ref, scale_ref, gains_ref, cos_ref, sin_ref, hat_ref, inner_ref, gain_ref):
    width = dk_ref.shape[1]
    cos_two = cos_ref[...]
    sin_two = sin_ref[...]

    @pl.when(pl.program_id(0) == 0)
    def _():
        gain_ref[...] = jnp.zeros_like(gain_ref)

    for which in range(2):
        scale = scale_ref[:, which : which + 1]
        inner = jnp.zeros((dk_ref.shape[0], HD), f32)
        for head in range(width // HD):
            cols = slice(head * HD, (head + 1) * HD)
            off = which * width + head * HD
            grad = dqt_ref[cols, :].T if which == 0 else dk_ref[:, cols]
            hat = turn(grad, cos_two, -sin_two)
            pre = qkv_ref[:, off : off + HD]
            prod = hat * pre
            gain_ref[which : which + 1, cols] += jnp.sum(prod * scale, axis=0, keepdims=True)
            inner = inner + prod * gains_ref[which : which + 1, cols]
            hat_ref[:, off : off + HD] = hat * gains_ref[which : which + 1, cols]
        inner_ref[:, which : which + 1] = jnp.sum(inner, axis=1, keepdims=True)


def unturn(dqt, dk, qkv, inv_scale, gains, cos_two, sin_two):
    seq_len, width = dk.shape
    block = min(256, seq_len)
    table = pl.BlockSpec((block, HD), lambda i: (i, 0))
    pair = pl.BlockSpec((block, 2), lambda i: (i, 0))
    return pl.pallas_call(
        unturn_kernel,
        grid=(seq_len // block,),
        in_specs=[
            pl.BlockSpec((width, block), lambda i: (0, i)),
            pl.BlockSpec((block, width), lambda i: (i, 0)),
            pl.BlockSpec((block, 2 * width), lambda i: (i, 0)),
            pair,
            pl.BlockSpec((2, width), lambda i: (0, 0)),
            table,
            table,
        ],
        out_specs=[
            pl.BlockSpec((block, 2 * width), lambda i: (i, 0)),
            pair,
            pl.BlockSpec((2, width), lambda i: (0, 0)),
        ],
        out_shape=[
            jax.ShapeDtypeStruct((seq_len, 2 * width), f32),
            jax.ShapeDtypeStruct((seq_len, 2), f32),
            jax.ShapeDtypeStruct((2, width), f32),
        ],
        compiler_params=pltpu.CompilerParams(vmem_limit_bytes=48 << 20),
        cost_estimate=pl.CostEstimate(flops=20 * seq_len * width, bytes_accessed=24 * seq_len * width, transcendentals=0),
        name="unturn",
    )(dqt, dk, qkv, inv_scale, gains, cos_two, sin_two)


class Job:
    def __init__(self, gather, scatter, merge, weights, pieces, dim, spread, tile_ins, outs, slots, sums, body):
        self.gather, self.scatter, self.merge, self.spread = gather, scatter, merge, spread
        self.weights, self.pieces, self.dim = weights, pieces, dim
        self.tile_ins, self.outs = tile_ins, outs
        self.slots, self.sums, self.body = slots, sums, body


def tile_kernel(job, tp, chunks, *refs):
    refs = list(refs)

    def take(count):
        got = refs[:count]
        del refs[:count]
        return got

    (src_ref,) = take(1)
    w_hbm = [take(max(1, job.pieces)) for _ in range(job.weights)]
    ti_hbm = take(job.tile_ins)
    quarter_ref = take(1)[0] if job.spread else None
    full_ref = take(1)[0] if job.gather else src_ref
    out_hbm = take(job.outs)
    w_out = take(job.weights) if job.pieces else None
    spread_ref = take(1)[0] if job.spread else None
    total_ref = take(1)[0] if job.scatter else None
    w_ref = take(job.weights)
    (tile_ref,) = take(1)
    ti_ref = take(job.tile_ins)
    out_ref = take(job.outs)
    y_ref, rbuf, zbuf, tbuf = take(4) if job.scatter else (None,) * 4
    w_sem, tile_sem, ti_sem, out_sem, loc_sem = take(5)
    t_send, t_recv, r_send, r_recv = take(4)
    y_send, y_recv, z_send, z_recv = take(4)
    wl_sem, wr_send, wr_recv, q_send, q_recv = take(5)

    n_dp = lax.axis_size("dp")
    d, r, g, t = (lax.axis_index(name) for name in ("dp", "row", "zh", "zl"))
    rows = tile_ref.shape[1]
    if job.merge:
        mc = rows // (2 * chunks)
        order = [(s, 0) for s in range(tp)]
    else:
        mc = rows // 2
        order = [(s, c) for c in range(chunks) for s in range(tp)]
    if not job.gather:
        order = [(s, c) for s in list(range(1, tp)) + [0] for c in range(chunks)]
    row_dev = (d, 1 - r, g, t)

    def peer(step):
        return (d, r, g, lax.rem(t + step + tp, tp))

    def remote(src, dst, send, recv, dev):
        return pltpu.make_async_remote_copy(
            src_ref=src, dst_ref=dst, send_sem=send, recv_sem=recv, device_id=dev,
            device_id_type=pl.DeviceIdType.MESH,
        )

    def piece(s, c, rho):
        return full_ref.at[pl.ds(((s * chunks + c) * 2 + rho) * mc, mc)]

    barrier = pltpu.get_barrier_semaphore()
    pl.semaphore_signal(barrier, inc=1, device_id=row_dev, device_id_type=pl.DeviceIdType.MESH)
    for s in range(1, tp):
        pl.semaphore_signal(barrier, inc=1, device_id=peer(s), device_id_type=pl.DeviceIdType.MESH)

    count = tp
    if job.spread:
        for k in range(1, n_dp):
            dev = (lax.rem(d + k, n_dp), r, g, t)
            pl.semaphore_signal(barrier, inc=1, device_id=dev, device_id_type=pl.DeviceIdType.MESH)
            count += 1
    same = r == g
    other_core = jnp.logical_not(same)

    def half_view(i, half, row_at, row_count, col_at, col_count):
        ref = w_ref[i]
        if job.dim == 0:
            size = ref.shape[0] // 2
            start = pl.multiple_of(half * size + row_at, row_count)
            return ref.at[pl.ds(start, row_count), pl.ds(col_at, col_count)]
        size = ref.shape[1] // 2
        return ref.at[pl.ds(row_at, row_count), pl.ds(pl.multiple_of(half * size + col_at, col_count), col_count)]

    def piece_list(i):
        if len(w_hbm[i]) == 2:
            other = w_hbm[i][1]
            return [(other, 0, other.shape[0], 0, other.shape[1])]
        one, two, one_x, one_y, two_y, two_x = w_hbm[i][1:]
        rows_q, cut = one.shape
        low_bit, high_bit = lax.rem(d, 2), d // 2
        places = [
            ((high_bit * (1 - 2 * (k // 2)) + k // 2) * 2 + low_bit * (1 - 2 * (k % 2)) + k % 2) * rows_q
            for k in range(4)
        ]
        upper, lower = pl.ds(0, rows_q), pl.ds(rows_q, rows_q)
        return [
            (one, places[0], rows_q, 0, cut),
            (one_x, places[1], rows_q, 0, cut),
            (one_y.at[upper], places[2], rows_q, 0, cut),
            (one_y.at[lower], places[3], rows_q, 0, cut),
            (two, places[0], rows_q, cut, cut),
            (two_x.at[upper], places[1], rows_q, cut, cut),
            (two_y, places[2], rows_q, cut, cut),
            (two_x.at[lower], places[3], rows_q, cut, cut),
        ]

    def piece_recv_places(i):
        return [half_view(i, 1 - r, *spot[1:]) for spot in piece_list(i)]

    def low_copies(i):
        low = w_hbm[i][0]
        there = half_view(i, r, 0, low.shape[0], 0, low.shape[1])
        here = half_view(i, 1 - r, 0, low.shape[0], 0, low.shape[1])
        keep = pltpu.make_async_copy(low, there, wl_sem.at[i, 0])
        give = pltpu.make_async_remote_copy(
            src_ref=low, dst_ref=there, send_sem=wr_send.at[i, 0], recv_sem=wr_recv.at[i, 0],
            device_id=row_dev, device_id_type=pl.DeviceIdType.MESH,
        )
        got = pltpu.make_async_remote_copy(
            src_ref=low, dst_ref=here, send_sem=wr_send.at[i, 0], recv_sem=wr_recv.at[i, 0],
            device_id=row_dev, device_id_type=pl.DeviceIdType.MESH,
        )
        return keep, give, got

    def part_copies(i):
        keeps, gives, gots = [], [], []
        for p, spot in enumerate(piece_list(i)):
            there = half_view(i, r, *spot[1:])
            here = piece_recv_places(i)[p]
            keeps.append(pltpu.make_async_copy(spot[0], there, wl_sem.at[i, p]))
            for dst, into in ((there, gives), (here, gots)):
                into.append(
                    pltpu.make_async_remote_copy(
                        src_ref=spot[0], dst_ref=dst, send_sem=wr_send.at[i, p], recv_sem=wr_recv.at[i, p],
                        device_id=row_dev, device_id_type=pl.DeviceIdType.MESH,
                    )
                )
        return keeps, gives, gots

    def w_start(i):
        if not job.pieces:
            pltpu.make_async_copy(w_hbm[i][0], w_ref[i], w_sem.at[i]).start()
            return

        @pl.when(same)
        def _():
            low_copies(i)[0].start()
            for cp in part_copies(i)[1]:
                cp.start()

        @pl.when(other_core)
        def _():
            low_copies(i)[1].start()
            for cp in part_copies(i)[0]:
                cp.start()

    def w_wait(i):
        if not job.pieces:
            pltpu.make_async_copy(w_hbm[i][0], w_ref[i], w_sem.at[i]).wait()
            return

        @pl.when(same)
        def _():
            low_copies(i)[0].wait()
            low_copies(i)[2].wait_recv()

        @pl.when(other_core)
        def _():
            for cp in part_copies(i)[0]:
                cp.wait()
            for cp in part_copies(i)[2]:
                cp.wait_recv()

        pltpu.make_async_copy(w_ref[i], w_out[i], w_sem.at[i]).start()

    def w_end(i):

        @pl.when(same)
        def _():
            for cp in part_copies(i)[1]:
                cp.wait_send()

        @pl.when(other_core)
        def _():
            low_copies(i)[1].wait_send()

        pltpu.make_async_copy(w_ref[i], w_out[i], w_sem.at[i]).wait()

    if not job.pieces:
        for i in range(job.weights):
            w_start(i)
    pl.semaphore_wait(barrier, count)
    seen = set()

    def need(i):
        if i not in seen:
            seen.add(i)
            w_wait(i)

    sends = []

    def go(cp):
        cp.start()
        sends.append(cp)

    local = {}
    if job.gather:
        for c in range(chunks):
            own = src_ref.at[pl.ds(c * mc, mc)]
            for s in range(1, tp):
                go(remote(own, piece(s, c, 0), t_send.at[s, c], t_recv.at[s, c], peer(-s)))
            local[c] = pltpu.make_async_copy(own, piece(0, c, 0), loc_sem.at[c])
            local[c].start()
            go(remote(own, piece(0, c, 1), r_send.at[0, c], r_recv.at[0, c], row_dev))

    if job.pieces:
        for i in range(job.weights):
            w_start(i)
    if job.spread:
        rows_q = quarter_ref.shape[0]
        mine = spread_ref.at[pl.ds(pl.multiple_of(d * rows_q, rows_q), rows_q)]
        q_local = pltpu.make_async_copy(quarter_ref, mine, q_send.at[0])
        q_local.start()
        for k in range(1, n_dp):
            go(remote(quarter_ref, mine, q_send.at[k], q_recv.at[k], (lax.rem(d + k, n_dp), r, g, t)))

    relayed = set()

    def relay(s, c):
        if job.gather and s > 0 and (s, c) not in relayed:
            relayed.add((s, c))
            remote(piece(s, c, 0), piece(s, c, 0), t_send.at[s, c], t_recv.at[s, c], peer(-s)).wait_recv()
            go(remote(piece(s, c, 0), piece(s, c, 1), r_send.at[s, c], r_recv.at[s, c], row_dev))

    def tile_load(i):
        s, c = order[i]
        at = pl.ds((s if job.merge else s * chunks + c) * rows, rows)
        return pltpu.make_async_copy(full_ref.at[at], tile_ref.at[i % 2], tile_sem.at[i % 2])

    def ti_loads(i):
        s, c = order[i]
        at = pl.ds((s if job.merge else s * chunks + c) * rows, rows)
        return [pltpu.make_async_copy(ti_hbm[j].at[at], ti_ref[j], ti_sem.at[j]) for j in range(job.tile_ins)]

    def out_copies(i):
        s, c = order[i]
        at = pl.ds((s if job.merge else s * chunks + c) * rows, rows)
        slot = i % job.slots
        return [
            pltpu.make_async_copy(out_ref[j].at[slot], out_hbm[j].at[at], out_sem.at[j, slot])
            for j in range(job.outs)
        ]

    def combine(i):
        s, c = order[i]
        k = s * chunks + c
        cp = remote(
            y_ref.at[i % job.sums, pl.ds(mc, mc)], rbuf.at[k], y_send.at[s, c], y_recv.at[s, c], row_dev
        )
        cp.wait()
        step = min(64, mc)

        def add(b, carry):
            at = pl.ds(pl.multiple_of(b * step, step), step)
            summed = y_ref[i % job.sums, at, :].astype(f32) + rbuf[k, at, :].astype(f32)
            if s == 0:
                total_ref[pl.ds(pl.multiple_of(c * mc + b * step, step), step), :] = summed
            else:
                zbuf[k - chunks, at, :] = summed.astype(bf16)
            return carry

        lax.fori_loop(0, mc // step, add, 0)
        if s > 0:
            go(remote(zbuf.at[k - chunks], tbuf.at[k - chunks], z_send.at[s, c], z_recv.at[s, c], peer(s)))

    for cp in ti_loads(0):
        cp.start()
    if not job.gather:
        tile_load(0).start()
    for i, (s, c) in enumerate(order):
        if job.gather:
            held = range(chunks) if job.merge else [c]
            for cc in held:
                relay(s, cc)
                if s == 0:
                    local[cc].wait()
            for cc in held:
                remote(piece(s, cc, 1), piece(s, cc, 1), r_send.at[s, cc], r_recv.at[s, cc], row_dev).wait_recv()
            tile_load(i).start()
        tile_load(i).wait()
        if not job.gather and i + 1 < len(order):
            tile_load(i + 1).start()
        for cp in ti_loads(i):
            cp.wait()
        if i >= job.slots:
            for cp in out_copies(i - job.slots):
                cp.wait()

        def mid(i=i):
            if i + 1 < len(order):
                relay(*order[i + 1])
                for cp in ti_loads(i + 1):
                    cp.start()
            if job.scatter:
                for cp in out_copies(i):
                    cp.start()
                if i >= 1:
                    combine(i - 1)

        outs = [ref.at[i % job.slots] for ref in out_ref]
        y = y_ref.at[i % job.sums] if job.scatter else None
        job.body(tile_ref.at[i % 2], w_ref, need, ti_ref, outs, y, mid)
        if job.scatter:
            k = s * chunks + c
            remote(y.at[pl.ds(mc, mc)], rbuf.at[k], y_send.at[s, c], y_recv.at[s, c], row_dev).start()
        else:
            for cp in out_copies(i):
                cp.start()
    last = len(order)
    for i in range(max(0, last - job.slots), last):
        for cp in out_copies(i):
            cp.wait()
    if job.scatter:
        combine(last - 1)
        for c in range(chunks):
            for s in range(1, tp):
                k = (s - 1) * chunks + c
                remote(zbuf.at[k], tbuf.at[k], z_send.at[s, c], z_recv.at[s, c], peer(s)).wait_recv()
                step = min(64, mc)

                def add(b, carry, k=k, c=c):
                    at = pl.ds(pl.multiple_of(b * step, step), step)
                    to = pl.ds(pl.multiple_of(c * mc + b * step, step), step)
                    total_ref[to, :] = total_ref[to, :] + tbuf[k, at, :].astype(f32)
                    return carry

                lax.fori_loop(0, mc // step, add, 0)
    if job.pieces:
        for i in range(job.weights):
            w_end(i)
    if job.spread:
        q_local.wait()
        for k in range(1, n_dp):
            came = lax.rem(d + n_dp - k, n_dp)
            remote(
                quarter_ref, spread_ref.at[pl.ds(pl.multiple_of(came * rows_q, rows_q), rows_q)],
                q_send.at[k], q_recv.at[k], row_dev,
            ).wait_recv()
    for cp in sends:
        cp.wait_send()


def tile_call(job, ident, name, src, weights, shapes, tile_ins, out_widths, sum_width, flops, quarter=None):
    tp = lax.axis_size("zl")
    n_dp = lax.axis_size("dp")
    flat_weights = [v for group in weights for v in group]
    width = src.shape[1]
    m = src.shape[0] if job.gather else src.shape[0] // (2 * tp)
    chunks = 2 if tp == 2 else 1
    mc = m // chunks
    rows = 2 * (m if job.merge else mc)
    total_rows = 2 * tp * m
    anywhere = pl.BlockSpec(memory_space=pl.ANY)
    dma = pltpu.SemaphoreType.DMA
    out_specs, out_shape = [], []
    if job.gather:
        out_specs.append(anywhere)
        out_shape.append(jax.ShapeDtypeStruct((total_rows, width), bf16))
    for w in out_widths:
        out_specs.append(anywhere)
        out_shape.append(jax.ShapeDtypeStruct((total_rows, w), bf16))
    if job.pieces:
        out_specs.extend([anywhere] * len(shapes))
        out_shape.extend(jax.ShapeDtypeStruct(shape, bf16) for shape in shapes)
    if job.spread:
        out_specs.append(anywhere)
        out_shape.append(jax.ShapeDtypeStruct((n_dp * quarter.shape[0], quarter.shape[1]), bf16))
    if job.scatter:
        out_specs.append(pl.BlockSpec(memory_space=pltpu.VMEM))
        out_shape.append(jax.ShapeDtypeStruct((m, sum_width), f32))
    scratch = [pltpu.VMEM(shape, bf16) for shape in shapes]
    scratch.append(pltpu.VMEM((2, rows, width), bf16))
    scratch.extend(pltpu.VMEM((rows, v.shape[1]), bf16) for v in tile_ins)
    scratch.extend(pltpu.VMEM((job.slots, rows, w), bf16) for w in out_widths)
    if job.scatter:
        scratch.append(pltpu.VMEM((job.sums, rows, sum_width), bf16))
        scratch.append(pltpu.VMEM((tp * chunks, mc, sum_width), bf16))
        scratch.append(pltpu.VMEM(((tp - 1) * chunks, mc, sum_width), bf16))
        scratch.append(pltpu.VMEM(((tp - 1) * chunks, mc, sum_width), bf16))
    scratch.extend(
        [dma((len(weights),)), dma((2,)), dma((max(1, len(tile_ins)),)), dma((max(1, job.outs), job.slots)), dma((chunks,))]
    )
    scratch.extend(dma((tp, chunks)) for _ in range(8))
    scratch.extend(dma((len(weights), 8)) for _ in range(3))
    scratch.extend(dma((n_dp,)) for _ in range(2))
    extra = [quarter] if job.spread else []
    return pl.pallas_call(
        functools.partial(tile_kernel, job, tp, chunks),
        in_specs=[anywhere] * (1 + len(flat_weights) + len(tile_ins) + len(extra)),
        out_specs=out_specs,
        out_shape=out_shape,
        scratch_shapes=scratch,
        compiler_params=pltpu.CompilerParams(
            collective_id=ident, has_side_effects=True, vmem_limit_bytes=60 << 20
        ),
        cost_estimate=pl.CostEstimate(flops=flops, bytes_accessed=8 * total_rows * width, transcendentals=0),
        name=name,
    )(src, *flat_weights, *tile_ins, *extra)


def columns(n, size):
    return pl.ds(pl.multiple_of(n * size, size), size)


def loop(first, last, step):
    def body(n, carry):
        step(n)
        return carry

    lax.fori_loop(first, last, body, 0)


def gate_up_body(tile, w, need, ti, outs, y, mid):
    hidden_width = w[0].shape[1]
    nb = min(512, hidden_width)
    count = hidden_width // nb
    need(0)
    need(1)

    def step(n):
        cols = columns(n, nb)
        rows = tile[...]
        gate = jnp.dot(rows, w[0][:, cols], preferred_element_type=f32)
        up = jnp.dot(rows, w[1][:, cols], preferred_element_type=f32)
        outs[0][:, cols] = gate.astype(bf16)
        outs[1][:, cols] = up.astype(bf16)
        outs[2][:, cols] = (gate * jax.nn.sigmoid(gate) * up).astype(bf16)

    loop(0, count // 2, step)
    mid()
    loop(count // 2, count, step)


def down_body(tile, w, need, ti, outs, y, mid):
    nb = min(1024, w[0].shape[1])
    count = w[0].shape[1] // nb
    need(0)

    def step(n):
        cols = columns(n, nb)
        y[:, cols] = jnp.dot(tile[...], w[0][:, cols], preferred_element_type=f32).astype(bf16)

    loop(0, count // 2, step)
    mid()
    loop(count // 2, count, step)


def back_body(tile, w, need, ti, outs, y, mid):
    hidden_width = w[0].shape[0]
    nb = min(512, hidden_width)
    need(0)

    def first(n):
        cols = columns(n, nb)
        grad = lax.dot_general(tile[...], w[0][cols, :], NT, preferred_element_type=f32)
        grad = grad.astype(bf16).astype(f32)
        gate = ti[0][:, cols].astype(f32)
        up = ti[1][:, cols].astype(f32)
        sig = jax.nn.sigmoid(gate)
        passed = grad * sig
        outs[0][:, cols] = (passed * up * (1.0 + gate * (1.0 - sig))).astype(bf16)
        outs[1][:, cols] = (passed * gate).astype(bf16)

    loop(0, hidden_width // nb, first)
    mid()
    need(1)
    need(2)
    nd = 512

    def second(n):
        cols = columns(n, nd)
        grad = lax.dot_general(outs[0][...], w[1][cols, :], NT, preferred_element_type=f32)
        grad = grad + lax.dot_general(outs[1][...], w[2][cols, :], NT, preferred_element_type=f32)
        y[:, cols] = grad.astype(bf16)

    loop(0, w[1].shape[0] // nd, second)


gate_up_job = Job(True, False, True, 2, 7, 0, True, 0, 3, 2, 0, gate_up_body)
down_job = Job(False, True, False, 1, 2, 1, False, 0, 0, 1, 2, down_body)
back_job = Job(True, True, False, 3, 0, 0, False, 2, 2, 1, 1, back_body)


def last_kernel(
    chunks, dx_ref, grad_ref, out_ref, sum_ref, own, from_row, near, from_t, give, from_zh,
    g_own, g_in, g_sum, g_late,
    own_sem, row_send, row_recv, t_send, t_recv, zh_send, zh_recv, g_sem, d_send, d_recv, f_send, f_recv,
):
    n_dp = lax.axis_size("dp")
    tp = lax.axis_size("zl")
    d, r, g, t = (lax.axis_index(name) for name in ("dp", "row", "zh", "zl"))
    same = r == g
    other_core = jnp.logical_not(same)
    seq_len, width = dx_ref.shape
    half = width // 2
    feat = half // (2 * tp)
    step = seq_len // chunks
    part = g_own.shape[1]

    def remote(src, dst, send, recv, dev):
        return pltpu.make_async_remote_copy(
            src_ref=src, dst_ref=dst, send_sem=send, recv_sem=recv, device_id=dev,
            device_id_type=pl.DeviceIdType.MESH,
        )

    row_dev = (d, 1 - r, g, t)
    zh_dev = (d, r, 1 - g, t)
    cross_dev = (d, 1 - r, 1 - g, t)

    def dp_dev(k):
        return (lax.rem(d + k, n_dp), r, g, t)

    def t_dev(s):
        return (d, r, g, lax.rem(t + s, tp))

    partners = [row_dev, zh_dev, cross_dev]
    partners += [dp_dev(k) for k in range(1, n_dp)] + [t_dev(s) for s in range(1, tp)]
    barrier = pltpu.get_barrier_semaphore()
    for dev in partners:
        pl.semaphore_signal(barrier, inc=1, device_id=dev, device_id_type=pl.DeviceIdType.MESH)
    pl.semaphore_wait(barrier, len(partners))

    def cols_at(which):
        return pl.ds(pl.multiple_of(which * half, half), half)

    rows_copies, own_copies = [], []
    for c in range(chunks):
        rows = pl.ds(c * step, step)
        cp = remote(dx_ref.at[rows, cols_at(1 - r)], from_row.at[c], row_send.at[c], row_recv.at[c], row_dev)
        cp.start()
        rows_copies.append(cp)
        cp = pltpu.make_async_copy(dx_ref.at[rows, cols_at(r)], own.at[c], own_sem.at[c])
        cp.start()
        own_copies.append(cp)

    def grad_rows(which, group):
        return grad_ref.at[pl.ds(pl.multiple_of((which * n_dp + group) * part, part), part)]

    g_copies, g_loads = [], []
    for which in range(2):
        cp = pltpu.make_async_copy(grad_rows(which, d), g_own.at[which], g_sem.at[which])
        cp.start()
        g_loads.append(cp)
        for k in range(1, n_dp):
            cp = remote(
                grad_rows(which, lax.rem(d + k, n_dp)), g_in.at[k - 1, which],
                d_send.at[k, which], d_recv.at[k, which], dp_dev(k),
            )
            cp.start()
            g_copies.append(cp)

    t_copies = {}

    def row_stage(c):
        own_copies[c].wait()
        rows_copies[c].wait_recv()
        total = own[c].astype(f32) + from_row[c].astype(f32)
        for b in range(2 * tp):
            near[c, b] = total[:, b * feat : (b + 1) * feat].astype(bf16)
        for zh in range(2):
            for s in range(1, tp):
                cp = remote(
                    near.at[c, zh * tp + lax.rem(t + s, tp)], from_t.at[c, zh, s - 1],
                    t_send.at[c, zh, s], t_recv.at[c, zh, s], t_dev(s),
                )
                cp.start()
                t_copies[(c, zh, s)] = cp

    zh_copies = []

    def t_stage(c):
        for zh in range(2):
            for s in range(1, tp):
                t_copies[(c, zh, s)].wait_recv()

        def total_of(zh):
            total = near[c, zh * tp + t].astype(f32)
            for s in range(1, tp):
                total = total + from_t[c, zh, s - 1].astype(f32)
            return total

        give[c] = total_of(1 - g).astype(bf16)
        cp = remote(give.at[c], from_zh.at[c], zh_send.at[c], zh_recv.at[c], zh_dev)
        cp.start()
        zh_copies.append(cp)
        out_ref[pl.ds(pl.multiple_of(g * seq_len + c * step, step), step), :] = total_of(g)

    def grad_stage():
        for cp in g_loads:
            cp.wait()
        for cp in g_copies:
            cp.wait_recv()
        block = min(64, part)
        for which in range(2):

            def add(i, carry, which=which):
                at = pl.ds(pl.multiple_of(i * block, block), block)
                total = g_own[which, at, :].astype(f32)
                for k in range(n_dp - 1):
                    total = total + g_in[k, which, at, :].astype(f32)
                g_sum[which, at, :] = total.astype(bf16)
                return carry

            lax.fori_loop(0, part // block, add, 0)

    to_row = remote(g_sum.at[1 - r], g_late.at[0], f_send.at[0], f_recv.at[0], row_dev)
    to_zh = remote(g_sum.at[r], g_late.at[0], f_send.at[1], f_recv.at[1], zh_dev)
    to_cross = remote(g_sum.at[1 - r], g_late.at[1], f_send.at[2], f_recv.at[2], cross_dev)

    for c in range(chunks):
        row_stage(c)
        if c >= 2:
            t_stage(c - 2)
    grad_stage()

    @pl.when(same)
    def _():
        to_row.start()

    @pl.when(other_core)
    def _():
        to_zh.start()
        to_cross.start()

    for c in range(max(0, chunks - 2), chunks):
        t_stage(c)
    for c in range(chunks):
        zh_copies[c].wait_recv()
        out_ref[pl.ds(pl.multiple_of((1 - g) * seq_len + c * step, step), step), :] = from_zh[c].astype(f32)

    @pl.when(same)
    def _():
        to_zh.wait_recv()
        sum_ref[...] = g_sum[r].astype(f32) + g_late[0].astype(f32)
        to_row.wait_send()

    @pl.when(other_core)
    def _():
        to_row.wait_recv()
        to_cross.wait_recv()
        sum_ref[...] = g_late[0].astype(f32) + g_late[1].astype(f32)
        to_zh.wait_send()
        to_cross.wait_send()

    for cp in rows_copies + g_copies + list(t_copies.values()) + zh_copies:
        cp.wait_send()


def last_sums(dx, grad):
    n_dp = lax.axis_size("dp")
    tp = lax.axis_size("zl")
    seq_len, width = dx.shape
    chunks = 4
    half = width // 2
    feat = half // (2 * tp)
    step = seq_len // chunks
    part = grad.shape[0] // (2 * n_dp)
    cols = grad.shape[1]
    anywhere = pl.BlockSpec(memory_space=pl.ANY)
    vmem = pl.BlockSpec(memory_space=pltpu.VMEM)
    dma = pltpu.SemaphoreType.DMA
    return pl.pallas_call(
        functools.partial(last_kernel, chunks),
        in_specs=[anywhere] * 2,
        out_specs=[vmem] * 2,
        out_shape=[
            jax.ShapeDtypeStruct((2 * seq_len, feat), f32),
            jax.ShapeDtypeStruct((part, cols), f32),
        ],
        scratch_shapes=[
            pltpu.VMEM((chunks, step, half), bf16),
            pltpu.VMEM((chunks, step, half), bf16),
            pltpu.VMEM((chunks, 2 * tp, step, feat), bf16),
            pltpu.VMEM((chunks, 2, tp - 1, step, feat), bf16),
            pltpu.VMEM((chunks, step, feat), bf16),
            pltpu.VMEM((chunks, step, feat), bf16),
            pltpu.VMEM((2, part, cols), bf16),
            pltpu.VMEM((n_dp - 1, 2, part, cols), bf16),
            pltpu.VMEM((2, part, cols), bf16),
            pltpu.VMEM((2, part, cols), bf16),
            dma((chunks,)),
            dma((chunks,)),
            dma((chunks,)),
            dma((chunks, 2, tp)),
            dma((chunks, 2, tp)),
            dma((chunks,)),
            dma((chunks,)),
            dma((2,)),
            dma((n_dp, 2)),
            dma((n_dp, 2)),
            dma((3,)),
            dma((3,)),
        ],
        compiler_params=pltpu.CompilerParams(collective_id=4, has_side_effects=True, vmem_limit_bytes=60 << 20),
        cost_estimate=pl.CostEstimate(flops=0, bytes_accessed=8 * seq_len * width, transcendentals=0),
        name="last_sums",
    )(dx, grad)


def rotary(seq_len):
    half_width = HD // 2
    freqs = rope_base ** (-(jnp.arange(half_width, dtype=f32) * 2.0) / HD)
    angles = jnp.arange(seq_len, dtype=f32)[:, None] * freqs[None, :]
    cos_table, sin_table = jnp.cos(angles), jnp.sin(angles)
    return (
        jnp.concatenate([cos_table, cos_table], axis=1),
        jnp.concatenate([-sin_table, sin_table], axis=1),
    )


def norm_scale(vals):
    return lax.rsqrt(jnp.mean(vals * vals, axis=1, keepdims=True) + norm_eps)


def norm_back(pre_vals, scale, gains, gradient):
    weighted = gradient * gains
    inner = jnp.mean(weighted * pre_vals, axis=1, keepdims=True)
    grad_pre = scale * weighted - pre_vals * (scale * scale * scale * inner)
    grad_gain = jnp.sum(gradient * pre_vals * scale, axis=0)
    return grad_pre, grad_gain


def adamw_step(weight, gradient, first_mom, second_mom, step_rate, decay_rate):
    first_new = beta_one * first_mom + (1.0 - beta_one) * gradient
    second_new = beta_two * second_mom + (1.0 - beta_two) * gradient * gradient
    fix_one = 1.0 - beta_one**STEP
    fix_two = 1.0 - beta_two**STEP
    direction = first_new / fix_one / (jnp.sqrt(second_new / fix_two) + adam_eps)
    return (first_new, second_new, weight - step_rate * (direction + decay_rate * weight))


def matmul(left, right, dims=NN):
    return lax.dot_general(left, right, dims, preferred_element_type=f32)


def shards(
    tokens, cotangent, doc_lengths, qkv_weight, out_weight, gate_weight, up_weight, down_weight,
    head_gains, post_gains, qkv_first, qkv_second, out_first, out_second, gate_first, gate_second,
    up_first, up_second, down_first, down_second, head_first, head_second, post_first, post_second,
):
    n_dp = lax.axis_size("dp")
    tp = lax.axis_size("zl")
    group = 2 * tp
    n_col = 2 * tp
    d, r, g, t = (lax.axis_index(name) for name in ("dp", "row", "zh", "zl"))
    same = r == g
    block_at = r * tp + t
    rows_dev, feat = tokens.shape
    width = feat * 2 * n_col
    seq_len = rows_dev // 2
    mine = seq_len // group
    col_width = qkv_weight.shape[2]

    ends = jnp.cumsum(jnp.where(same, doc_lengths, swap(doc_lengths, "row")), axis=1)[0]

    qkv_low = jnp.concatenate([qkv_weight[:, i, :].astype(bf16) for i in range(3)], axis=1)
    x_full, qkv_full, post_all = first_gather(tokens, qkv_low, post_gains.T)
    x_tok = lax.dynamic_slice_in_dim(x_full, block_at * mine, mine, 0)

    def halves(quarter):
        cut = quarter.shape[1] // 2
        return quarter[:, :cut], quarter[:, cut:]

    def gathered(one, two, one_x, two_y):
        one_y = swap_bit(jnp.concatenate([one, one_x]), "dp", 2)
        two_x = swap_bit(jnp.concatenate([two, two_y]), "dp", 1)
        return [one, two, one_x, one_y, two_y, two_x]

    def quarter_of(weight):
        rows = weight.shape[0] // n_dp
        return lax.dynamic_slice_in_dim(weight, d * rows, rows, 0).astype(bf16)

    gate_one, gate_two = halves(quarter_of(gate_weight))
    gate_one, gate_two, post_all = tie(gate_one, gate_two, post_all)
    gate_one = swap(gate_one, "zh")

    out_rows = out_weight.shape[0] // n_dp
    out_part = lax.dynamic_slice_in_dim(out_weight, d * out_rows, out_rows, 0).astype(bf16)
    out_part, post_all = tie(lax.all_gather(out_part, ("zh", "zl"), axis=0), post_all)
    out_part = lax.all_gather(out_part, "dp", axis=1)

    cos_two, sin_two = rotary(seq_len)
    gains = jnp.where(same, head_gains, swap(head_gains, "zh"))
    qkv = matmul(x_full, qkv_full)
    squares = jnp.stack(
        [
            jnp.sum(jnp.square(qkv[:, :col_width]), axis=1),
            jnp.sum(jnp.square(qkv[:, col_width : 2 * col_width]), axis=1),
        ],
        axis=0,
    )
    inv_scale = lax.rsqrt(small_sum(squares, ("row", "zl")) / width + norm_eps).T
    gate_two = swap(gate_two, "zh")
    up_one, up_two = halves(quarter_of(up_weight))
    up_one, up_two = swap(up_one, "zh"), swap(up_two, "zh")
    down_quarter = swap(quarter_of(down_weight), "zh")
    inv_scale, gate_one = tie(inv_scale, gate_one)
    query, key, key_t, value, value_t = prepare(qkv, inv_scale, gains, cos_two, sin_two)
    ends, gate_two = tie(ends, gate_two)
    gate_one_x, gate_two_y = swap_bit(gate_one, "dp", 1), swap_bit(gate_two, "dp", 2)
    out_part, key_t = tie(out_part, key_t)
    out_full = lax.all_gather(out_part.reshape(width, width // 2), "row", axis=1, tiled=True)
    att, log_total = attend(query, key, value_t, ends)
    att, up_one, gate_one_x, gate_two_y = tie(att, up_one, gate_one_x, gate_two_y)
    gate_pieces = gathered(gate_one, gate_two, gate_one_x, gate_two_y)

    def to_tokens(vals):
        got = lax.all_to_all(vals.reshape(group, mine, col_width), ("row", "zl"), 0, 0)
        return got.transpose(1, 0, 2).reshape(mine, width)

    def to_heads(vals):
        sent = vals.reshape(mine, group, col_width).transpose(1, 0, 2)
        return lax.all_to_all(sent, ("row", "zl"), 0, 0).reshape(seq_len, col_width)

    att_tok = to_tokens(att)

    gain_attn, gain_mlp = post_all[0:1], post_all[1:2]
    att_tok, up_two, gate_pieces[3], gate_pieces[5] = tie(att_tok, up_two, gate_pieces[3], gate_pieces[5])
    a_pre = matmul(att_tok, out_full)
    a_scale = norm_scale(a_pre)
    h_tok = x_tok.astype(f32) + a_pre * a_scale * gain_attn

    cot = cotangent.reshape(2, 2, tp, mine, feat).transpose(1, 0, 2, 3, 4).reshape(2 * n_col, mine, feat)
    cot, a_scale = tie(cot, a_scale)
    cot = lax.all_to_all(cot, ("row", "zh", "zl"), 0, 0)
    cot_tok = cot.transpose(1, 0, 2).reshape(mine, width).astype(f32)

    up_pieces = gathered(up_one, up_two, swap_bit(up_one, "dp", 1), swap_bit(up_two, "dp", 2))
    gate_low, up_low, down_low = (
        v.astype(bf16) for v in (gate_weight, up_weight, down_weight)
    )
    hidden_width = gate_low.shape[1]
    work = 2 * seq_len * width * hidden_width
    wide, tall = (width, hidden_width), (hidden_width, width)
    h_full, gate_all, up_all, hidden, gate_full, up_full, down_other = tile_call(
        gate_up_job, 1, "gate_up", h_tok.astype(bf16), [[gate_low, *gate_pieces], [up_low, *up_pieces]],
        [wide, wide], [], [hidden_width] * 3, 0, 2 * work, down_quarter,
    )
    down_full, m_pre = tile_call(
        down_job, 2, "down", hidden, [[down_low, down_other]], [tall], [], [], width, work
    )
    m_scale = norm_scale(m_pre)
    mixed_tok = (h_tok + m_pre * m_scale * gain_mlp).astype(bf16)

    def to_features(vals):
        out = lax.all_to_all(
            vals.reshape(mine, 2 * n_col, feat).transpose(1, 0, 2), ("row", "zh", "zl"), 0, 0
        )
        return out.reshape(2, 2, tp, mine, feat).transpose(1, 0, 2, 3, 4).reshape(rows_dev, feat)

    mixed = to_features(mixed_tok)

    grad_m, grad_gain_mlp = norm_back(m_pre, m_scale, gain_mlp, cot_tok)
    dm_full, grad_gate, grad_up, dh_sum = tile_call(
        back_job, 3, "feed_back", grad_m.astype(bf16), [[down_full], [gate_full], [up_full]], [tall, wide, wide],
        [gate_all, up_all], [hidden_width] * 2, width, 3 * work,
    )
    grad_down_w = matmul(hidden, dm_full, TN).astype(bf16)
    grad_gate_w = matmul(h_full, grad_gate, TN).astype(bf16)
    grad_up_w = matmul(h_full, grad_up, TN).astype(bf16)
    dh_tok = cot_tok + dh_sum

    low_bit, high_bit = d % 2, d // 2

    def pick(vals, dim, index):
        return lax.dynamic_slice_in_dim(vals, index, 1, dim)

    def trade(vals, dim, bit, index):
        got = swap_bit(pick(vals, dim, 1 - index), "dp", bit)
        return (pick(vals, dim, index).astype(f32) + got.astype(f32)).astype(bf16)

    view = grad_down_w.reshape(n_dp // 2, 2, hidden_width // n_dp, width)
    down_one = trade(view[..., : width // 2], 1, 1, low_bit)
    down_two = trade(view[..., width // 2 :], 0, 2, high_bit)

    grad_a, grad_gain_attn = norm_back(a_pre, a_scale, gain_attn, dh_tok)
    grad_a = grad_a.astype(bf16)
    grad_att = to_heads(matmul(grad_a, out_full, NT).astype(bf16))
    grad_out = matmul(att_tok, grad_a, TN).astype(bf16)

    ends, down_one, down_two = tie(ends, down_one, down_two)
    dqt, dk, dv = attend_back(query, key, key_t, value, grad_att, att, log_total, ends)
    down_one = trade(down_one, 0, 2, high_bit)[0, 0]
    down_two = trade(down_two, 1, 1, low_bit)[0, 0]
    inv_scale, down_one, down_two = tie(inv_scale, down_one, down_two)
    weighted, inner, grad_head = unturn(dqt, dk, qkv, inv_scale, gains, cos_two, sin_two)
    inner = (small_sum(inner.T, ("row", "zl")) / width).T
    cube = inv_scale * inv_scale * inv_scale * inner
    dqkv = jnp.concatenate(
        [
            (inv_scale[:, 0:1] * weighted[:, :col_width] - qkv[:, :col_width] * cube[:, 0:1]).astype(bf16),
            (inv_scale[:, 1:2] * weighted[:, col_width:] - qkv[:, col_width : 2 * col_width] * cube[:, 1:2]).astype(bf16),
            dv,
        ],
        axis=1,
    )
    grad_qkv = matmul(x_full, dqkv, TN).astype(bf16)

    dx = matmul(dqkv, qkv_full, NT).astype(bf16)
    here = lax.dynamic_slice_in_dim(dx, block_at * mine, mine, 0).astype(f32) + dh_tok
    dx = lax.dynamic_update_slice_in_dim(dx, here.astype(bf16), block_at * mine, 0)
    dtokens, sum_qkv = last_sums(dx, grad_qkv)
    sum_qkv = sum_qkv.reshape(qkv_first.shape)

    def data_sums(grad):
        half = grad.shape[0] // 2
        return [
            lax.psum_scatter(grad[i * half : (i + 1) * half], "dp", scatter_dimension=0, tiled=True)
            for i in range(2)
        ]

    def to_owner(pieces):
        keep = jnp.where(r == 0, pieces[0], pieces[1])
        give = jnp.where(r == 0, pieces[1], pieces[0])
        axes = ("row", "zh")
        total = jnp.where(same, keep.astype(f32), 0.0)
        total = total + lax.ppermute(keep, axes, [(1, 0), (2, 3)]).astype(f32)
        total = total + lax.ppermute(give, axes, [(1, 2), (2, 1)]).astype(f32)
        return total + lax.ppermute(give, axes, [(0, 2), (3, 1)]).astype(f32)

    sum_down = to_owner([down_one, down_two])
    gate_sums, up_sums = data_sums(grad_gate_w), data_sums(grad_up_w)
    *gate_sums, grad_head = tie(*gate_sums, grad_head)
    *up_sums, sum_qkv = tie(*up_sums, sum_qkv)
    sum_gate = to_owner(gate_sums)
    sum_up = to_owner(up_sums)
    half_w = width // 2
    half = lax.dynamic_slice_in_dim(grad_out, r * half_w, half_w, 1).astype(f32) + swap(
        lax.dynamic_slice_in_dim(grad_out, (1 - r) * half_w, half_w, 1), "row"
    ).astype(f32)
    half = half.astype(bf16).reshape(n_col, n_dp, out_rows, width // 2)
    half = lax.psum_scatter(half, "dp", scatter_dimension=1, tiled=False)
    sum_out = lax.psum_scatter(half, ("zh", "zl"), scatter_dimension=0, tiled=False).astype(f32)

    head_place = lax.dynamic_update_slice_in_dim(
        jnp.zeros((2, width), f32), grad_head, block_at * col_width, 1
    )
    small = jnp.concatenate([head_place, grad_gain_attn[None], grad_gain_mlp[None]], axis=0)
    small = small_sum(small, ("dp", "row", "zh", "zl"))
    col_at = g * tp + t
    sum_head = lax.dynamic_slice_in_dim(small[:2], col_at * col_width, col_width, 1)
    post_rows = post_first.shape[0]
    sum_post = lax.dynamic_slice_in_dim(
        small[2:], ((r * n_col + col_at) * n_dp + d) * post_rows, post_rows, 1
    ).T

    def owned_rows(weight, part_rows):
        return lax.dynamic_slice_in_dim(weight, d * part_rows, part_rows, 0)

    results = []
    for weight, total, first, second in (
        (qkv_weight, sum_qkv, qkv_first, qkv_second),
        (out_weight, sum_out, out_first, out_second),
        (gate_weight, sum_gate, gate_first, gate_second),
        (up_weight, sum_up, up_first, up_second),
        (down_weight, sum_down, down_first, down_second),
    ):
        results.extend(
            adamw_step(owned_rows(weight, total.shape[0]), total, first, second, rate_matrix, weight_decay)
        )
    results.extend(adamw_step(head_gains, sum_head, head_first, head_second, rate_gain, 0.0))
    results.extend(
        adamw_step(owned_rows(post_gains, post_rows), sum_post, post_first, post_second, rate_gain, 0.0)
    )
    return (mixed, dtokens, *results)


def solution(mesh):
    n_dp, n_row, n_col = (mesh.shape[name] for name in ("dp", "row", "col"))
    grid = Mesh(mesh.devices.reshape(n_dp, n_row, 2, n_col // 2), ("dp", "row", "zh", "zl"))
    col = ("zh", "zl")
    moved = P("dp", ("row", *col))
    qkv_part = P(("row", "dp"), None, col)
    flat_part = P((*col, "dp"), "row")
    wide_part = P(("row", "dp"), col)
    head_part = P(None, col)
    post_part = P(("row", *col, "dp"), None)
    in_specs = (
        moved,
        moved,
        P(("dp", "row"), None),
        P("row", None, col),
        P(col, "row"),
        P("row", col),
        P("row", col),
        P(col, "row"),
        head_part,
        P(("row", *col), None),
        *[spec for spec in (qkv_part, flat_part, wide_part, wide_part, flat_part, head_part, post_part) for _ in range(2)],
    )
    out_specs = (
        moved,
        moved,
        *[spec for spec in (qkv_part, flat_part, wide_part, wide_part, flat_part, head_part, post_part) for _ in range(3)],
    )
    return jax.shard_map(shards, mesh=grid, in_specs=in_specs, out_specs=out_specs, check_vma=False)
```

time: 3080 us -> 1400 us (0.45)
  waiting for transfers between devices: 2170 us -> 246 us
  Pallas kernels: 0 us -> 683 us
  matrix products: 417 us -> 146 us
  blocking collectives: 163 us -> 0 us
  other arithmetic: 252 us -> 126 us
  starting transfers between devices: 1.21 us -> 80.5 us
  local copies, waits for them, and re-layouts: 48.4 us -> 102 us
    reduce_scatter x12 -> x5, waiting for transfers between devices: 1320 us -> 0.04 us  [the longest x4 0.04 us: data_sums(): lax.psum_scatter(grad[i * half:(i + 1) * half], 'dp', scatter_dimension=0...]
    pallas_call x0 -> x9, Pallas kernels: none -> 683 us  [the longest x3 315 us: tile_call(): pl.pallas_call(functools.partial(tile_kernel, job, tp, chunks), in_specs=...]
    all_gather x7 -> x3, waiting for transfers between devices: 645 us -> 0.01 us  [the longest x1 0.01 us: shards(): lax.all_gather(out_part, ('zh', 'zl'), axis=0)]
    dot_general x36 -> x9, matrix products: 417 us -> 146 us  [matmul(): return lax.dot_general(left, right, dims, preferred_element_type=f32)]
    ppermute x0 -> x38, waiting for transfers between devices: none -> 245 us  [the longest x21 115 us: swap_bit(): lax.ppermute(piece, axis, [(i, i ^ bit) for i in range(lax.axis_size(axis...]
    psum x1 -> x0, waiting for transfers between devices: 188 us -> none  [shards(): gate_up_all = lax.psum(gate_up_part, 'row')]
    psum x7 -> x0, blocking collectives: 163 us -> none  [the longest x4 112 us: token_total(): return lax.psum(values, ('row', 'col'))]
    ppermute x0 -> x38, starting transfers between devices: none -> 63.5 us  [the longest x8 26.4 us: swap(): return lax.ppermute(piece, axis, [(0, 1), (1, 0)])]
  transfers between devices with their start and end apart: 21 -> 51, of which waited for: 19 -> 11; matrix products, arithmetic and copies ran while one was open for 6% -> 23% of each run, Pallas kernels for 0% -> 39%
where the time goes in v1:
time: 1400 us
  Pallas kernels  683 us (49%)
  waiting for transfers between devices  246 us (18%)
  matrix products  146 us (10%)
  other arithmetic  126 us (9%)
  local copies, waits for them, and re-layouts  102 us (7%)
  starting transfers between devices  80.5 us (6%)
  between operations  15.2 us (1%)
    pallas_call x3, Pallas kernels, tile_call(): pl.pallas_call(functools.partial(tile_kernel, job, tp, chunks), in_specs=...  315 us
    dot_general x9, matrix products, matmul(): return lax.dot_general(left, right, dims, preferred_element_type=f32)  146 us
    pallas_call x1, Pallas kernels, last_sums(): pl.pallas_call(functools.partial(last_kernel, chunks), in_specs=[anywhere...  140 us
    pallas_call x1, Pallas kernels, first_gather(): pl.pallas_call(functools.partial(gather_kernel, chunks), in_specs=[anywhe...  134 us
    ppermute x21, waiting for transfers between devices, swap_bit(): lax.ppermute(piece, axis, [(i, i ^ bit) for i in range(lax.axis_size(axis...  115 us
    ppermute x8, waiting for transfers between devices, swap(): return lax.ppermute(piece, axis, [(0, 1), (1, 0)])  75.7 us
    ppermute x3, waiting for transfers between devices, to_owner(): total = total + lax.ppermute(keep, axes, [(1, 0), (2, 3)]).astype(f32)  54.7 us
    unnamed x123, local copies, waits for them, and re-layouts  38.4 us
  transfers between devices with their start and end apart: 51, of which 11 were waited for; matrix products, arithmetic and copies ran while one was open for 23% of the time, Pallas kernels for 39%

profile of v1, /device:TPU:0, one launch (start us, length us, event | category | flops | bytes accessed | tf_op | source)
XLA Modules:
  0.0 1398.7 jit_solution(11646520443945991748)
XLA Ops:
  9.1 4.9 convert.8
  17.8 134.3 %first_gather.1 = (bf16[8,2048,256]{2,1,0:T(8,128)(2,1)}, bf16[2048,1536]{1,0:T(8,128)(2,1)}, f32[8,2,256]{2,1,0:T(2,128)}, bf16[256,1536]{1,0:T(8,128)(2,1)}) custom-call(bf16[4096,256]{1,0:T(8,128)(2,1)} %tok_ref.1, bf16[1024,1536]{1,0:T(8,128)(2,1)} %pad_maximum_fusion.1.low_ref, f32[2,256]{1,0:T(2,128)} %bitcast.153), custom_call_target="tpu_custom_call" | custom-call | bytes 25165824 | tf_op jit(solution)/shard_map/first_gather/pallas_call | solution.py:292
  155.8 7.9 copy.134
  163.6 17.5 %fusion.39.qkv_ref = f32[2048,1536]{1,0:T(8,128)S(1)} fusion(bf16[2048,2048]{1,0:T(8,128)(2,1)} %bitcast.112, bf16[2048,1536]{1,0:T(8,128)(2,1)} %get-tuple-element.91), kind=kOutput, calls=%fused_computation.135 | convolution fusion | flops 12884901888 | bytes 27262976 | tf_op jit(solution)/shard_map/dot_general | solution.py:1363
  181.9 20.3 %collective-permute-start.4 = (bf16[256,1024]{1,0:T(8,128)(2,1)}, bf16[256,1024]{1,0:T(8,128)(2,1)}, u32[]{:S(2)}, u32[]{:S(2)}) collective-permute-start(bf16[256,1024]{1,0:T(8,128)(2,1)} %get-tuple-element.92), channel_id=1, source_target_pairs={{0,2},{2,0},{1,3},{3,1},{4,6},{6,4},{5,7},{7,5},{8,10},{10,8},{9,1... | collective-permute-start | bytes 1572872 | tf_op jit(solution)/shard_map/ppermute | solution.py:33
  202.2 3.9 fusion.13
  208.5 17.5 %collective-permute-done.5 = f32[2,512]{1,0:T(2,128)S(1)} collective-permute-done((f32[2,512]{1,0:T(2,128)S(1)}, f32[2,512]{1,0:T(2,128)S(1)}, u32[]{:S(2)}, u32[]{:S(2)}) %collective-permute-start.5) | collective-permute-done | bytes 4128 | tf_op jit(solution)/shard_map/ppermute | solution.py:33
  230.5 12.0 prepare.1
  250.0 32.0 %collective-permute-done.1.refs_3_ = bf16[256,1024]{1,0:T(8,128)(2,1)} collective-permute-done((bf16[256,1024]{1,0:T(8,128)(2,1)S(1)}, bf16[256,1024]{1,0:T(8,128)(2,1)}, u32[]{:S(2)}, u32[]{:S(2)}) %collective-permute-start.1) | collective-permute-done | bytes 524320 | tf_op jit(solution)/shard_map/ppermute | solution.py:33
  286.7 29.6 %attend.1 = (bf16[2048,512]{1,0:T(8,128)(2,1)S(1)}, f32[4,1,2048]{2,1,0:T(1,128)S(1)}) custom-call(s32[4]{0:T(128)S(1)} %bitcast.107, bf16[2048,512]{1,0:T(8,128)(2,1)S(1)} %copy-done.8, bf16[2048,512]{1,0:T(8,128)(2,1)} %get-tuple-element.95.k_ref, bf16[512,2048]{1,0:T(8,128)(2,1)} %get-tuple-element.96.vt_ref), custom_call_target="tpu_custom_call" | custom-call | flops 4294967296 | bytes 8388608 | tf_op jit(solution)/shard_map/attend/pallas_call | solution.py:378
  319.1 3.6 all-to-all-start
  334.9 6.2 convert_element_type.185.refs_1_
  341.1 6.3 convert_element_type.186.refs_8_
  351.6 26.3 %collective-permute-done.9.refs_10_ = bf16[256,1024]{1,0:T(8,128)(2,1)} collective-permute-done((bf16[256,1024]{1,0:T(8,128)(2,1)}, bf16[256,1024]{1,0:T(8,128)(2,1)}, u32[]{:S(2)}, u32[]{:S(2)}) %collective-permute-start.9) | collective-permute-done | bytes 524320 | tf_op jit(solution)/shard_map/ppermute | solution.py:33
  382.2 10.8 collective-permute-done.14.refs_13_
  395.9 9.5 multiply_reduce_fusion.5
  405.4 3.6 all-to-all-start.2
  409.1 4.9 fusion.refs_0_
  415.5 114.4 %gate_up.1 = (bf16[2048,2048]{1,0:T(8,128)(2,1)}, bf16[2048,2048]{1,0:T(8,128)(2,1)}, bf16[2048,2048]{1,0:T(8,128)(2,1)}, bf16[2048,2048]{1,0:T(8,128)(2,1)}, bf...) custom-call(bf16[512,2048]{1,0:T(8,128)(2,1)} %fusion.refs_0_, ...), custom_call_target="tpu_custom_call" | custom-call | flops 34359738368 | bytes 33554432 | tf_op jit(solution)/shard_map/gate_up/pallas_call | solution.py:1017
  529.9 65.6 %down.1 = (bf16[2048,2048]{1,0:T(8,128)(2,1)}, f32[512,2048]{1,0:T(8,128)}) custom-call(bf16[2048,2048]{1,0:T(8,128)(2,1)} %get-tuple-element.113.refs_0_, bf16[2048,1024]{1,0:T(8,128)(2,1)} %convert_element_type.188.refs_1_, bf16[2048,1024]{1,0:T(8,128)(2,1)} %get-tuple-element.114.refs_2_), custom_call_target="tpu_custom_call" | custom-call | flops 17179869184 | bytes 33554432 | tf_op jit(solution)/shard_map/down/pallas_call | solution.py:1017
  599.0 3.1 copy-done.18
  604.3 4.6 subtract_convert_fusion.3
  608.9 134.8 %feed_back.1 = (bf16[2048,2048]{1,0:T(8,128)(2,1)}, bf16[2048,2048]{1,0:T(8,128)(2,1)}, bf16[2048,2048]{1,0:T(8,128)(2,1)}, f32[512,2048]{1,0:T(8,128)}) custom-call(bf16[512,2048]{1,0:T(8,128)(2,1)} %get-tuple-element.260.refs_0_, bf16[2048,2048]{1,0:T(8,128)(2,1)} %get-tuple-element.117.refs_1_, bf16[2048,2048]{1,0:T(8,128)(2,1)} %get-tuple-element.118.refs_2_, ...), custom_call_target="tpu_custom_call" | custom-call | flops 51539607552 | bytes 33554432 | tf_op jit(solution)/shard_map/feed_back/pallas_call | solution.py:1017
  743.7 22.4 %convolution_convert_fusion = bf16[2048,2048]{1,0:T(8,128)(2,1)S(1)} fusion(bf16[2048,2048]{1,0:T(8,128)(2,1)} %get-tuple-element.138, bf16[2048,2048]{1,0:T(8,128)(2,1)} %get-tuple-element.142), kind=kOutput, calls=%fused_computation.1 | convolution fusion | flops 17184063488 | bytes 25165824 | tf_op jit(solution)/shard_map/dot_general | solution.py:1363
  766.1 3.5 fusion.32
  770.3 22.4 %convolution_convert_fusion.2 = bf16[2048,2048]{1,0:T(8,128)(2,1)S(1)} fusion(bf16[2048,2048]{1,0:T(8,128)(2,1)} %get-tuple-element.138, bf16[2048,2048]{1,0:T(8,128)(2,1)} %get-tuple-element.139), kind=kOutput, calls=%fused_computation.3 | convolution fusion | flops 17184063488 | bytes 25165824 | tf_op jit(solution)/shard_map/dot_general | solution.py:1363
  792.7 3.7 fusion.33
  796.5 22.9 %convolution_convert_fusion.4 = bf16[2048,2048]{1,0:T(8,128)(2,1)S(1)} fusion(bf16[2048,2048]{1,0:T(8,128)(2,1)} %get-tuple-element.113.refs_0_, bf16[2048,2048]{1,0:T(8,128)(2,1)} %get-tuple-element.122), kind=kOutput, calls=%fused_computation.5 | convolution fusion | flops 17184063488 | bytes 25165824 | tf_op jit(solution)/shard_map/dot_general | solution.py:1363
  828.3 3.7 multiply_reduce_fusion.1
  834.6 8.5 convolution_convert_fusion.6
  844.6 4.6 all-to-all-start.3
  849.3 49.3 %collective-permute-done.17 = bf16[2,1,512,1024]{3,2,1,0:T(8,128)(2,1)S(1)} collective-permute-done((bf16[2,1,512,1024]{3,2,1,0:T(8,128)(2,1)}, bf16[2,1,512,1024]{3,2,1,0:T(8,128)(2,1)S(1)}, u32[]{:S(2)}, u32[]{:S(2)}) %collective-permute-start.17) | collective-permute-done | bytes 2097184 | tf_op jit(solution)/shard_map/ppermute | solution.py:42
  901.3 3.6 collective-permute-done.18
  911.5 4.7 convolution_convert_fusion.1
  916.3 3.1 constant_dynamic-slice_fusion.2
  923.6 3.0 copy.131
  926.6 3.0 copy.124
  929.6 3.1 copy.122
  932.7 3.2 copy.139
  935.9 11.3 collective-permute-done.19
  952.8 4.4 all-to-all-start.1
  958.8 37.5 %attend_back.1 = (f32[512,2048]{1,0:T(8,128)}, f32[2048,512]{1,0:T(8,128)}, bf16[2048,512]{1,0:T(8,128)(2,1)S(1)}) custom-call(s32[4]{0:T(128)S(1)} %bitcast.108, bf16[2048,512]{1,0:T(8,128)(2,1)S(1)} %copy-done.9, bf16[2048,512]{1,0:T(8,128)(2,1)} %get-tuple-element.95.k_ref, bf16[512,2048]{1,0:T(8,128)(2,1)} %get-tuple-element.127.kt_ref, ...), custom_call_target="tpu_custom_call" | custom-call | flops 10737418240 | bytes 20971520 | tf_op jit(solution)/shard_map/attend_back/pallas_call | solution.py:470
  996.4 14.1 %unturn.1 = (f32[2048,1024]{1,0:T(8,128)}, f32[2048,2]{1,0:T(8,128)S(1)}, f32[2,512]{1,0:T(2,128)S(1)}) custom-call(f32[512,2048]{1,0:T(8,128)} %get-tuple-element.132.dqt_ref, f32[2048,512]{1,0:T(8,128)} %get-tuple-element.133.dk_ref, f32[2048,1536]{1,0:T(8,128)} %copy-done.12, f32[2048,2]{1,0:T(8,128)S(1)} %copy-done.1, f32[2,512]{1,0:T(2,128)S(1)} %copy-done.6, ...), custom_call_target="tpu_custom_call" | custom-call | flops 20971520 | bytes 25165824 | tf_op jit(solution)/shard_map/unturn/pallas_call | solution.py:593
  1011.5 3.0 broadcast_select_fusion.1
  1027.5 9.1 subtract_convert_fusion.1
  1036.7 4.3 add_convert_fusion
  1045.1 18.8 %convolution_convert_fusion.5.grad_ref = bf16[2048,1536]{1,0:T(8,128)(2,1)} fusion(bf16[2048,2048]{1,0:T(8,128)(2,1)} %bitcast.115, bf16[2048,512]{1,0:T(8,128)(2,1)S(1)} %copy-done.11, bf16[2048,512]{1,0:T(8,128)(2,1)} %get-tuple-element.253, bf16[2048,512]{1,0:T(8,128)(2,1)} %get-tuple-element.252), kind=kOutput, calls=%fused_computation.6 | convolution fusion | flops 12906921984 | bytes 20971520 | tf_op jit(solution)/shard_map/dot_general | solution.py:1363
  1063.9 19.6 %convolution_convert_fusion.3 = bf16[2048,2048]{1,0:T(8,128)(2,1)} fusion(bf16[2048,1536]{1,0:T(8,128)(2,1)} %get-tuple-element.91, bf16[2048,512]{1,0:T(8,128)(2,1)S(1)} %copy-done.11, bf16[2048,512]{1,0:T(8,128)(2,1)} %get-tuple-element.253, bf16[2048,512]{1,0:T(8,128)(2,1)} %get-tuple-element.252), kind=kOutput, calls=%fused_computation.4 | convolution fusion | flops 12907970560 | bytes 20971520 | tf_op jit(solution)/shard_map/dot_general | solution.py:1363
  1083.7 5.5 fusion.4.dx_ref
  1089.2 140.3 %last_sums.1 = (f32[4096,256]{1,0:T(8,128)}, f32[256,1536]{1,0:T(8,128)}) custom-call(bf16[2048,2048]{1,0:T(8,128)(2,1)} %fusion.4.dx_ref, bf16[2048,1536]{1,0:T(8,128)(2,1)} %convolution_convert_fusion.5.grad_ref), custom_call_target="tpu_custom_call" | custom-call | bytes 33554432 | tf_op jit(solution)/shard_map/last_sums/pallas_call | solution.py:1292
  1229.5 3.0 copy.123
  1232.5 3.2 copy.113
  1237.6 7.4 multiply_subtract_fusion
  1246.2 3.4 collective-permute-start.26
  1252.6 4.6 collective-permute-start.36
  1257.1 3.0 broadcast_select_fusion.3
  1260.1 38.1 %collective-permute-done.36 = f32[4,2048]{1,0:T(4,128)S(1)} collective-permute-done((f32[4,2048]{1,0:T(4,128)S(1)}, f32[4,2048]{1,0:T(4,128)S(1)}, u32[]{:S(2)}, u32[]{:S(2)}) %collective-permute-start.36) | collective-permute-done | bytes 32800 | tf_op jit(solution)/shard_map/ppermute | solution.py:42
  1298.4 4.3 multiply_subtract_fusion.3
  1302.7 3.0 copy.127
  1305.7 3.1 copy.128
  1315.6 8.5 multiply_subtract_fusion.2
  1324.2 54.7 %collective-permute-done.27 = bf16[256,2048]{1,0:T(8,128)(2,1)S(1)} collective-permute-done((bf16[256,2048]{1,0:T(8,128)(2,1)}, bf16[256,2048]{1,0:T(8,128)(2,1)S(1)}, u32[]{:S(2)}, u32[]{:S(2)}) %collective-permute-start.27) | collective-permute-done | bytes 1048608 | tf_op jit(solution)/shard_map/ppermute | solution.py:1547
  1378.9 6.0 multiply_subtract_fusion.1
  1387.4 4.5 copy.143
  (282 shorter events, 130.6 us)
Async XLA Ops:
  7.2 148.5 %all-gather.8.cloned.1.call-start = ((), (), s32[]{:S(2)}) async-start(), calls=%async_computation.16 | async-start | bytes 1310720 | tf_op jit(solution)/shard_map/all_gather | solution.py:1409
  9.1 235.7 %all-gather.10.cloned.1.call-start = ((), (), s32[]{:S(2)}) async-start(), calls=%async_computation.17 | async-start | bytes 5242880 | tf_op jit(solution)/shard_map/all_gather | solution.py:1410
  155.7 240.1 %all-gather.6.cloned.1.call-start = ((), (), s32[]{:S(2)}) async-start(), calls=%async_computation.10 | async-start | bytes 12582912 | tf_op jit(solution)/shard_map/all_gather | solution.py:1432
  181.8 24.9 %collective-permute-start.2 = (f32[2,2048]{1,0:T(2,128)S(1)}, f32[2,2048]{1,0:T(2,128)S(1)}, u32[]{:S(2)}, u32[]{:S(2)}) collective-permute-start(f32[2,2048]{1,0:T(2,128)S(1)} %pad_maximum_fusion.11), channel_id=1, source_target_pairs={{0,4},{4,0},{1,5},{5,1},{2,6},{6,2},{3,7},{7,3},{8,12},{12,8},{9,1... | collective-permute-start | bytes 49160 | tf_op jit(solution)/shard_map/ppermute | solution.py:42
  181.9 48.5 %collective-permute-start.4 = (bf16[256,1024]{1,0:T(8,128)(2,1)}, bf16[256,1024]{1,0:T(8,128)(2,1)}, u32[]{:S(2)}, u32[]{:S(2)}) collective-permute-start(bf16[256,1024]{1,0:T(8,128)(2,1)} %get-tuple-element.92), channel_id=1, source_target_pairs={{0,2},{2,0},{1,3},{3,1},{4,6},{6,4},{5,7},{7,5},{8,10},{10,8},{9,1... | collective-permute-start | bytes 1572872 | tf_op jit(solution)/shard_map/ppermute | solution.py:33
  202.2 23.8 %collective-permute-start.5 = (f32[2,512]{1,0:T(2,128)S(1)}, f32[2,512]{1,0:T(2,128)S(1)}, u32[]{:S(2)}, u32[]{:S(2)}) collective-permute-start(f32[2,512]{1,0:T(2,128)S(1)} %copy-done.45), channel_id=1, source_target_pairs={{0,2},{2,0},{1,3},{3,1},{4,6},{6,4},{5,7},{7,5},{8,10},{10,8},{9,1... | collective-permute-start | bytes 12296 | tf_op jit(solution)/shard_map/ppermute | solution.py:33
  206.8 20.6 %collective-permute-start.3 = (f32[2,2048]{1,0:T(2,128)S(1)}, f32[2,2048]{1,0:T(2,128)S(1)}, u32[]{:S(2)}, u32[]{:S(2)}) collective-permute-start(f32[2,2048]{1,0:T(2,128)S(1)} %fusion.22), channel_id=1, source_target_pairs={{0,1},{1,0},{2,3},{3,2},{4,5},{5,4},{6,7},{7,6},{8,9},{9,8},{10,11... | collective-permute-start | bytes 49160 | tf_op jit(solution)/shard_map/ppermute | solution.py:42
  245.8 36.1 %collective-permute-start.1 = (bf16[256,1024]{1,0:T(8,128)(2,1)S(1)}, bf16[256,1024]{1,0:T(8,128)(2,1)}, u32[]{:S(2)}, u32[]{:S(2)}) collective-permute-start(bf16[256,1024]{1,0:T(8,128)(2,1)S(1)} %copy-done.42), channel_id=1, source_target_pairs={{0,2},{2,0},{1,3},{3,1},{4,6},{6,4},{5,7},{7,5},{8,10},{10,8},{9,1... | collective-permute-start | bytes 1572872 | tf_op jit(solution)/shard_map/ppermute | solution.py:33
  245.8 4.0 collective-permute-start
  246.9 69.4 %collective-permute-start.6 = (bf16[256,1024]{1,0:T(8,128)(2,1)}, bf16[256,1024]{1,0:T(8,128)(2,1)}, u32[]{:S(2)}, u32[]{:S(2)}) collective-permute-start(bf16[256,1024]{1,0:T(8,128)(2,1)} %get-tuple-element.272), channel_id=1, source_target_pairs={{0,2},{2,0},{1,3},{3,1},{4,6},{6,4},{5,7},{7,5},{8,10},{10,8},{9,1... | collective-permute-start | bytes 1572872 | tf_op jit(solution)/shard_map/ppermute | solution.py:33
  282.0 34.4 %collective-permute-start.7 = (bf16[256,1024]{1,0:T(8,128)(2,1)}, bf16[256,1024]{1,0:T(8,128)(2,1)}, u32[]{:S(2)}, u32[]{:S(2)}) collective-permute-start(bf16[256,1024]{1,0:T(8,128)(2,1)} %collective-permute-done.4.refs_2_), channel_id=1, source_target_pairs={{0,8},{8,0},{16,24},{24,16},{1,9},{9,1},{17,25},{25,17},{2,10},{10... | collective-permute-start | bytes 1572872 | tf_op jit(solution)/shard_map/ppermute | solution.py:42
  283.7 32.7 %collective-permute-start.8 = (bf16[256,1024]{1,0:T(8,128)(2,1)}, bf16[256,1024]{1,0:T(8,128)(2,1)}, u32[]{:S(2)}, u32[]{:S(2)}) collective-permute-start(bf16[256,1024]{1,0:T(8,128)(2,1)} %collective-permute-done.1.refs_3_), channel_id=1, source_target_pairs={{0,16},{8,24},{16,0},{24,8},{1,17},{9,25},{17,1},{25,9},{2,18},{10... | collective-permute-start | bytes 1572872 | tf_op jit(solution)/shard_map/ppermute | solution.py:42
  319.1 58.7 %all-to-all-start = ((bf16[4,512,512]{1,2,0:T(8,128)(2,1)}), bf16[4,512,512]{1,2,0:T(8,128)(2,1)S(1)}, u32[]{:S(2)}, u32[]{:S(2)}) async-start(bf16[4,512,512]{1,2,0:T(8,128)(2,1)} %copy.111), calls=%async_computation | async-start | bytes 4194304 | tf_op jit(solution)/shard_map/all_to_all | solution.py:1438
  325.0 52.8 %collective-permute-start.10 = (bf16[512,1024]{1,0:T(8,128)(2,1)}, bf16[512,1024]{1,0:T(8,128)(2,1)}, u32[]{:S(2)}, u32[]{:S(2)}) collective-permute-start(bf16[512,1024]{1,0:T(8,128)(2,1)} %pad_maximum_fusion.6), channel_id=1, source_target_pairs={{0,16},{8,24},{16,0},{24,8},{1,17},{9,25},{17,1},{25,9},{2,18},{10... | collective-permute-start | bytes 3145736 | tf_op jit(solution)/shard_map/ppermute | solution.py:42
  327.2 50.6 %collective-permute-start.11 = (bf16[512,1024]{1,0:T(8,128)(2,1)}, bf16[512,1024]{1,0:T(8,128)(2,1)}, u32[]{:S(2)}, u32[]{:S(2)}) collective-permute-start(bf16[512,1024]{1,0:T(8,128)(2,1)} %pad_maximum_fusion.7), channel_id=1, source_target_pairs={{0,8},{8,0},{16,24},{24,16},{1,9},{9,1},{17,25},{25,17},{2,10},{10... | collective-permute-start | bytes 3145736 | tf_op jit(solution)/shard_map/ppermute | solution.py:42
  328.1 49.7 %collective-permute-start.9 = (bf16[256,1024]{1,0:T(8,128)(2,1)}, bf16[256,1024]{1,0:T(8,128)(2,1)}, u32[]{:S(2)}, u32[]{:S(2)}) collective-permute-start(bf16[256,1024]{1,0:T(8,128)(2,1)} %get-tuple-element.271), channel_id=1, source_target_pairs={{0,2},{2,0},{1,3},{3,1},{4,6},{6,4},{5,7},{7,5},{8,10},{10,8},{9,1... | collective-permute-start | bytes 1572872 | tf_op jit(solution)/shard_map/ppermute | solution.py:33
  328.4 50.7 %collective-permute-start.12 = (bf16[256,1024]{1,0:T(8,128)(2,1)}, bf16[256,1024]{1,0:T(8,128)(2,1)}, u32[]{:S(2)}, u32[]{:S(2)}) collective-permute-start(bf16[256,1024]{1,0:T(8,128)(2,1)} %collective-permute-done.6.refs_9_), channel_id=1, source_target_pairs={{0,8},{8,0},{16,24},{24,16},{1,9},{9,1},{17,25},{25,17},{2,10},{10... | collective-permute-start | bytes 1572872 | tf_op jit(solution)/shard_map/ppermute | solution.py:42
  332.0 82.0 %collective-permute-start.16 = (bf16[512,1024]{1,0:T(8,128)(2,1)}, bf16[512,1024]{1,0:T(8,128)(2,1)}, u32[]{:S(2)}, u32[]{:S(2)}) collective-permute-start(bf16[512,1024]{1,0:T(8,128)(2,1)} %dynamic-slice_convert_fusion), channel_id=1, source_target_pairs={{0,2},{2,0},{1,3},{3,1},{4,6},{6,4},{5,7},{7,5},{8,10},{10,8},{9,1... | collective-permute-start | bytes 3145736 | tf_op jit(solution)/shard_map/ppermute | solution.py:33
  351.6 30.6 %copy-start.47 = (f32[8,2,256]{2,1,0:T(2,128)S(1)}, f32[8,2,256]{2,1,0:T(2,128)}, u32[]{:S(2)}) copy-start(f32[8,2,256]{2,1,0:T(2,128)} %get-tuple-element.88) | copy-start | bytes 49156
  377.8 15.1 %collective-permute-start.14 = (bf16[256,1024]{1,0:T(8,128)(2,1)}, bf16[256,1024]{1,0:T(8,128)(2,1)S(1)}, u32[]{:S(2)}, u32[]{:S(2)}) collective-permute-start(bf16[256,1024]{1,0:T(8,128)(2,1)} %collective-permute-done.9.refs_10_), channel_id=1, source_target_pairs={{0,16},{8,24},{16,0},{24,8},{1,17},{9,25},{17,1},{25,9},{2,18},{10... | collective-permute-start | bytes 1572872 | tf_op jit(solution)/shard_map/ppermute | solution.py:42
  381.3 32.7 %collective-permute-start.13 = (bf16[512,1024]{1,0:T(8,128)(2,1)}, bf16[512,1024]{1,0:T(8,128)(2,1)}, u32[]{:S(2)}, u32[]{:S(2)}) collective-permute-start(bf16[512,1024]{1,0:T(8,128)(2,1)} %pad_maximum_fusion.8), channel_id=1, source_target_pairs={{0,16},{8,24},{16,0},{24,8},{1,17},{9,25},{17,1},{25,9},{2,18},{10... | collective-permute-start | bytes 3145736 | tf_op jit(solution)/shard_map/ppermute | solution.py:42
  395.9 19.6 %collective-permute-start.15 = (bf16[512,1024]{1,0:T(8,128)(2,1)}, bf16[512,1024]{1,0:T(8,128)(2,1)}, u32[]{:S(2)}, u32[]{:S(2)}) collective-permute-start(bf16[512,1024]{1,0:T(8,128)(2,1)} %pad_maximum_fusion.9), channel_id=1, source_target_pairs={{0,8},{8,0},{16,24},{24,16},{1,9},{9,1},{17,25},{25,17},{2,10},{10... | collective-permute-start | bytes 3145736 | tf_op jit(solution)/shard_map/ppermute | solution.py:42
  405.4 192.6 %all-to-all-start.2 = ((bf16[8,512,256]{2,1,0:T(8,128)(2,1)}), bf16[8,512,256]{2,1,0:T(8,128)(2,1)S(1)}, u32[]{:S(2)}, u32[]{:S(2)}) async-start(bf16[8,512,256]{2,1,0:T(8,128)(2,1)} %bitcast.124), calls=%async_computation.2 | async-start | bytes 4194304 | tf_op jit(solution)/shard_map/all_to_all | solution.py:1455
  409.0 674.5 %reduce-scatter.15.cloned.1.call-start = ((), (), s32[]{:S(2)}) async-start(), calls=%async_computation.14 | async-start | bytes 5242880 | tf_op jit(solution)/shard_map/reduce_scatter | solution.py:1538
  769.6 313.9 %reduce-scatter.17.cloned.1.call-start = ((), (), s32[]{:S(2)}) async-start(), calls=%async_computation.15 | async-start | bytes 5242880 | tf_op jit(solution)/shard_map/reduce_scatter | solution.py:1538
  770.2 481.0 %reduce-scatter.9.cloned.1.call-start = ((), (), s32[]{:S(2)}) async-start(), calls=%async_computation.11 | async-start | bytes 5242880 | tf_op jit(solution)/shard_map/reduce_scatter | solution.py:1538
  796.4 454.8 %reduce-scatter.11.cloned.1.call-start = ((), (), s32[]{:S(2)}) async-start(), calls=%async_computation.12 | async-start | bytes 5242880 | tf_op jit(solution)/shard_map/reduce_scatter | solution.py:1538
  821.9 76.7 %collective-permute-start.17 = (bf16[2,1,512,1024]{3,2,1,0:T(8,128)(2,1)}, bf16[2,1,512,1024]{3,2,1,0:T(8,128)(2,1)S(1)}, u32[]{:S(2)}, u32[]{:S(2)}) collective-permute-start(bf16[2,1,512,1024]{3,2,1,0:T(8,128)(2,1)} %constant_dynamic-slice_fusion.8), channel_id=1, source_target_pairs={{0,8},{8,0},{16,24},{24,16},{1,9},{9,1},{17,25},{25,17},{2,10},{10... | collective-permute-start | bytes 6291464 | tf_op jit(solution)/shard_map/ppermute | solution.py:42
  825.2 79.7 %collective-permute-start.18 = (bf16[1,2,512,1024]{3,2,1,0:T(8,128)(2,1)}, bf16[1,2,512,1024]{3,2,1,0:T(8,128)(2,1)}, u32[]{:S(2)}, u32[]{:S(2)}) collective-permute-start(bf16[1,2,512,1024]{3,2,1,0:T(8,128)(2,1)} %constant_dynamic-slice_fusion.7), channel_id=1, source_target_pairs={{0,16},{8,24},{16,0},{24,8},{1,17},{9,25},{17,1},{25,9},{2,18},{10... | collective-permute-start | bytes 6291464 | tf_op jit(solution)/shard_map/ppermute | solution.py:42
  844.6 108.2 %all-to-all-start.3 = ((bf16[4,512,512]{2,1,0:T(8,128)(2,1)}), bf16[4,512,512]{2,1,0:T(8,128)(2,1)}, u32[]{:S(2)}, u32[]{:S(2)}) async-start(bf16[4,512,512]{2,1,0:T(8,128)(2,1)} %bitcast.102), calls=%async_computation.3 | async-start | bytes 4194304 | tf_op jit(solution)/shard_map/all_to_all | solution.py:1443
  849.3 55.6 %copy-start.20 = (bf16[2,2,512,1024]{3,2,1,0:T(8,128)(2,1)S(1)}, bf16[2,2,512,1024]{3,2,1,0:T(8,128)(2,1)}, u32[]{:S(2)}) copy-start(bf16[2,2,512,1024]{3,2,1,0:T(8,128)(2,1)} %copy-done.19) | copy-start | bytes 12582916
  908.5 38.7 %collective-permute-start.19 = (bf16[1,1,512,1024]{3,2,1,0:T(8,128)(2,1)}, bf16[1,1,512,1024]{3,2,1,0:T(8,128)(2,1)}, u32[]{:S(2)}, u32[]{:S(2)}) collective-permute-start(bf16[1,1,512,1024]{3,2,1,0:T(8,128)(2,1)} %constant_dynamic-slice_fusion.6), channel_id=1, source_target_pairs={{0,16},{8,24},{16,0},{24,8},{1,17},{9,25},{17,1},{25,9},{2,18},{10... | collective-permute-start | bytes 3145736 | tf_op jit(solution)/shard_map/ppermute | solution.py:42
  909.7 40.5 %collective-permute-start.20 = (bf16[1,1,512,1024]{3,2,1,0:T(8,128)(2,1)}, bf16[1,1,512,1024]{3,2,1,0:T(8,128)(2,1)}, u32[]{:S(2)}, u32[]{:S(2)}) collective-permute-start(bf16[1,1,512,1024]{3,2,1,0:T(8,128)(2,1)} %constant_dynamic-slice_fusion.5), channel_id=1, source_target_pairs={{0,8},{8,0},{16,24},{24,16},{1,9},{9,1},{17,25},{25,17},{2,10},{10... | collective-permute-start | bytes 3145736 | tf_op jit(solution)/shard_map/ppermute | solution.py:42
  920.9 115.8 %collective-permute-start.23 = (bf16[2048,1024]{1,0:T(8,128)(2,1)}, bf16[2048,1024]{1,0:T(8,128)(2,1)}, u32[]{:S(2)}, u32[]{:S(2)}) collective-permute-start(bf16[2048,1024]{1,0:T(8,128)(2,1)} %constant_dynamic-slice_fusion.2), channel_id=1, source_target_pairs={{0,4},{4,0},{1,5},{5,1},{2,6},{6,2},{3,7},{7,3},{8,12},{12,8},{9,1... | collective-permute-start | bytes 12582920 | tf_op jit(solution)/shard_map/ppermute | solution.py:33
  952.8 279.7 %all-to-all-start.1 = ((bf16[8,512,256]{2,1,0:T(8,128)(2,1)}), bf16[8,512,256]{2,1,0:T(8,128)(2,1)}, u32[]{:S(2)}, u32[]{:S(2)}) async-start(bf16[8,512,256]{2,1,0:T(8,128)(2,1)} %bitcast.123), calls=%async_computation.1 | async-start | bytes 4194304 | tf_op jit(solution)/shard_map/all_to_all | solution.py:1476
  957.2 355.5 %reduce-scatter.19.cloned.1.call-start = ((), (), s32[]{:S(2)}) async-start(), calls=%async_computation.18 | async-start | bytes 5242880
  958.8 37.5 %copy-start.1 = (f32[2048,2]{1,0:T(8,128)S(1)}, f32[2048,2]{1,0:T(8,128)}, u32[]{:S(2)}) copy-start(f32[2048,2]{1,0:T(8,128)} %copy-done) | copy-start | bytes 49156
  958.8 37.5 %copy-start.3 = (f32[2048,128]{1,0:T(8,128)S(1)}, f32[2048,128]{1,0:T(8,128)}, u32[]{:S(2)}) copy-start(f32[2048,128]{1,0:T(8,128)} %copy-done.2) | copy-start | bytes 3145732
  958.8 37.5 %copy-start.6 = (f32[2,512]{1,0:T(2,128)S(1)}, f32[2,512]{1,0:T(2,128)}, u32[]{:S(2)}) copy-start(f32[2,512]{1,0:T(2,128)} %copy-done.5) | copy-start | bytes 12292
  1010.8 3.6 collective-permute-start.21
  1017.5 8.4 collective-permute-start.22
  1020.1 217.4 %collective-permute-start.32 = (bf16[512,1024]{1,0:T(8,128)(2,1)}, bf16[512,1024]{1,0:T(8,128)(2,1)}, u32[]{:S(2)}, u32[]{:S(2)}) collective-permute-start(bf16[512,1024]{1,0:T(8,128)(2,1)} %get-tuple-element.266), channel_id=1, source_target_pairs={{0,4},{6,2},{1,5},{7,3},{8,12},{14,10},{9,13},{15,11},{16,20},{22,... | collective-permute-start | bytes 3145736 | tf_op jit(solution)/shard_map/ppermute | solution.py:1549
  1023.0 214.6 %collective-permute-start.31 = (bf16[512,1024]{1,0:T(8,128)(2,1)}, bf16[512,1024]{1,0:T(8,128)(2,1)}, u32[]{:S(2)}, u32[]{:S(2)}) collective-permute-start(bf16[512,1024]{1,0:T(8,128)(2,1)} %get-tuple-element.266), channel_id=1, source_target_pairs={{2,4},{4,2},{3,5},{5,3},{10,12},{12,10},{11,13},{13,11},{18,20},{2... | collective-permute-start | bytes 3145736 | tf_op jit(solution)/shard_map/ppermute | solution.py:1548
  1024.6 212.9 %collective-permute-start.30 = (bf16[512,1024]{1,0:T(8,128)(2,1)}, bf16[512,1024]{1,0:T(8,128)(2,1)}, u32[]{:S(2)}, u32[]{:S(2)}) collective-permute-start(bf16[512,1024]{1,0:T(8,128)(2,1)} %get-tuple-element.265), channel_id=1, source_target_pairs={{2,0},{4,6},{3,1},{5,7},{10,8},{12,14},{11,9},{13,15},{18,16},{20,... | collective-permute-start | bytes 3145736 | tf_op jit(solution)/shard_map/ppermute | solution.py:1547
  1043.5 341.4 %reduce-scatter.13.cloned.1.call-start = ((), (), s32[]{:S(2)}) async-start(), calls=%async_computation.13 | async-start | bytes 1310720 | tf_op jit(solution)/shard_map/reduce_scatter | solution.py:1563
  1083.6 152.1 %collective-permute-start.33 = (f32[4,2048]{1,0:T(4,128)S(1)}, f32[4,2048]{1,0:T(4,128)S(1)}, u32[]{:S(2)}, u32[]{:S(2)}) collective-permute-start(f32[4,2048]{1,0:T(4,128)S(1)} %pad_maximum_fusion.10), channel_id=1, source_target_pairs={{0,8},{8,0},{16,24},{24,16},{1,9},{9,1},{17,25},{25,17},{2,10},{10... | collective-permute-start | bytes 98312 | tf_op jit(solution)/shard_map/ppermute | solution.py:42
  1235.8 9.2 collective-permute-start.34
  1245.0 7.5 collective-permute-start.35
  1245.1 53.2 %copy-start.27 = (f32[256,3,512]{0,2,1:T(8,128)S(1)}, f32[256,3,512]{0,2,1:T(8,128)}, u32[]{:S(2)}) copy-start(f32[256,3,512]{0,2,1:T(8,128)} %copy.122) | copy-start | bytes 4718596
  1246.2 67.2 %collective-permute-start.26 = (bf16[256,2048]{1,0:T(8,128)(2,1)}, bf16[256,2048]{1,0:T(8,128)(2,1)}, u32[]{:S(2)}, u32[]{:S(2)}) collective-permute-start(bf16[256,2048]{1,0:T(8,128)(2,1)} %get-tuple-element.270), channel_id=1, source_target_pairs={{0,4},{6,2},{1,5},{7,3},{8,12},{14,10},{9,13},{15,11},{16,20},{22,... | collective-permute-start | bytes 3145736 | tf_op jit(solution)/shard_map/ppermute | solution.py:1549
  1249.6 66.0 %collective-permute-start.25 = (bf16[256,2048]{1,0:T(8,128)(2,1)}, bf16[256,2048]{1,0:T(8,128)(2,1)}, u32[]{:S(2)}, u32[]{:S(2)}) collective-permute-start(bf16[256,2048]{1,0:T(8,128)(2,1)} %get-tuple-element.270), channel_id=1, source_target_pairs={{2,4},{4,2},{3,5},{5,3},{10,12},{12,10},{11,13},{13,11},{18,20},{2... | collective-permute-start | bytes 3145736 | tf_op jit(solution)/shard_map/ppermute | solution.py:1548
  1251.2 64.4 %collective-permute-start.24 = (bf16[256,2048]{1,0:T(8,128)(2,1)S(1)}, bf16[256,2048]{1,0:T(8,128)(2,1)}, u32[]{:S(2)}, u32[]{:S(2)}) collective-permute-start(bf16[256,2048]{1,0:T(8,128)(2,1)S(1)} %get-tuple-element.269), channel_id=1, source_target_pairs={{2,0},{4,6},{3,1},{5,7},{10,8},{12,14},{11,9},{13,15},{18,16},{20,... | collective-permute-start | bytes 3145736 | tf_op jit(solution)/shard_map/ppermute | solution.py:1547
  1252.5 45.8 %copy-start.25 = (f32[256,3,512]{0,2,1:T(8,128)S(1)}, f32[256,3,512]{0,2,1:T(8,128)}, u32[]{:S(2)}) copy-start(f32[256,3,512]{0,2,1:T(8,128)} %copy.131) | copy-start | bytes 4718596
  1252.5 45.8 %copy-start.26 = (f32[256,3,512]{0,2,1:T(8,128)S(1)}, f32[256,3,512]{0,2,1:T(8,128)}, u32[]{:S(2)}) copy-start(f32[256,3,512]{0,2,1:T(8,128)} %copy.124) | copy-start | bytes 4718596
  1252.6 45.7 %collective-permute-start.36 = (f32[4,2048]{1,0:T(4,128)S(1)}, f32[4,2048]{1,0:T(4,128)S(1)}, u32[]{:S(2)}, u32[]{:S(2)}) collective-permute-start(f32[4,2048]{1,0:T(4,128)S(1)} %add.356), channel_id=1, source_target_pairs={{0,2},{2,0},{1,3},{3,1},{4,6},{6,4},{5,7},{7,5},{8,10},{10,8},{9,1... | collective-permute-start | bytes 98312 | tf_op jit(solution)/shard_map/ppermute | solution.py:42
  1298.3 13.6 collective-permute-start.37
  1310.5 13.6 collective-permute-start.29
  1311.9 12.3 collective-permute-start.28
  1313.4 65.5 %collective-permute-start.27 = (bf16[256,2048]{1,0:T(8,128)(2,1)}, bf16[256,2048]{1,0:T(8,128)(2,1)S(1)}, u32[]{:S(2)}, u32[]{:S(2)}) collective-permute-start(bf16[256,2048]{1,0:T(8,128)(2,1)} %get-tuple-element.267), channel_id=1, source_target_pairs={{2,0},{4,6},{3,1},{5,7},{10,8},{12,14},{11,9},{13,15},{18,16},{20,... | collective-permute-start | bytes 3145736 | tf_op jit(solution)/shard_map/ppermute | solution.py:1547
  1315.6 63.3 %copy-start.29 = (bf16[256,2048]{1,0:T(8,128)(2,1)S(1)}, bf16[256,2048]{1,0:T(8,128)(2,1)}, u32[]{:S(2)}) copy-start(bf16[256,2048]{1,0:T(8,128)(2,1)} %get-tuple-element.267) | copy-start | bytes 3145732
  1315.6 63.3 %copy-start.32 = (f32[256,2048]{1,0:T(8,128)S(1)}, f32[256,2048]{1,0:T(8,128)}, u32[]{:S(2)}) copy-start(f32[256,2048]{1,0:T(8,128)} %param.41) | copy-start | bytes 6291460
  1315.6 63.3 %copy-start.33 = (f32[256,2048]{1,0:T(8,128)S(1)}, f32[256,2048]{1,0:T(8,128)}, u32[]{:S(2)}) copy-start(f32[256,2048]{1,0:T(8,128)} %param.40) | copy-start | bytes 6291460
  1324.2 60.8 %copy-start.40 = (f32[128,1024]{1,0:T(8,128)S(1)}, f32[128,1024]{1,0:T(8,128)}, u32[]{:S(2)}) copy-start(f32[128,1024]{1,0:T(8,128)} %param.37) | copy-start | bytes 1572868
  1324.2 60.8 %copy-start.41 = (f32[128,1024]{1,0:T(8,128)S(1)}, f32[128,1024]{1,0:T(8,128)}, u32[]{:S(2)}) copy-start(f32[128,1024]{1,0:T(8,128)} %param.36) | copy-start | bytes 1572868
  (45 other events, 312.4 us)
Sparse Core Ops, SparseCore 0:
  10.2 55.9 all-gather.7
  155.8 69.8 all-gather.9
  244.9 19.1 all-gather.5
  769.8 51.2 reduce-scatter.14
  824.2 83.6 reduce-scatter.16
  910.7 63.2 reduce-scatter.8
  977.3 52.6 reduce-scatter.10
  1043.6 57.9 reduce-scatter.18
  1312.9 47.3 reduce-scatter.12

commit v2 on v1

--- a/solution.py
+++ b/solution.py
@@ -322,7 +322,7 @@
         name="first_gather",
     )(tokens, low, post)
     x_full = x_full.transpose(1, 0, 2).reshape(seq_len, width)
-    return x_full, w_full, post_all.transpose(1, 0, 2).reshape(2, width)
+    return x_full, w_full, post_all
 
 
 def doc_start(ends_ref, docs, places):
@@ -1042,19 +1042,21 @@
 
 def gate_up_body(tile, w, need, ti, outs, y, mid):
     hidden_width = w[0].shape[1]
-    nb = min(512, hidden_width)
+    nb = min(256, hidden_width)
+    mb = min(128, tile.shape[0])
     count = hidden_width // nb
     need(0)
     need(1)
 
     def step(n):
         cols = columns(n, nb)
-        rows = tile[...]
-        gate = jnp.dot(rows, w[0][:, cols], preferred_element_type=f32)
-        up = jnp.dot(rows, w[1][:, cols], preferred_element_type=f32)
-        outs[0][:, cols] = gate.astype(bf16)
-        outs[1][:, cols] = up.astype(bf16)
-        outs[2][:, cols] = (gate * jax.nn.sigmoid(gate) * up).astype(bf16)
+        for m in range(tile.shape[0] // mb):
+            at = slice(m * mb, (m + 1) * mb)
+            gate = jnp.dot(tile[at, :], w[0][:, cols], preferred_element_type=f32)
+            up = jnp.dot(tile[at, :], w[1][:, cols], preferred_element_type=f32)
+            outs[0][at, cols] = gate.astype(bf16)
+            outs[1][at, cols] = up.astype(bf16)
+            outs[2][at, cols] = (gate * jax.nn.sigmoid(gate) * up).astype(bf16)
 
     loop(0, count // 2, step)
     mid()
@@ -1106,14 +1108,15 @@
     loop(0, w[1].shape[0] // nd, second)
 
 
-gate_up_job = Job(True, False, True, 2, 7, 0, True, 0, 3, 2, 0, gate_up_body)
+gate_up_job = Job(True, False, False, 2, 7, 0, True, 0, 3, 2, 0, gate_up_body)
 down_job = Job(False, True, False, 1, 2, 1, False, 0, 0, 1, 2, down_body)
 back_job = Job(True, True, False, 3, 0, 0, False, 2, 2, 1, 1, back_body)
 
 
 def last_kernel(
-    chunks, dx_ref, grad_ref, out_ref, sum_ref, own, from_row, near, from_t, give, from_zh,
-    g_own, g_in, g_sum, g_late,
+    chunks, dx_ref, grad_ref, far_one, far_two, out_ref, sum_ref, far_out_one, far_out_two,
+    own, from_row, near, from_t, give, from_zh,
+    g_own, g_in, g_sum, g_late, stay_one, stay_two, late_one, late_two, far_local, far_send, far_recv,
     own_sem, row_send, row_recv, t_send, t_recv, zh_send, zh_recv, g_sem, d_send, d_recv, f_send, f_recv,
 ):
     n_dp = lax.axis_size("dp")
@@ -1149,6 +1152,48 @@
     for dev in partners:
         pl.semaphore_signal(barrier, inc=1, device_id=dev, device_id_type=pl.DeviceIdType.MESH)
     pl.semaphore_wait(barrier, len(partners))
+
+    fars = [(far_one, far_out_one, stay_one, late_one), (far_two, far_out_two, stay_two, late_two)]
+
+    def far_copies(i):
+        pieces, _, stay, late = fars[i]
+        return (
+            pltpu.make_async_copy(pieces.at[r], stay, far_local.at[i]),
+            remote(pieces.at[1 - r], late.at[0], far_send.at[i, 0], far_recv.at[i, 0], row_dev),
+            remote(pieces.at[r], late.at[0], far_send.at[i, 1], far_recv.at[i, 1], zh_dev),
+            remote(pieces.at[1 - r], late.at[1], far_send.at[i, 2], far_recv.at[i, 2], cross_dev),
+        )
+
+    def far_start(i):
+        @pl.when(same)
+        def _():
+            far_copies(i)[0].start()
+            far_copies(i)[1].start()
+
+        @pl.when(other_core)
+        def _():
+            far_copies(i)[2].start()
+            far_copies(i)[3].start()
+
+    def far_end(i):
+        pieces, total, stay, late = fars[i]
+
+        @pl.when(same)
+        def _():
+            far_copies(i)[0].wait()
+            far_copies(i)[2].wait_recv()
+            total[...] = stay[...].astype(f32) + late[0].astype(f32)
+            far_copies(i)[1].wait_send()
+
+        @pl.when(other_core)
+        def _():
+            far_copies(i)[1].wait_recv()
+            far_copies(i)[3].wait_recv()
+            total[...] = late[0].astype(f32) + late[1].astype(f32)
+            far_copies(i)[2].wait_send()
+            far_copies(i)[3].wait_send()
+
+    far_start(0)
 
     def cols_at(which):
         return pl.ds(pl.multiple_of(which * half, half), half)
@@ -1237,6 +1282,7 @@
     to_zh = remote(g_sum.at[r], g_late.at[0], f_send.at[1], f_recv.at[1], zh_dev)
     to_cross = remote(g_sum.at[1 - r], g_late.at[1], f_send.at[2], f_recv.at[2], cross_dev)
 
+    far_start(1)
     for c in range(chunks):
         row_stage(c)
         if c >= 2:
@@ -1272,11 +1318,13 @@
         to_zh.wait_send()
         to_cross.wait_send()
 
+    far_end(0)
+    far_end(1)
     for cp in rows_copies + g_copies + list(t_copies.values()) + zh_copies:
         cp.wait_send()
 
 
-def last_sums(dx, grad):
+def last_sums(dx, grad, fars):
     n_dp = lax.axis_size("dp")
     tp = lax.axis_size("zl")
     seq_len, width = dx.shape
@@ -1291,11 +1339,12 @@
     dma = pltpu.SemaphoreType.DMA
     return pl.pallas_call(
         functools.partial(last_kernel, chunks),
-        in_specs=[anywhere] * 2,
-        out_specs=[vmem] * 2,
+        in_specs=[anywhere] * 4,
+        out_specs=[vmem] * 4,
         out_shape=[
             jax.ShapeDtypeStruct((2 * seq_len, feat), f32),
             jax.ShapeDtypeStruct((part, cols), f32),
+            *[jax.ShapeDtypeStruct(v.shape[1:], f32) for v in fars],
         ],
         scratch_shapes=[
             pltpu.VMEM((chunks, step, half), bf16),
@@ -1308,6 +1357,11 @@
             pltpu.VMEM((n_dp - 1, 2, part, cols), bf16),
             pltpu.VMEM((2, part, cols), bf16),
             pltpu.VMEM((2, part, cols), bf16),
+            *[pltpu.VMEM(v.shape[1:], bf16) for v in fars],
+            *[pltpu.VMEM(v.shape, bf16) for v in fars],
+            dma((2,)),
+            dma((2, 3)),
+            dma((2, 3)),
             dma((chunks,)),
             dma((chunks,)),
             dma((chunks,)),
@@ -1324,7 +1378,7 @@
         compiler_params=pltpu.CompilerParams(collective_id=4, has_side_effects=True, vmem_limit_bytes=60 << 20),
         cost_estimate=pl.CostEstimate(flops=0, bytes_accessed=8 * seq_len * width, transcendentals=0),
         name="last_sums",
-    )(dx, grad)
+    )(dx, grad, *fars)
 
 
 def rotary(seq_len):
@@ -1381,10 +1435,19 @@
     mine = seq_len // group
     col_width = qkv_weight.shape[2]
 
-    ends = jnp.cumsum(jnp.where(same, doc_lengths, swap(doc_lengths, "row")), axis=1)[0]
-
     qkv_low = jnp.concatenate([qkv_weight[:, i, :].astype(bf16) for i in range(3)], axis=1)
-    x_full, qkv_full, post_all = first_gather(tokens, qkv_low, post_gains.T)
+    docs = doc_lengths.shape[1]
+    small = [post_gains.T.reshape(-1), head_gains.reshape(-1), doc_lengths[0].astype(f32)]
+    small = jnp.concatenate(small)
+    pad = -small.shape[0] % 1024
+    small = jnp.concatenate([small, jnp.zeros((pad,), f32)]).reshape(-1, 128)
+    x_full, qkv_full, small_all = first_gather(tokens, qkv_low, small)
+    small_all = small_all.reshape(2 * n_col, -1)
+    cut_one, cut_two = 2 * feat, 2 * feat + 2 * col_width
+    post_all = small_all[:, :cut_one].reshape(2 * n_col, 2, feat).transpose(1, 0, 2).reshape(2, width)
+    gains = lax.dynamic_slice_in_dim(small_all, block_at, 1, 0)[0, cut_one:cut_two].reshape(2, col_width)
+    lengths = lax.dynamic_slice_in_dim(small_all, g * n_col, 1, 0)[0, cut_two : cut_two + docs]
+    ends = jnp.cumsum(lengths.astype(jnp.int32))
     x_tok = lax.dynamic_slice_in_dim(x_full, block_at * mine, mine, 0)
 
     def halves(quarter):
@@ -1410,7 +1473,6 @@
     out_part = lax.all_gather(out_part, "dp", axis=1)
 
     cos_two, sin_two = rotary(seq_len)
-    gains = jnp.where(same, head_gains, swap(head_gains, "zh"))
     qkv = matmul(x_full, qkv_full)
     squares = jnp.stack(
         [
@@ -1485,10 +1547,17 @@
         back_job, 3, "feed_back", grad_m.astype(bf16), [[down_full], [gate_full], [up_full]], [tall, wide, wide],
         [gate_all, up_all], [hidden_width] * 2, width, 3 * work,
     )
-    grad_down_w = matmul(hidden, dm_full, TN).astype(bf16)
+    dh_tok = cot_tok + dh_sum
+
+    grad_a, grad_gain_attn = norm_back(a_pre, a_scale, gain_attn, dh_tok)
+    grad_a = grad_a.astype(bf16)
+    datt = matmul(grad_a, out_full, NT).astype(bf16)
+    datt, hidden, h_full = tie(datt, hidden, h_full)
+    grad_att = to_heads(datt)
     grad_gate_w = matmul(h_full, grad_gate, TN).astype(bf16)
     grad_up_w = matmul(h_full, grad_up, TN).astype(bf16)
-    dh_tok = cot_tok + dh_sum
+    grad_down_w = matmul(hidden, dm_full, TN).astype(bf16)
+    grad_out = matmul(att_tok, grad_a, TN).astype(bf16)
 
     low_bit, high_bit = d % 2, d // 2
 
@@ -1503,17 +1572,35 @@
     down_one = trade(view[..., : width // 2], 1, 1, low_bit)
     down_two = trade(view[..., width // 2 :], 0, 2, high_bit)
 
-    grad_a, grad_gain_attn = norm_back(a_pre, a_scale, gain_attn, dh_tok)
-    grad_a = grad_a.astype(bf16)
-    grad_att = to_heads(matmul(grad_a, out_full, NT).astype(bf16))
-    grad_out = matmul(att_tok, grad_a, TN).astype(bf16)
-
-    ends, down_one, down_two = tie(ends, down_one, down_two)
     dqt, dk, dv = attend_back(query, key, key_t, value, grad_att, att, log_total, ends)
+    inv_scale, down_one, down_two = tie(inv_scale, down_one, down_two)
     down_one = trade(down_one, 0, 2, high_bit)[0, 0]
     down_two = trade(down_two, 1, 1, low_bit)[0, 0]
-    inv_scale, down_one, down_two = tie(inv_scale, down_one, down_two)
     weighted, inner, grad_head = unturn(dqt, dk, qkv, inv_scale, gains, cos_two, sin_two)
+    def data_sums(grad):
+        half = grad.shape[0] // 2
+        return [
+            lax.psum_scatter(grad[i * half : (i + 1) * half], "dp", scatter_dimension=0, tiled=True)
+            for i in range(2)
+        ]
+
+    def owner_parts(pieces):
+        keep = jnp.where(r == 0, pieces[0], pieces[1])
+        give = jnp.where(r == 0, pieces[1], pieces[0])
+        axes = ("row", "zh")
+        return [
+            keep,
+            lax.ppermute(keep, axes, [(1, 0), (2, 3)]),
+            lax.ppermute(give, axes, [(1, 2), (2, 1)]),
+            lax.ppermute(give, axes, [(0, 2), (3, 1)]),
+        ]
+
+    gate_parts = owner_parts(data_sums(grad_gate_w))
+    up_sums = data_sums(grad_up_w)
+    inner, *gate_parts = tie(inner, *gate_parts)
+    sum_gate = jnp.where(same, gate_parts[0].astype(f32), 0.0)
+    for part in gate_parts[1:]:
+        sum_gate = sum_gate + part.astype(f32)
     inner = (small_sum(inner.T, ("row", "zl")) / width).T
     cube = inv_scale * inv_scale * inv_scale * inner
     dqkv = jnp.concatenate(
@@ -1529,31 +1616,11 @@
     dx = matmul(dqkv, qkv_full, NT).astype(bf16)
     here = lax.dynamic_slice_in_dim(dx, block_at * mine, mine, 0).astype(f32) + dh_tok
     dx = lax.dynamic_update_slice_in_dim(dx, here.astype(bf16), block_at * mine, 0)
-    dtokens, sum_qkv = last_sums(dx, grad_qkv)
+    dtokens, sum_qkv, sum_up, sum_down = last_sums(
+        dx, grad_qkv, [jnp.stack(up_sums), jnp.stack([down_one, down_two])]
+    )
     sum_qkv = sum_qkv.reshape(qkv_first.shape)
 
-    def data_sums(grad):
-        half = grad.shape[0] // 2
-        return [
-            lax.psum_scatter(grad[i * half : (i + 1) * half], "dp", scatter_dimension=0, tiled=True)
-            for i in range(2)
-        ]
-
-    def to_owner(pieces):
-        keep = jnp.where(r == 0, pieces[0], pieces[1])
-        give = jnp.where(r == 0, pieces[1], pieces[0])
-        axes = ("row", "zh")
-        total = jnp.where(same, keep.astype(f32), 0.0)
-        total = total + lax.ppermute(keep, axes, [(1, 0), (2, 3)]).astype(f32)
-        total = total + lax.ppermute(give, axes, [(1, 2), (2, 1)]).astype(f32)
-        return total + lax.ppermute(give, axes, [(0, 2), (3, 1)]).astype(f32)
-
-    sum_down = to_owner([down_one, down_two])
-    gate_sums, up_sums = data_sums(grad_gate_w), data_sums(grad_up_w)
-    *gate_sums, grad_head = tie(*gate_sums, grad_head)
-    *up_sums, sum_qkv = tie(*up_sums, sum_qkv)
-    sum_gate = to_owner(gate_sums)
-    sum_up = to_owner(up_sums)
     half_w = width // 2
     half = lax.dynamic_slice_in_dim(grad_out, r * half_w, half_w, 1).astype(f32) + swap(
         lax.dynamic_slice_in_dim(grad_out, (1 - r) * half_w, half_w, 1), "row"

time: 1400 us -> 1380 us (0.986)
  waiting for transfers between devices: 246 us -> 183 us
  Pallas kernels: 683 us -> 717 us
    pallas_call x1, Pallas kernels: 140 us -> 195 us  [last_sums(): pl.pallas_call(functools.partial(last_kernel, chunks), in_specs=[anywhere...]
    ppermute x21, waiting for transfers between devices: 115 us -> 84.3 us  [swap_bit(): lax.ppermute(piece, axis, [(i, i ^ bit) for i in range(lax.axis_size(axis...]
    ppermute x9 -> x3, waiting for transfers between devices: 54.7 us -> 29.3 us  [the longest x1 29.3 us: owner_parts(): lax.ppermute(keep, axes, [(1, 0), (2, 3)])]
    ppermute x8 -> x6, waiting for transfers between devices: 75.7 us -> 68.8 us  [swap(): return lax.ppermute(piece, axis, [(0, 1), (1, 0)])]
    unnamed x123 -> x133, local copies, waits for them, and re-layouts: 38.4 us -> 40.8 us
  transfers between devices with their start and end apart: 51 -> 43, of which waited for: 11 -> 11; matrix products, arithmetic and copies ran while one was open for 23% -> 22% of each run, Pallas kernels for 39% -> 42%
where the time goes in v2:
time: 1380 us; the launch traced here: 1370 us
  Pallas kernels  717 us (52%)
  waiting for transfers between devices  183 us (13%)
  matrix products  144 us (10%)
  other arithmetic  125 us (9%)
  local copies, waits for them, and re-layouts  107 us (8%)
  starting transfers between devices  79.6 us (6%)
  between operations  15.2 us (1%)
    pallas_call x3, Pallas kernels, tile_call(): pl.pallas_call(functools.partial(tile_kernel, job, tp, chunks), in_specs=...  306 us
    pallas_call x1, Pallas kernels, last_sums(): pl.pallas_call(functools.partial(last_kernel, chunks), in_specs=[anywhere...  195 us
    dot_general x9, matrix products, matmul(): return lax.dot_general(left, right, dims, preferred_element_type=f32)  144 us
    pallas_call x1, Pallas kernels, first_gather(): pl.pallas_call(functools.partial(gather_kernel, chunks), in_specs=[anywhe...  134 us
    ppermute x21, waiting for transfers between devices, swap_bit(): lax.ppermute(piece, axis, [(i, i ^ bit) for i in range(lax.axis_size(axis...  84.3 us
    ppermute x6, waiting for transfers between devices, swap(): return lax.ppermute(piece, axis, [(0, 1), (1, 0)])  68.8 us
    unnamed x133, local copies, waits for them, and re-layouts  40.8 us
    pallas_call x1, Pallas kernels, attend_back(): pl.pallas_call(functools.partial(attend_back_kernel, docs, block), grid_s...  30.8 us
  transfers between devices with their start and end apart: 43, of which 11 were waited for; matrix products, arithmetic and copies ran while one was open for 22% of the time, Pallas kernels for 42%

profile of v2, /device:TPU:0, one launch (start us, length us, event | category | flops | bytes accessed | tf_op | source)
XLA Modules:
  0.0 1370.4 jit_solution(308521529465140996)
XLA Ops:
  9.1 3.2 convert.8
  15.1 134.5 %first_gather.1 = (bf16[8,2048,256]{2,1,0:T(8,128)(2,1)}, bf16[2048,1536]{1,0:T(8,128)(2,1)}, f32[8,16,128]{2,1,0:T(8,128)}, bf16[256,1536]{1,0:T(8,128)(2,1)}) custom-call(bf16[4096,256]{1,0:T(8,128)(2,1)} %tok_ref.1, bf16[1024,1536]{1,0:T(8,128)(2,1)} %pad_maximum_fusion.1.low_ref, f32[16,128]{1,0:T(8,128)} %bitcast.172), custom_call_target="tpu_custom_call" | custom-call | bytes 25165824 | tf_op jit(solution)/shard_map/first_gather/pallas_call | solution.py:292
  154.1 7.8 copy.134
  161.9 17.5 %fusion.39.qkv_ref = f32[2048,1536]{1,0:T(8,128)S(1)} fusion(bf16[2048,2048]{1,0:T(8,128)(2,1)} %bitcast.127, bf16[2048,1536]{1,0:T(8,128)(2,1)} %get-tuple-element.92), kind=kOutput, calls=%fused_computation.133 | convolution fusion | flops 12884901888 | bytes 27262976 | tf_op jit(solution)/shard_map/dot_general | solution.py:1417
  180.2 21.3 %collective-permute-start.3 = (bf16[256,1024]{1,0:T(8,128)(2,1)}, bf16[256,1024]{1,0:T(8,128)(2,1)}, u32[]{:S(2)}, u32[]{:S(2)}) collective-permute-start(bf16[256,1024]{1,0:T(8,128)(2,1)} %get-tuple-element.93), channel_id=1, source_target_pairs={{0,2},{2,0},{1,3},{3,1},{4,6},{6,4},{5,7},{7,5},{8,10},{10,8},{9,1... | collective-permute-start | bytes 1572872 | tf_op jit(solution)/shard_map/ppermute | solution.py:33
  201.6 3.9 fusion.13
  207.7 5.9 collective-permute-done.2
  216.7 8.7 collective-permute-done.3.refs_2_
  225.3 12.0 prepare.1
  244.9 32.6 %collective-permute-done.refs_3_ = bf16[256,1024]{1,0:T(8,128)(2,1)} collective-permute-done((bf16[256,1024]{1,0:T(8,128)(2,1)S(1)}, bf16[256,1024]{1,0:T(8,128)(2,1)}, u32[]{:S(2)}, u32[]{:S(2)}) %collective-permute-start) | collective-permute-done | bytes 524320 | tf_op jit(solution)/shard_map/ppermute | solution.py:33
  282.1 23.5 %attend.1 = (bf16[2048,512]{1,0:T(8,128)(2,1)S(1)}, f32[4,1,2048]{2,1,0:T(1,128)S(1)}) custom-call(s32[4]{0:T(128)S(1)} %bitcast.122, bf16[2048,512]{1,0:T(8,128)(2,1)S(1)} %copy-done.8, bf16[2048,512]{1,0:T(8,128)(2,1)} %get-tuple-element.96.k_ref, bf16[512,2048]{1,0:T(8,128)(2,1)} %get-tuple-element.97.vt_ref), custom_call_target="tpu_custom_call" | custom-call | flops 4294967296 | bytes 8388608 | tf_op jit(solution)/shard_map/attend/pallas_call | solution.py:378
  308.4 3.6 all-to-all-start
  317.1 6.1 collective-permute-start.9
  328.8 6.2 convert_element_type.184.refs_1_
  335.0 6.2 convert_element_type.185.refs_8_
  345.3 27.5 %collective-permute-done.7.refs_10_ = bf16[256,1024]{1,0:T(8,128)(2,1)} collective-permute-done((bf16[256,1024]{1,0:T(8,128)(2,1)}, bf16[256,1024]{1,0:T(8,128)(2,1)}, u32[]{:S(2)}, u32[]{:S(2)}) %collective-permute-start.7) | collective-permute-done | bytes 524320 | tf_op jit(solution)/shard_map/ppermute | solution.py:33
  377.2 10.8 collective-permute-done.12.refs_13_
  390.9 9.5 multiply_reduce_fusion.5
  400.4 3.6 all-to-all-start.2
  404.1 4.9 fusion.refs_0_
  411.6 106.1 %gate_up.1 = (bf16[2048,2048]{1,0:T(8,128)(2,1)}, bf16[2048,2048]{1,0:T(8,128)(2,1)}, bf16[2048,2048]{1,0:T(8,128)(2,1)}, bf16[2048,2048]{1,0:T(8,128)(2,1)}, bf...) custom-call(bf16[512,2048]{1,0:T(8,128)(2,1)} %fusion.refs_0_, ...), custom_call_target="tpu_custom_call" | custom-call | flops 34359738368 | bytes 33554432 | tf_op jit(solution)/shard_map/gate_up/pallas_call | solution.py:1017
  517.7 65.3 %down.1 = (bf16[2048,2048]{1,0:T(8,128)(2,1)}, f32[512,2048]{1,0:T(8,128)}) custom-call(bf16[2048,2048]{1,0:T(8,128)(2,1)} %get-tuple-element.126.refs_0_, bf16[2048,1024]{1,0:T(8,128)(2,1)} %convert_element_type.187.refs_1_, bf16[2048,1024]{1,0:T(8,128)(2,1)} %get-tuple-element.115.refs_2_), custom_call_target="tpu_custom_call" | custom-call | flops 17179869184 | bytes 33554432 | tf_op jit(solution)/shard_map/down/pallas_call | solution.py:1017
  586.6 3.2 copy-done.17
  591.9 4.6 subtract_convert_fusion.3
  596.6 135.0 %feed_back.1 = (bf16[2048,2048]{1,0:T(8,128)(2,1)}, bf16[2048,2048]{1,0:T(8,128)(2,1)}, bf16[2048,2048]{1,0:T(8,128)(2,1)}, f32[512,2048]{1,0:T(8,128)}) custom-call(bf16[512,2048]{1,0:T(8,128)(2,1)} %get-tuple-element.262.refs_0_, bf16[2048,2048]{1,0:T(8,128)(2,1)} %get-tuple-element.119.refs_1_, bf16[2048,2048]{1,0:T(8,128)(2,1)} %get-tuple-element.120.refs_2_, ...), custom_call_target="tpu_custom_call" | custom-call | flops 51539607552 | bytes 33554432 | tf_op jit(solution)/shard_map/feed_back/pallas_call | solution.py:1017
  731.6 6.2 multiply_reduce_fusion.1
  740.0 9.5 convolution_convert_fusion.6
  749.6 21.1 %convolution_convert_fusion.3 = bf16[2048,2048]{1,0:T(8,128)(2,1)S(1)} fusion(bf16[2048,2048]{1,0:T(8,128)(2,1)S(1)} %bitcast.180, bf16[2048,2048]{1,0:T(8,128)(2,1)} %get-tuple-element.138), kind=kOutput, calls=%fused_computation.4 | convolution fusion | flops 17184063488 | bytes 25165824 | tf_op jit(solution)/shard_map/dot_general | solution.py:1417
  770.6 3.6 fusion.33
  774.9 22.4 %convolution_convert_fusion.1 = bf16[2048,2048]{1,0:T(8,128)(2,1)S(1)} fusion(bf16[2048,2048]{1,0:T(8,128)(2,1)} %get-tuple-element.137, bf16[2048,2048]{1,0:T(8,128)(2,1)} %get-tuple-element.141), kind=kOutput, calls=%fused_computation.2 | convolution fusion | flops 17184063488 | bytes 25165824 | tf_op jit(solution)/shard_map/dot_general | solution.py:1417
  797.3 3.6 fusion.32
  802.5 4.4 all-to-all-start.3
  807.0 23.9 %convolution_convert_fusion.4 = bf16[2048,2048]{1,0:T(8,128)(2,1)} fusion(bf16[2048,2048]{1,0:T(8,128)(2,1)} %get-tuple-element.126.refs_0_, bf16[2048,2048]{1,0:T(8,128)(2,1)} %get-tuple-element.127), kind=kOutput, calls=%fused_computation.5 | convolution fusion | flops 17184063488 | bytes 25165824 | tf_op jit(solution)/shard_map/dot_general | solution.py:1417
  830.9 5.3 fusion.34
  840.9 3.2 constant_dynamic-slice_fusion.7
  847.1 4.7 convolution_convert_fusion
  854.6 2.9 copy-done.25
  857.8 59.4 %collective-permute-done.15 = bf16[2,1,512,1024]{3,2,1,0:T(8,128)(2,1)} collective-permute-done((bf16[2,1,512,1024]{3,2,1,0:T(8,128)(2,1)}, bf16[2,1,512,1024]{3,2,1,0:T(8,128)(2,1)}, u32[]{:S(2)}, u32[]{:S(2)}) %collective-permute-start.15) | collective-permute-done | bytes 2097184 | tf_op jit(solution)/shard_map/ppermute | solution.py:42
  919.8 3.3 add_convert_fusion.2
  927.3 4.6 all-to-all-start.1
  933.6 30.8 %attend_back.1 = (f32[512,2048]{1,0:T(8,128)}, f32[2048,512]{1,0:T(8,128)}, bf16[2048,512]{1,0:T(8,128)(2,1)S(1)}) custom-call(s32[4]{0:T(128)S(1)} %bitcast.123, bf16[2048,512]{1,0:T(8,128)(2,1)S(1)} %copy-done.9, bf16[2048,512]{1,0:T(8,128)(2,1)} %get-tuple-element.96.k_ref, bf16[512,2048]{1,0:T(8,128)(2,1)} %get-tuple-element.129.kt_ref, ...), custom_call_target="tpu_custom_call" | custom-call | flops 10737418240 | bytes 20971520 | tf_op jit(solution)/shard_map/attend_back/pallas_call | solution.py:470
  964.4 14.4 %unturn.1 = (f32[2048,1024]{1,0:T(8,128)}, f32[2048,2]{1,0:T(8,128)S(1)}, f32[2,512]{1,0:T(2,128)S(1)}) custom-call(f32[512,2048]{1,0:T(8,128)} %get-tuple-element.133.dqt_ref, f32[2048,512]{1,0:T(8,128)} %get-tuple-element.134.dk_ref, f32[2048,1536]{1,0:T(8,128)} %copy-done.12, f32[2048,2]{1,0:T(8,128)S(1)} %copy-done.1, f32[2,512]{1,0:T(2,128)S(1)} %copy-done.6, ...), custom_call_target="tpu_custom_call" | custom-call | flops 20971520 | bytes 25165824 | tf_op jit(solution)/shard_map/unturn/pallas_call | solution.py:593
  978.9 8.3 collective-permute-start.25
  989.9 3.0 copy.131
  993.0 3.0 copy.124
  996.0 3.0 copy.122
  1000.0 3.4 collective-permute-done.26
  1018.8 4.8 collective-permute-start.19
  1025.6 5.6 add_convert_fusion
  1035.1 3.0 copy.113
  1038.1 29.3 %collective-permute-done.17 = bf16[256,2048]{1,0:T(8,128)(2,1)} collective-permute-done((bf16[256,2048]{1,0:T(8,128)(2,1)S(1)}, bf16[256,2048]{1,0:T(8,128)(2,1)}, u32[]{:S(2)}, u32[]{:S(2)}) %collective-permute-start.17) | collective-permute-done | bytes 1048608 | tf_op jit(solution)/shard_map/ppermute | solution.py:1593
  1067.8 3.2 pad_maximum_fusion.4.far_one
  1074.3 8.6 multiply_subtract_fusion.2
  1084.5 7.5 subtract_convert_fusion.1
  1093.4 16.4 %convolution_convert_fusion.5.grad_ref = bf16[2048,1536]{1,0:T(8,128)(2,1)} fusion(bf16[2048,2048]{1,0:T(8,128)(2,1)S(1)} %bitcast.132, bf16[2048,512]{1,0:T(8,128)(2,1)S(1)} %copy-done.11, bf16[2048,512]{1,0:T(8,128)(2,1)S(1)} %get-tuple-element.255, bf16[2048,512]{1,0:T(8,128)(2,1)S(1)} %get-tuple-element.254), kind=kOutput, calls=%fused_computation.6 | convolution fusion | flops 12906921984 | bytes 20971520 | tf_op jit(solution)/shard_map/dot_general | solution.py:1417
  1109.8 18.7 %convolution_convert_fusion.2 = bf16[2048,2048]{1,0:T(8,128)(2,1)} fusion(bf16[2048,1536]{1,0:T(8,128)(2,1)} %get-tuple-element.92, bf16[2048,512]{1,0:T(8,128)(2,1)S(1)} %copy-done.11, bf16[2048,512]{1,0:T(8,128)(2,1)} %copy-done.32, bf16[2048,512]{1,0:T(8,128)(2,1)S(1)} %get-tuple-element.254), kind=kOutput, calls=%fused_computation.3 | convolution fusion | flops 12907970560 | bytes 20971520 | tf_op jit(solution)/shard_map/dot_general | solution.py:1417
  1128.6 4.9 fusion.4.dx_ref
  1133.4 195.3 %last_sums.1 = (f32[4096,256]{1,0:T(8,128)}, f32[256,1536]{1,0:T(8,128)}, f32[256,2048]{1,0:T(8,128)}, f32[512,1024]{1,0:T(8,128)}) custom-call(bf16[2048,2048]{1,0:T(8,128)(2,1)} %fusion.4.dx_ref, bf16[2048,1536]{1,0:T(8,128)(2,1)} %convolution_convert_fusion.5.grad_ref, bf16[2,256,2048]{2,1,0:T(8,128)(2,1)} %pad_maximum_fusion.4.far_one, ...), custom_call_target="tpu_custom_call" | custom-call | bytes 33554432 | tf_op jit(solution)/shard_map/last_sums/pallas_call | solution.py:1340
  1328.8 3.2 copy.123
  1332.0 4.8 multiply_subtract_fusion.3
  1336.8 3.1 copy.127
  1343.1 7.7 multiply_subtract_fusion
  1350.9 5.7 multiply_subtract_fusion.1
  1359.2 4.5 copy.149
  (282 shorter events, 120.8 us)
Async XLA Ops:
  7.2 146.9 %all-gather.8.cloned.1.call-start = ((), (), s32[]{:S(2)}) async-start(), calls=%async_computation.16 | async-start | bytes 1310720 | tf_op jit(solution)/shard_map/all_gather | solution.py:1472
  9.1 230.5 %all-gather.10.cloned.1.call-start = ((), (), s32[]{:S(2)}) async-start(), calls=%async_computation.17 | async-start | bytes 5242880 | tf_op jit(solution)/shard_map/all_gather | solution.py:1473
  154.1 236.8 %all-gather.6.cloned.1.call-start = ((), (), s32[]{:S(2)}) async-start(), calls=%async_computation.10 | async-start | bytes 12582912 | tf_op jit(solution)/shard_map/all_gather | solution.py:1494
  179.5 26.1 %copy-start.12 = (f32[2048,1536]{1,0:T(8,128)}, f32[2048,1536]{1,0:T(8,128)S(1)}, u32[]{:S(2)}) copy-start(f32[2048,1536]{1,0:T(8,128)S(1)} %fusion.39.qkv_ref) | copy-start | bytes 37748740
  180.2 25.3 %collective-permute-start.1 = (f32[2,2048]{1,0:T(2,128)S(1)}, f32[2,2048]{1,0:T(2,128)S(1)}, u32[]{:S(2)}, u32[]{:S(2)}) collective-permute-start(f32[2,2048]{1,0:T(2,128)S(1)} %pad_maximum_fusion.13), channel_id=1, source_target_pairs={{0,4},{4,0},{1,5},{5,1},{2,6},{6,2},{3,7},{7,3},{8,12},{12,8},{9,1... | collective-permute-start | bytes 49160 | tf_op jit(solution)/shard_map/ppermute | solution.py:42
  180.2 45.1 %collective-permute-start.3 = (bf16[256,1024]{1,0:T(8,128)(2,1)}, bf16[256,1024]{1,0:T(8,128)(2,1)}, u32[]{:S(2)}, u32[]{:S(2)}) collective-permute-start(bf16[256,1024]{1,0:T(8,128)(2,1)} %get-tuple-element.93), channel_id=1, source_target_pairs={{0,2},{2,0},{1,3},{3,1},{4,6},{6,4},{5,7},{7,5},{8,10},{10,8},{9,1... | collective-permute-start | bytes 1572872 | tf_op jit(solution)/shard_map/ppermute | solution.py:33
  205.5 8.1 collective-permute-start.2
  206.2 19.1 %copy-start.2 = (f32[2048,128]{1,0:T(8,128)}, f32[2048,128]{1,0:T(8,128)S(1)}, u32[]{:S(2)}) copy-start(f32[2048,128]{1,0:T(8,128)S(1)} %get-tuple-element.284.cos_ref) | copy-start | bytes 3145732
  206.4 18.9 %copy-start.5 = (f32[2,512]{1,0:T(2,128)}, f32[2,512]{1,0:T(2,128)S(1)}, u32[]{:S(2)}) copy-start(f32[2,512]{1,0:T(2,128)S(1)} %reshape_squeeze.3.gains_ref) | copy-start | bytes 12292
  240.6 36.8 %collective-permute-start = (bf16[256,1024]{1,0:T(8,128)(2,1)S(1)}, bf16[256,1024]{1,0:T(8,128)(2,1)}, u32[]{:S(2)}, u32[]{:S(2)}) collective-permute-start(bf16[256,1024]{1,0:T(8,128)(2,1)S(1)} %copy-done.43), channel_id=1, source_target_pairs={{0,2},{2,0},{1,3},{3,1},{4,6},{6,4},{5,7},{7,5},{8,10},{10,8},{9,1... | collective-permute-start | bytes 1572872 | tf_op jit(solution)/shard_map/ppermute | solution.py:33
  241.7 63.9 %collective-permute-start.4 = (bf16[256,1024]{1,0:T(8,128)(2,1)}, bf16[256,1024]{1,0:T(8,128)(2,1)}, u32[]{:S(2)}, u32[]{:S(2)}) collective-permute-start(bf16[256,1024]{1,0:T(8,128)(2,1)} %get-tuple-element.270), channel_id=1, source_target_pairs={{0,2},{2,0},{1,3},{3,1},{4,6},{6,4},{5,7},{7,5},{8,10},{10,8},{9,1... | collective-permute-start | bytes 1572872 | tf_op jit(solution)/shard_map/ppermute | solution.py:33
  277.5 28.2 %collective-permute-start.5 = (bf16[256,1024]{1,0:T(8,128)(2,1)}, bf16[256,1024]{1,0:T(8,128)(2,1)}, u32[]{:S(2)}, u32[]{:S(2)}) collective-permute-start(bf16[256,1024]{1,0:T(8,128)(2,1)} %collective-permute-done.3.refs_2_), channel_id=1, source_target_pairs={{0,8},{8,0},{16,24},{24,16},{1,9},{9,1},{17,25},{25,17},{2,10},{10... | collective-permute-start | bytes 1572872 | tf_op jit(solution)/shard_map/ppermute | solution.py:42
  279.0 26.6 %collective-permute-start.6 = (bf16[256,1024]{1,0:T(8,128)(2,1)}, bf16[256,1024]{1,0:T(8,128)(2,1)}, u32[]{:S(2)}, u32[]{:S(2)}) collective-permute-start(bf16[256,1024]{1,0:T(8,128)(2,1)} %collective-permute-done.refs_3_), channel_id=1, source_target_pairs={{0,16},{8,24},{16,0},{24,8},{1,17},{9,25},{17,1},{25,9},{2,18},{10... | collective-permute-start | bytes 1572872 | tf_op jit(solution)/shard_map/ppermute | solution.py:42
  308.4 64.4 %all-to-all-start = ((bf16[4,512,512]{1,2,0:T(8,128)(2,1)}), bf16[4,512,512]{1,2,0:T(8,128)(2,1)S(1)}, u32[]{:S(2)}, u32[]{:S(2)}) async-start(bf16[4,512,512]{1,2,0:T(8,128)(2,1)} %copy.111), calls=%async_computation | async-start | bytes 4194304 | tf_op jit(solution)/shard_map/all_to_all | solution.py:1500
  314.3 58.6 %collective-permute-start.8 = (bf16[512,1024]{1,0:T(8,128)(2,1)}, bf16[512,1024]{1,0:T(8,128)(2,1)}, u32[]{:S(2)}, u32[]{:S(2)}) collective-permute-start(bf16[512,1024]{1,0:T(8,128)(2,1)} %pad_maximum_fusion.8), channel_id=1, source_target_pairs={{0,16},{8,24},{16,0},{24,8},{1,17},{9,25},{17,1},{25,9},{2,18},{10... | collective-permute-start | bytes 3145736 | tf_op jit(solution)/shard_map/ppermute | solution.py:42
  317.1 55.8 %collective-permute-start.9 = (bf16[512,1024]{1,0:T(8,128)(2,1)}, bf16[512,1024]{1,0:T(8,128)(2,1)}, u32[]{:S(2)}, u32[]{:S(2)}) collective-permute-start(bf16[512,1024]{1,0:T(8,128)(2,1)} %pad_maximum_fusion.9), channel_id=1, source_target_pairs={{0,8},{8,0},{16,24},{24,16},{1,9},{9,1},{17,25},{25,17},{2,10},{10... | collective-permute-start | bytes 3145736 | tf_op jit(solution)/shard_map/ppermute | solution.py:42
  323.1 49.7 %collective-permute-start.7 = (bf16[256,1024]{1,0:T(8,128)(2,1)}, bf16[256,1024]{1,0:T(8,128)(2,1)}, u32[]{:S(2)}, u32[]{:S(2)}) collective-permute-start(bf16[256,1024]{1,0:T(8,128)(2,1)} %get-tuple-element.269), channel_id=1, source_target_pairs={{0,2},{2,0},{1,3},{3,1},{4,6},{6,4},{5,7},{7,5},{8,10},{10,8},{9,1... | collective-permute-start | bytes 1572872 | tf_op jit(solution)/shard_map/ppermute | solution.py:33
  323.1 49.8 %collective-permute-start.10 = (bf16[256,1024]{1,0:T(8,128)(2,1)}, bf16[256,1024]{1,0:T(8,128)(2,1)}, u32[]{:S(2)}, u32[]{:S(2)}) collective-permute-start(bf16[256,1024]{1,0:T(8,128)(2,1)} %collective-permute-done.4.refs_9_), channel_id=1, source_target_pairs={{0,8},{8,0},{16,24},{24,16},{1,9},{9,1},{17,25},{25,17},{2,10},{10... | collective-permute-start | bytes 1572872 | tf_op jit(solution)/shard_map/ppermute | solution.py:42
  327.3 81.7 %collective-permute-start.14 = (bf16[512,1024]{1,0:T(8,128)(2,1)}, bf16[512,1024]{1,0:T(8,128)(2,1)}, u32[]{:S(2)}, u32[]{:S(2)}) collective-permute-start(bf16[512,1024]{1,0:T(8,128)(2,1)} %dynamic-slice_convert_fusion), channel_id=1, source_target_pairs={{0,2},{2,0},{1,3},{3,1},{4,6},{6,4},{5,7},{7,5},{8,10},{10,8},{9,1... | collective-permute-start | bytes 3145736 | tf_op jit(solution)/shard_map/ppermute | solution.py:33
  328.8 12.4 slice-start.2
  372.9 18.0 %copy-start.34 = (bf16[4,512,512]{1,2,0:T(8,128)(2,1)}, bf16[4,512,512]{1,2,0:T(8,128)(2,1)S(1)}, u32[]{:S(2)}) copy-start(bf16[4,512,512]{1,2,0:T(8,128)(2,1)S(1)} %all-to-all-done) | copy-start | bytes 6291460
  372.9 15.1 %collective-permute-start.12 = (bf16[256,1024]{1,0:T(8,128)(2,1)}, bf16[256,1024]{1,0:T(8,128)(2,1)S(1)}, u32[]{:S(2)}, u32[]{:S(2)}) collective-permute-start(bf16[256,1024]{1,0:T(8,128)(2,1)} %collective-permute-done.7.refs_10_), channel_id=1, source_target_pairs={{0,16},{8,24},{16,0},{24,8},{1,17},{9,25},{17,1},{25,9},{2,18},{10... | collective-permute-start | bytes 1572872 | tf_op jit(solution)/shard_map/ppermute | solution.py:42
  375.9 33.1 %collective-permute-start.11 = (bf16[512,1024]{1,0:T(8,128)(2,1)}, bf16[512,1024]{1,0:T(8,128)(2,1)}, u32[]{:S(2)}, u32[]{:S(2)}) collective-permute-start(bf16[512,1024]{1,0:T(8,128)(2,1)} %pad_maximum_fusion.10), channel_id=1, source_target_pairs={{0,16},{8,24},{16,0},{24,8},{1,17},{9,25},{17,1},{25,9},{2,18},{10... | collective-permute-start | bytes 3145736 | tf_op jit(solution)/shard_map/ppermute | solution.py:42
  390.9 20.8 %collective-permute-start.13 = (bf16[512,1024]{1,0:T(8,128)(2,1)}, bf16[512,1024]{1,0:T(8,128)(2,1)}, u32[]{:S(2)}, u32[]{:S(2)}) collective-permute-start(bf16[512,1024]{1,0:T(8,128)(2,1)} %pad_maximum_fusion.11), channel_id=1, source_target_pairs={{0,8},{8,0},{16,24},{24,16},{1,9},{9,1},{17,25},{25,17},{2,10},{10... | collective-permute-start | bytes 3145736 | tf_op jit(solution)/shard_map/ppermute | solution.py:42
  400.4 185.2 %all-to-all-start.2 = ((bf16[8,512,256]{2,1,0:T(8,128)(2,1)}), bf16[8,512,256]{2,1,0:T(8,128)(2,1)S(1)}, u32[]{:S(2)}, u32[]{:S(2)}) async-start(bf16[8,512,256]{2,1,0:T(8,128)(2,1)} %bitcast.138), calls=%async_computation.2 | async-start | bytes 4194304 | tf_op jit(solution)/shard_map/all_to_all | solution.py:1517
  404.0 610.2 %reduce-scatter.11.cloned.1.call-start = ((), (), s32[]{:S(2)}) async-start(), calls=%async_computation.12 | async-start | bytes 5242880 | tf_op jit(solution)/shard_map/reduce_scatter | solution.py:1583
  737.9 11.7 slice-start.4
  740.0 9.6 copy-start.38
  740.0 9.6 slice-start.5
  774.3 239.9 %reduce-scatter.9.cloned.1.call-start = ((), (), s32[]{:S(2)}) async-start(), calls=%async_computation.11 | async-start | bytes 5242880 | tf_op jit(solution)/shard_map/reduce_scatter | solution.py:1583
  774.9 292.9 %reduce-scatter.15.cloned.1.call-start = ((), (), s32[]{:S(2)}) async-start(), calls=%async_computation.14 | async-start | bytes 5242880 | tf_op jit(solution)/shard_map/reduce_scatter | solution.py:1583
  802.5 124.9 %all-to-all-start.3 = ((bf16[4,512,512]{2,1,0:T(8,128)(2,1)}), bf16[4,512,512]{2,1,0:T(8,128)(2,1)}, u32[]{:S(2)}, u32[]{:S(2)}) async-start(bf16[4,512,512]{2,1,0:T(8,128)(2,1)} %bitcast.116), calls=%async_computation.3 | async-start | bytes 4194304 | tf_op jit(solution)/shard_map/all_to_all | solution.py:1505
  806.9 260.9 %reduce-scatter.13.cloned.1.call-start = ((), (), s32[]{:S(2)}) async-start(), calls=%async_computation.13 | async-start | bytes 5242880 | tf_op jit(solution)/shard_map/reduce_scatter | solution.py:1583
  838.8 78.4 %collective-permute-start.15 = (bf16[2,1,512,1024]{3,2,1,0:T(8,128)(2,1)}, bf16[2,1,512,1024]{3,2,1,0:T(8,128)(2,1)}, u32[]{:S(2)}, u32[]{:S(2)}) collective-permute-start(bf16[2,1,512,1024]{3,2,1,0:T(8,128)(2,1)} %constant_dynamic-slice_fusion.8), channel_id=1, source_target_pairs={{0,8},{8,0},{16,24},{24,16},{1,9},{9,1},{17,25},{25,17},{2,10},{10... | collective-permute-start | bytes 6291464 | tf_op jit(solution)/shard_map/ppermute | solution.py:42
  844.1 75.7 %collective-permute-start.16 = (bf16[1,2,512,1024]{3,2,1,0:T(8,128)(2,1)}, bf16[1,2,512,1024]{3,2,1,0:T(8,128)(2,1)}, u32[]{:S(2)}, u32[]{:S(2)}) collective-permute-start(bf16[1,2,512,1024]{3,2,1,0:T(8,128)(2,1)} %constant_dynamic-slice_fusion.7), channel_id=1, source_target_pairs={{0,16},{8,24},{16,0},{24,8},{1,17},{9,25},{17,1},{25,9},{2,18},{10... | collective-permute-start | bytes 6291464 | tf_op jit(solution)/shard_map/ppermute | solution.py:42
  851.8 65.4 %copy-start.20 = (bf16[2,2,512,1024]{3,2,1,0:T(8,128)(2,1)S(1)}, bf16[2,2,512,1024]{3,2,1,0:T(8,128)(2,1)}, u32[]{:S(2)}) copy-start(bf16[2,2,512,1024]{3,2,1,0:T(8,128)(2,1)} %copy-done.19) | copy-start | bytes 12582916
  857.5 62.3 %copy-start.18 = (bf16[2,2,512,1024]{3,2,1,0:T(8,128)(2,1)S(1)}, bf16[2,2,512,1024]{3,2,1,0:T(8,128)(2,1)}, u32[]{:S(2)}) copy-start(bf16[2,2,512,1024]{3,2,1,0:T(8,128)(2,1)} %get-tuple-element.260) | copy-start | bytes 12582916
  857.5 168.1 %collective-permute-start.24 = (bf16[2048,1024]{1,0:T(8,128)(2,1)}, bf16[2048,1024]{1,0:T(8,128)(2,1)}, u32[]{:S(2)}, u32[]{:S(2)}) collective-permute-start(bf16[2048,1024]{1,0:T(8,128)(2,1)} %constant_dynamic-slice_fusion.2), channel_id=1, source_target_pairs={{0,4},{4,0},{1,5},{5,1},{2,6},{6,2},{3,7},{7,3},{8,12},{12,8},{9,1... | collective-permute-start | bytes 12582920 | tf_op jit(solution)/shard_map/ppermute | solution.py:33
  924.2 79.3 %collective-permute-start.23 = (bf16[1,1,512,1024]{3,2,1,0:T(8,128)(2,1)}, bf16[1,1,512,1024]{3,2,1,0:T(8,128)(2,1)}, u32[]{:S(2)}, u32[]{:S(2)}) collective-permute-start(bf16[1,1,512,1024]{3,2,1,0:T(8,128)(2,1)} %constant_dynamic-slice_fusion.4), channel_id=1, source_target_pairs={{0,8},{8,0},{16,24},{24,16},{1,9},{9,1},{17,25},{25,17},{2,10},{10... | collective-permute-start | bytes 3145736 | tf_op jit(solution)/shard_map/ppermute | solution.py:42
  925.6 81.3 %collective-permute-start.22 = (bf16[1,1,512,1024]{3,2,1,0:T(8,128)(2,1)}, bf16[1,1,512,1024]{3,2,1,0:T(8,128)(2,1)}, u32[]{:S(2)}, u32[]{:S(2)}) collective-permute-start(bf16[1,1,512,1024]{3,2,1,0:T(8,128)(2,1)} %constant_dynamic-slice_fusion.5), channel_id=1, source_target_pairs={{0,16},{8,24},{16,0},{24,8},{1,17},{9,25},{17,1},{25,9},{2,18},{10... | collective-permute-start | bytes 3145736 | tf_op jit(solution)/shard_map/ppermute | solution.py:42
  927.3 107.7 %all-to-all-start.1 = ((bf16[8,512,256]{2,1,0:T(8,128)(2,1)}), bf16[8,512,256]{2,1,0:T(8,128)(2,1)}, u32[]{:S(2)}, u32[]{:S(2)}) async-start(bf16[8,512,256]{2,1,0:T(8,128)(2,1)} %bitcast.118), calls=%async_computation.1 | async-start | bytes 4194304 | tf_op jit(solution)/shard_map/all_to_all | solution.py:1538
  931.9 196.6 %reduce-scatter.19.cloned.1.call-start = ((), (), s32[]{:S(2)}) async-start(), calls=%async_computation.18 | async-start | bytes 5242880
  933.6 30.8 %copy-start.1 = (f32[2048,2]{1,0:T(8,128)S(1)}, f32[2048,2]{1,0:T(8,128)}, u32[]{:S(2)}) copy-start(f32[2048,2]{1,0:T(8,128)} %copy-done) | copy-start | bytes 49156
  933.6 30.8 %copy-start.3 = (f32[2048,128]{1,0:T(8,128)S(1)}, f32[2048,128]{1,0:T(8,128)}, u32[]{:S(2)}) copy-start(f32[2048,128]{1,0:T(8,128)} %copy-done.2) | copy-start | bytes 3145732
  933.6 30.8 %copy-start.6 = (f32[2,512]{1,0:T(2,128)S(1)}, f32[2,512]{1,0:T(2,128)}, u32[]{:S(2)}) copy-start(f32[2,512]{1,0:T(2,128)} %copy-done.5) | copy-start | bytes 12292
  964.4 14.5 %copy-start.10 = (bf16[2048,512]{1,0:T(8,128)(2,1)}, bf16[2048,512]{1,0:T(8,128)(2,1)S(1)}, u32[]{:S(2)}) copy-start(bf16[2048,512]{1,0:T(8,128)(2,1)S(1)} %get-tuple-element.140) | copy-start | bytes 6291460
  964.4 14.5 %copy-start.45 = (f32[2048]{0:T(1024)S(1)}, f32[2048]{0:T(1024)}, u32[]{:S(2)}) copy-start(f32[2048]{0:T(1024)} %get-tuple-element.226) | copy-start | bytes 24580
  978.9 20.1 %collective-permute-start.25 = (f32[4,2048]{1,0:T(4,128)S(1)}, f32[4,2048]{1,0:T(4,128)S(1)}, u32[]{:S(2)}, u32[]{:S(2)}) collective-permute-start(f32[4,2048]{1,0:T(4,128)S(1)} %pad_maximum_fusion.12), channel_id=1, source_target_pairs={{0,8},{8,0},{16,24},{24,16},{1,9},{9,1},{17,25},{25,17},{2,10},{10... | collective-permute-start | bytes 98312 | tf_op jit(solution)/shard_map/ppermute | solution.py:42
  999.0 4.4 collective-permute-start.26
  1003.5 1.7 collective-permute-start.27
  1005.2 4.9 collective-permute-start.28
  1010.1 4.0 collective-permute-start.29
  1014.2 10.8 copy-start.47
  1014.2 10.8 copy-start.50
  1014.2 10.8 copy-start.51
  1017.1 14.0 %copy-start.31 = (bf16[256,2048]{1,0:T(8,128)(2,1)}, bf16[256,2048]{1,0:T(8,128)(2,1)S(1)}, u32[]{:S(2)}) copy-start(bf16[256,2048]{1,0:T(8,128)(2,1)S(1)} %get-tuple-element.146) | copy-start | bytes 3145732
  1017.1 50.2 %collective-permute-start.18 = (bf16[256,2048]{1,0:T(8,128)(2,1)}, bf16[256,2048]{1,0:T(8,128)(2,1)}, u32[]{:S(2)}, u32[]{:S(2)}) collective-permute-start(bf16[256,2048]{1,0:T(8,128)(2,1)} %get-tuple-element.267), channel_id=1, source_target_pairs={{2,4},{4,2},{3,5},{5,3},{10,12},{12,10},{11,13},{13,11},{18,20},{2... | collective-permute-start | bytes 3145736 | tf_op jit(solution)/shard_map/ppermute | solution.py:1594
  1018.8 48.6 %collective-permute-start.19 = (bf16[256,2048]{1,0:T(8,128)(2,1)}, bf16[256,2048]{1,0:T(8,128)(2,1)}, u32[]{:S(2)}, u32[]{:S(2)}) collective-permute-start(bf16[256,2048]{1,0:T(8,128)(2,1)} %get-tuple-element.267), channel_id=1, source_target_pairs={{0,4},{6,2},{1,5},{7,3},{8,12},{14,10},{9,13},{15,11},{16,20},{22,... | collective-permute-start | bytes 3145736 | tf_op jit(solution)/shard_map/ppermute | solution.py:1595
  1023.6 43.8 %collective-permute-start.17 = (bf16[256,2048]{1,0:T(8,128)(2,1)S(1)}, bf16[256,2048]{1,0:T(8,128)(2,1)}, u32[]{:S(2)}, u32[]{:S(2)}) collective-permute-start(bf16[256,2048]{1,0:T(8,128)(2,1)S(1)} %get-tuple-element.146), channel_id=1, source_target_pairs={{2,0},{4,6},{3,1},{5,7},{10,8},{12,14},{11,9},{13,15},{18,16},{20,... | collective-permute-start | bytes 3145736 | tf_op jit(solution)/shard_map/ppermute | solution.py:1593
  1033.7 322.9 %reduce-scatter.17.cloned.1.call-start = ((), (), s32[]{:S(2)}) async-start(), calls=%async_computation.15 | async-start | bytes 1310720 | tf_op jit(solution)/shard_map/reduce_scatter | solution.py:1630
  1067.7 3.3 collective-permute-start.20
  1074.1 8.8 collective-permute-start.21
  1083.3 10.1 slice-start
  1084.5 8.9 copy-start.11
  (40 other events, 141.9 us)
Sparse Core Ops, SparseCore 0:
  10.2 55.7 all-gather.7
  154.2 70.6 all-gather.9
  239.7 19.6 all-gather.5
  774.4 52.3 reduce-scatter.10
  829.9 83.7 reduce-scatter.8
  916.5 73.1 reduce-scatter.14
  992.9 53.1 reduce-scatter.12
  1049.6 52.6 reduce-scatter.18
  1128.7 42.5 reduce-scatter.16

commit v3 on v2

--- a/solution.py
+++ b/solution.py
@@ -65,9 +65,9 @@
 
 
 def gather_kernel(
-    chunks, tok_ref, low_ref, post_ref, x_ref, w_ref, all_ref, ex_ref,
+    chunks, tok_ref, low_ref, post_ref, next_ref, x_ref, w_ref, all_ref, ex_ref, got_ref,
     own_sem, zh_send, zh_recv, t_send, t_recv, r_send, r_recv,
-    wz_send, wz_recv, wd_send, wd_recv, wr_send, wr_recv, wl_sem, p_send, p_recv,
+    wz_send, wz_recv, wd_send, wd_recv, wr_send, wr_recv, wl_sem, p_send, p_recv, n_send, n_recv,
 ):
     n_dp = lax.axis_size("dp")
     tp = lax.axis_size("zl")
@@ -208,6 +208,8 @@
             late.start()
     for late in zh_copies[lead:][n_dp - 1 :]:
         late.start()
+    following = remote(next_ref, got_ref, n_send, n_recv, zh_dev)
+    following.start()
     near_remote = remote(ex_ref, w_ref.at[spot], wd_send.at[0], wd_recv.at[0, r], row_dev)
     near_local = pltpu.make_async_copy(ex_ref, w_ref.at[spot], wl_sem.at[2])
 
@@ -239,6 +241,7 @@
         cp.wait_send()
     for cp in zh_copies:
         cp.wait_send()
+    following.wait()
     p_loc.wait()
     for cp in posts:
         cp.wait_send()
@@ -279,7 +282,7 @@
                 remote(ex_ref, w_ref.at[at], wd_send.at[dd], wd_recv.at[dd, src_r], row_dev).wait_recv()
 
 
-def first_gather(tokens, low, post):
+def first_gather(tokens, low, post, following):
     n_dp = lax.axis_size("dp")
     tp = lax.axis_size("zl")
     rows_dev, feat = tokens.shape
@@ -289,15 +292,16 @@
     anywhere = pl.BlockSpec(memory_space=pl.ANY)
     dma = pltpu.SemaphoreType.DMA
     x_shape = (4 * tp, seq_len, feat)
-    x_full, w_full, post_all, _ = pl.pallas_call(
+    x_full, w_full, post_all, _, got = pl.pallas_call(
         functools.partial(gather_kernel, chunks),
-        in_specs=[anywhere] * 3,
-        out_specs=[anywhere] * 4,
+        in_specs=[anywhere] * 4,
+        out_specs=[anywhere] * 5,
         out_shape=[
             jax.ShapeDtypeStruct(x_shape, bf16),
             jax.ShapeDtypeStruct((2 * low.shape[0], low.shape[1]), bf16),
             jax.ShapeDtypeStruct((4 * tp, *post.shape), f32),
             jax.ShapeDtypeStruct((low.shape[0] // n_dp, low.shape[1]), bf16),
+            jax.ShapeDtypeStruct(following.shape, bf16),
         ],
         scratch_shapes=[
             dma((chunks,)),
@@ -316,13 +320,15 @@
             dma((3,)),
             dma((4 * tp,)),
             dma((4 * tp,)),
+            dma(()),
+            dma(()),
         ],
         compiler_params=pltpu.CompilerParams(collective_id=0, has_side_effects=True),
         cost_estimate=pl.CostEstimate(flops=0, bytes_accessed=6 * seq_len * width, transcendentals=0),
         name="first_gather",
-    )(tokens, low, post)
+    )(tokens, low, post, following)
     x_full = x_full.transpose(1, 0, 2).reshape(seq_len, width)
-    return x_full, w_full, post_all
+    return x_full, w_full, post_all, got
 
 
 def doc_start(ends_ref, docs, places):
@@ -1042,21 +1048,19 @@
 
 def gate_up_body(tile, w, need, ti, outs, y, mid):
     hidden_width = w[0].shape[1]
-    nb = min(256, hidden_width)
-    mb = min(128, tile.shape[0])
+    nb = min(512, hidden_width)
     count = hidden_width // nb
     need(0)
     need(1)
 
     def step(n):
         cols = columns(n, nb)
-        for m in range(tile.shape[0] // mb):
-            at = slice(m * mb, (m + 1) * mb)
-            gate = jnp.dot(tile[at, :], w[0][:, cols], preferred_element_type=f32)
-            up = jnp.dot(tile[at, :], w[1][:, cols], preferred_element_type=f32)
-            outs[0][at, cols] = gate.astype(bf16)
-            outs[1][at, cols] = up.astype(bf16)
-            outs[2][at, cols] = (gate * jax.nn.sigmoid(gate) * up).astype(bf16)
+        rows = tile[...]
+        gate = jnp.dot(rows, w[0][:, cols], preferred_element_type=f32)
+        up = jnp.dot(rows, w[1][:, cols], preferred_element_type=f32)
+        outs[0][:, cols] = gate.astype(bf16)
+        outs[1][:, cols] = up.astype(bf16)
+        outs[2][:, cols] = (gate * jax.nn.sigmoid(gate) * up).astype(bf16)
 
     loop(0, count // 2, step)
     mid()
@@ -1114,10 +1118,11 @@
 
 
 def last_kernel(
-    chunks, dx_ref, grad_ref, far_one, far_two, out_ref, sum_ref, far_out_one, far_out_two,
+    chunks, dx_ref, down_ref, qkv_ref, up_ref, out_ref, down_out, qkv_out, up_out,
     own, from_row, near, from_t, give, from_zh,
-    g_own, g_in, g_sum, g_late, stay_one, stay_two, late_one, late_two, far_local, far_send, far_recv,
-    own_sem, row_send, row_recv, t_send, t_recv, zh_send, zh_recv, g_sem, d_send, d_recv, f_send, f_recv,
+    down_own, down_in, down_sum, down_late, qkv_own, qkv_in, qkv_sum, qkv_late, up_stay, up_late,
+    own_sem, row_send, row_recv, t_send, t_recv, zh_send, zh_recv,
+    g_sem, d_send, d_recv, f_local, f_send, f_recv,
 ):
     n_dp = lax.axis_size("dp")
     tp = lax.axis_size("zl")
@@ -1128,7 +1133,6 @@
     half = width // 2
     feat = half // (2 * tp)
     step = seq_len // chunks
-    part = g_own.shape[1]
 
     def remote(src, dst, send, recv, dev):
         return pltpu.make_async_remote_copy(
@@ -1153,47 +1157,66 @@
         pl.semaphore_signal(barrier, inc=1, device_id=dev, device_id_type=pl.DeviceIdType.MESH)
     pl.semaphore_wait(barrier, len(partners))
 
-    fars = [(far_one, far_out_one, stay_one, late_one), (far_two, far_out_two, stay_two, late_two)]
-
-    def far_copies(i):
-        pieces, _, stay, late = fars[i]
+    def owner_copies(i, pieces, late):
         return (
-            pltpu.make_async_copy(pieces.at[r], stay, far_local.at[i]),
-            remote(pieces.at[1 - r], late.at[0], far_send.at[i, 0], far_recv.at[i, 0], row_dev),
-            remote(pieces.at[r], late.at[0], far_send.at[i, 1], far_recv.at[i, 1], zh_dev),
-            remote(pieces.at[1 - r], late.at[1], far_send.at[i, 2], far_recv.at[i, 2], cross_dev),
+            remote(pieces.at[1 - r], late.at[0], f_send.at[i, 0], f_recv.at[i, 0], row_dev),
+            remote(pieces.at[r], late.at[0], f_send.at[i, 1], f_recv.at[i, 1], zh_dev),
+            remote(pieces.at[1 - r], late.at[1], f_send.at[i, 2], f_recv.at[i, 2], cross_dev),
         )
 
-    def far_start(i):
+    def owner_start(i, pieces, late):
         @pl.when(same)
         def _():
-            far_copies(i)[0].start()
-            far_copies(i)[1].start()
+            owner_copies(i, pieces, late)[0].start()
 
         @pl.when(other_core)
         def _():
-            far_copies(i)[2].start()
-            far_copies(i)[3].start()
-
-    def far_end(i):
-        pieces, total, stay, late = fars[i]
-
+            owner_copies(i, pieces, late)[1].start()
+            owner_copies(i, pieces, late)[2].start()
+
+    def owner_end(i, pieces, late, kept, total):
         @pl.when(same)
         def _():
-            far_copies(i)[0].wait()
-            far_copies(i)[2].wait_recv()
-            total[...] = stay[...].astype(f32) + late[0].astype(f32)
-            far_copies(i)[1].wait_send()
+            owner_copies(i, pieces, late)[1].wait_recv()
+            total[...] = kept[...].astype(f32) + late[0].astype(f32)
+            owner_copies(i, pieces, late)[0].wait_send()
 
         @pl.when(other_core)
         def _():
-            far_copies(i)[1].wait_recv()
-            far_copies(i)[3].wait_recv()
+            owner_copies(i, pieces, late)[0].wait_recv()
+            owner_copies(i, pieces, late)[2].wait_recv()
             total[...] = late[0].astype(f32) + late[1].astype(f32)
-            far_copies(i)[2].wait_send()
-            far_copies(i)[3].wait_send()
-
-    far_start(0)
+            owner_copies(i, pieces, late)[1].wait_send()
+            owner_copies(i, pieces, late)[2].wait_send()
+
+    up_local = pltpu.make_async_copy(up_ref.at[r], up_stay, f_local)
+    up_local.start()
+    owner_start(2, up_ref, up_late)
+
+    def down_piece(which, group):
+        rows, cols = down_own.shape[1:]
+        return down_ref.at[
+            pl.ds(pl.multiple_of(group * rows, rows), rows), pl.ds(pl.multiple_of(which * cols, cols), cols)
+        ]
+
+    def qkv_piece(which, group):
+        rows = qkv_own.shape[1]
+        return qkv_ref.at[pl.ds(pl.multiple_of((which * n_dp + group) * rows, rows), rows)]
+
+    def group_copies(i, piece, mine, inbox):
+        loads = [pltpu.make_async_copy(piece(which, d), mine.at[which], g_sem.at[i, which]) for which in range(2)]
+        sends = [
+            remote(
+                piece(which, lax.rem(d + k, n_dp)), inbox.at[k - 1, which],
+                d_send.at[i, k, which], d_recv.at[i, k, which], dp_dev(k),
+            )
+            for which in range(2)
+            for k in range(1, n_dp)
+        ]
+        return loads, sends
+
+    down_copies = group_copies(0, down_piece, down_own, down_in)
+    qkv_copies = group_copies(1, qkv_piece, qkv_own, qkv_in)
 
     def cols_at(which):
         return pl.ds(pl.multiple_of(which * half, half), half)
@@ -1207,22 +1230,9 @@
         cp = pltpu.make_async_copy(dx_ref.at[rows, cols_at(r)], own.at[c], own_sem.at[c])
         cp.start()
         own_copies.append(cp)
-
-    def grad_rows(which, group):
-        return grad_ref.at[pl.ds(pl.multiple_of((which * n_dp + group) * part, part), part)]
-
-    g_copies, g_loads = [], []
-    for which in range(2):
-        cp = pltpu.make_async_copy(grad_rows(which, d), g_own.at[which], g_sem.at[which])
-        cp.start()
-        g_loads.append(cp)
-        for k in range(1, n_dp):
-            cp = remote(
-                grad_rows(which, lax.rem(d + k, n_dp)), g_in.at[k - 1, which],
-                d_send.at[k, which], d_recv.at[k, which], dp_dev(k),
-            )
+    for loads, sends in (down_copies, qkv_copies):
+        for cp in loads + sends:
             cp.start()
-            g_copies.append(cp)
 
     t_copies = {}
 
@@ -1260,71 +1270,46 @@
         zh_copies.append(cp)
         out_ref[pl.ds(pl.multiple_of(g * seq_len + c * step, step), step), :] = total_of(g)
 
-    def grad_stage():
-        for cp in g_loads:
+    def group_stage(copies, mine, inbox, total_ref):
+        for cp in copies[0]:
             cp.wait()
-        for cp in g_copies:
+        for cp in copies[1]:
             cp.wait_recv()
+        part = mine.shape[1]
         block = min(64, part)
         for which in range(2):
 
             def add(i, carry, which=which):
                 at = pl.ds(pl.multiple_of(i * block, block), block)
-                total = g_own[which, at, :].astype(f32)
+                total = mine[which, at, :].astype(f32)
                 for k in range(n_dp - 1):
-                    total = total + g_in[k, which, at, :].astype(f32)
-                g_sum[which, at, :] = total.astype(bf16)
+                    total = total + inbox[k, which, at, :].astype(f32)
+                total_ref[which, at, :] = total.astype(bf16)
                 return carry
 
             lax.fori_loop(0, part // block, add, 0)
 
-    to_row = remote(g_sum.at[1 - r], g_late.at[0], f_send.at[0], f_recv.at[0], row_dev)
-    to_zh = remote(g_sum.at[r], g_late.at[0], f_send.at[1], f_recv.at[1], zh_dev)
-    to_cross = remote(g_sum.at[1 - r], g_late.at[1], f_send.at[2], f_recv.at[2], cross_dev)
-
-    far_start(1)
     for c in range(chunks):
         row_stage(c)
-        if c >= 2:
-            t_stage(c - 2)
-    grad_stage()
-
-    @pl.when(same)
-    def _():
-        to_row.start()
-
-    @pl.when(other_core)
-    def _():
-        to_zh.start()
-        to_cross.start()
-
-    for c in range(max(0, chunks - 2), chunks):
-        t_stage(c)
+        if c >= 1:
+            t_stage(c - 1)
+    t_stage(chunks - 1)
+    group_stage(down_copies, down_own, down_in, down_sum)
+    owner_start(0, down_sum, down_late)
+    group_stage(qkv_copies, qkv_own, qkv_in, qkv_sum)
+    owner_start(1, qkv_sum, qkv_late)
     for c in range(chunks):
         zh_copies[c].wait_recv()
         out_ref[pl.ds(pl.multiple_of((1 - g) * seq_len + c * step, step), step), :] = from_zh[c].astype(f32)
-
-    @pl.when(same)
-    def _():
-        to_zh.wait_recv()
-        sum_ref[...] = g_sum[r].astype(f32) + g_late[0].astype(f32)
-        to_row.wait_send()
-
-    @pl.when(other_core)
-    def _():
-        to_row.wait_recv()
-        to_cross.wait_recv()
-        sum_ref[...] = g_late[0].astype(f32) + g_late[1].astype(f32)
-        to_zh.wait_send()
-        to_cross.wait_send()
-
-    far_end(0)
-    far_end(1)
-    for cp in rows_copies + g_copies + list(t_copies.values()) + zh_copies:
+    up_local.wait()
+    owner_end(2, up_ref, up_late, up_stay, up_out)
+    owner_end(0, down_sum, down_late, down_sum.at[r], down_out)
+    owner_end(1, qkv_sum, qkv_late, qkv_sum.at[r], qkv_out)
+    for cp in rows_copies + down_copies[1] + qkv_copies[1] + list(t_copies.values()) + zh_copies:
         cp.wait_send()
 
 
-def last_sums(dx, grad, fars):
+def last_sums(dx, down, qkv, up):
     n_dp = lax.axis_size("dp")
     tp = lax.axis_size("zl")
     seq_len, width = dx.shape
@@ -1332,19 +1317,28 @@
     half = width // 2
     feat = half // (2 * tp)
     step = seq_len // chunks
-    part = grad.shape[0] // (2 * n_dp)
-    cols = grad.shape[1]
     anywhere = pl.BlockSpec(memory_space=pl.ANY)
     vmem = pl.BlockSpec(memory_space=pltpu.VMEM)
     dma = pltpu.SemaphoreType.DMA
+    down_shape = (down.shape[0] // n_dp, down.shape[1] // 2)
+    qkv_shape = (qkv.shape[0] // (2 * n_dp), qkv.shape[1])
+    sums = []
+    for shape in (down_shape, qkv_shape):
+        sums += [
+            pltpu.VMEM((2, *shape), bf16),
+            pltpu.VMEM((n_dp - 1, 2, *shape), bf16),
+            pltpu.VMEM((2, *shape), bf16),
+            pltpu.VMEM((2, *shape), bf16),
+        ]
     return pl.pallas_call(
         functools.partial(last_kernel, chunks),
         in_specs=[anywhere] * 4,
         out_specs=[vmem] * 4,
         out_shape=[
             jax.ShapeDtypeStruct((2 * seq_len, feat), f32),
-            jax.ShapeDtypeStruct((part, cols), f32),
-            *[jax.ShapeDtypeStruct(v.shape[1:], f32) for v in fars],
+            jax.ShapeDtypeStruct(down_shape, f32),
+            jax.ShapeDtypeStruct(qkv_shape, f32),
+            jax.ShapeDtypeStruct(up.shape[1:], f32),
         ],
         scratch_shapes=[
             pltpu.VMEM((chunks, step, half), bf16),
@@ -1353,15 +1347,9 @@
             pltpu.VMEM((chunks, 2, tp - 1, step, feat), bf16),
             pltpu.VMEM((chunks, step, feat), bf16),
             pltpu.VMEM((chunks, step, feat), bf16),
-            pltpu.VMEM((2, part, cols), bf16),
-            pltpu.VMEM((n_dp - 1, 2, part, cols), bf16),
-            pltpu.VMEM((2, part, cols), bf16),
-            pltpu.VMEM((2, part, cols), bf16),
-            *[pltpu.VMEM(v.shape[1:], bf16) for v in fars],
-            *[pltpu.VMEM(v.shape, bf16) for v in fars],
-            dma((2,)),
-            dma((2, 3)),
-            dma((2, 3)),
+            *sums,
+            pltpu.VMEM(up.shape[1:], bf16),
+            pltpu.VMEM(up.shape, bf16),
             dma((chunks,)),
             dma((chunks,)),
             dma((chunks,)),
@@ -1369,16 +1357,17 @@
             dma((chunks, 2, tp)),
             dma((chunks,)),
             dma((chunks,)),
-            dma((2,)),
-            dma((n_dp, 2)),
-            dma((n_dp, 2)),
-            dma((3,)),
-            dma((3,)),
+            dma((2, 2)),
+            dma((2, n_dp, 2)),
+            dma((2, n_dp, 2)),
+            dma(()),
+            dma((3, 3)),
+            dma((3, 3)),
         ],
         compiler_params=pltpu.CompilerParams(collective_id=4, has_side_effects=True, vmem_limit_bytes=60 << 20),
         cost_estimate=pl.CostEstimate(flops=0, bytes_accessed=8 * seq_len * width, transcendentals=0),
         name="last_sums",
-    )(dx, grad, *fars)
+    )(dx, down, qkv, up)
 
 
 def rotary(seq_len):
@@ -1441,7 +1430,12 @@
     small = jnp.concatenate(small)
     pad = -small.shape[0] % 1024
     small = jnp.concatenate([small, jnp.zeros((pad,), f32)]).reshape(-1, 128)
-    x_full, qkv_full, small_all = first_gather(tokens, qkv_low, small)
+
+    def quarter_of(weight):
+        rows = weight.shape[0] // n_dp
+        return lax.dynamic_slice_in_dim(weight, d * rows, rows, 0).astype(bf16)
+
+    x_full, qkv_full, small_all, gate_quarter = first_gather(tokens, qkv_low, small, quarter_of(gate_weight))
     small_all = small_all.reshape(2 * n_col, -1)
     cut_one, cut_two = 2 * feat, 2 * feat + 2 * col_width
     post_all = small_all[:, :cut_one].reshape(2 * n_col, 2, feat).transpose(1, 0, 2).reshape(2, width)
@@ -1459,13 +1453,11 @@
         two_x = swap_bit(jnp.concatenate([two, two_y]), "dp", 1)
         return [one, two, one_x, one_y, two_y, two_x]
 
-    def quarter_of(weight):
-        rows = weight.shape[0] // n_dp
-        return lax.dynamic_slice_in_dim(weight, d * rows, rows, 0).astype(bf16)
-
-    gate_one, gate_two = halves(quarter_of(gate_weight))
-    gate_one, gate_two, post_all = tie(gate_one, gate_two, post_all)
-    gate_one = swap(gate_one, "zh")
+    gate_one, gate_two = halves(gate_quarter)
+    up_one, up_two = halves(quarter_of(up_weight))
+    up_one, up_two, post_all = tie(up_one, up_two, post_all)
+    up_one, up_two = swap(up_one, "zh"), swap(up_two, "zh")
+    gate_one_x, gate_two_y = swap_bit(gate_one, "dp", 1), swap_bit(gate_two, "dp", 2)
 
     out_rows = out_weight.shape[0] // n_dp
     out_part = lax.dynamic_slice_in_dim(out_weight, d * out_rows, out_rows, 0).astype(bf16)
@@ -1482,19 +1474,16 @@
         axis=0,
     )
     inv_scale = lax.rsqrt(small_sum(squares, ("row", "zl")) / width + norm_eps).T
-    gate_two = swap(gate_two, "zh")
-    up_one, up_two = halves(quarter_of(up_weight))
-    up_one, up_two = swap(up_one, "zh"), swap(up_two, "zh")
     down_quarter = swap(quarter_of(down_weight), "zh")
-    inv_scale, gate_one = tie(inv_scale, gate_one)
+    inv_scale, gate_one_x, gate_two_y = tie(inv_scale, gate_one_x, gate_two_y)
     query, key, key_t, value, value_t = prepare(qkv, inv_scale, gains, cos_two, sin_two)
-    ends, gate_two = tie(ends, gate_two)
-    gate_one_x, gate_two_y = swap_bit(gate_one, "dp", 1), swap_bit(gate_two, "dp", 2)
+    ends, up_one = tie(ends, up_one)
     out_part, key_t = tie(out_part, key_t)
     out_full = lax.all_gather(out_part.reshape(width, width // 2), "row", axis=1, tiled=True)
     att, log_total = attend(query, key, value_t, ends)
-    att, up_one, gate_one_x, gate_two_y = tie(att, up_one, gate_one_x, gate_two_y)
     gate_pieces = gathered(gate_one, gate_two, gate_one_x, gate_two_y)
+    att, up_two, gate_pieces[3], gate_pieces[5] = tie(att, up_two, gate_pieces[3], gate_pieces[5])
+    up_one_x, up_two_y = swap_bit(up_one, "dp", 1), swap_bit(up_two, "dp", 2)
 
     def to_tokens(vals):
         got = lax.all_to_all(vals.reshape(group, mine, col_width), ("row", "zl"), 0, 0)
@@ -1507,7 +1496,7 @@
     att_tok = to_tokens(att)
 
     gain_attn, gain_mlp = post_all[0:1], post_all[1:2]
-    att_tok, up_two, gate_pieces[3], gate_pieces[5] = tie(att_tok, up_two, gate_pieces[3], gate_pieces[5])
+    att_tok, up_one_x, up_two_y = tie(att_tok, up_one_x, up_two_y)
     a_pre = matmul(att_tok, out_full)
     a_scale = norm_scale(a_pre)
     h_tok = x_tok.astype(f32) + a_pre * a_scale * gain_attn
@@ -1517,7 +1506,7 @@
     cot = lax.all_to_all(cot, ("row", "zh", "zl"), 0, 0)
     cot_tok = cot.transpose(1, 0, 2).reshape(mine, width).astype(f32)
 
-    up_pieces = gathered(up_one, up_two, swap_bit(up_one, "dp", 1), swap_bit(up_two, "dp", 2))
+    up_pieces = gathered(up_one, up_two, up_one_x, up_two_y)
     gate_low, up_low, down_low = (
         v.astype(bf16) for v in (gate_weight, up_weight, down_weight)
     )
@@ -1556,26 +1545,11 @@
     grad_att = to_heads(datt)
     grad_gate_w = matmul(h_full, grad_gate, TN).astype(bf16)
     grad_up_w = matmul(h_full, grad_up, TN).astype(bf16)
+    grad_att, grad_gate_w, grad_up_w = tie(grad_att, grad_gate_w, grad_up_w)
     grad_down_w = matmul(hidden, dm_full, TN).astype(bf16)
     grad_out = matmul(att_tok, grad_a, TN).astype(bf16)
 
-    low_bit, high_bit = d % 2, d // 2
-
-    def pick(vals, dim, index):
-        return lax.dynamic_slice_in_dim(vals, index, 1, dim)
-
-    def trade(vals, dim, bit, index):
-        got = swap_bit(pick(vals, dim, 1 - index), "dp", bit)
-        return (pick(vals, dim, index).astype(f32) + got.astype(f32)).astype(bf16)
-
-    view = grad_down_w.reshape(n_dp // 2, 2, hidden_width // n_dp, width)
-    down_one = trade(view[..., : width // 2], 1, 1, low_bit)
-    down_two = trade(view[..., width // 2 :], 0, 2, high_bit)
-
     dqt, dk, dv = attend_back(query, key, key_t, value, grad_att, att, log_total, ends)
-    inv_scale, down_one, down_two = tie(inv_scale, down_one, down_two)
-    down_one = trade(down_one, 0, 2, high_bit)[0, 0]
-    down_two = trade(down_two, 1, 1, low_bit)[0, 0]
     weighted, inner, grad_head = unturn(dqt, dk, qkv, inv_scale, gains, cos_two, sin_two)
     def data_sums(grad):
         half = grad.shape[0] // 2
@@ -1597,10 +1571,6 @@
 
     gate_parts = owner_parts(data_sums(grad_gate_w))
     up_sums = data_sums(grad_up_w)
-    inner, *gate_parts = tie(inner, *gate_parts)
-    sum_gate = jnp.where(same, gate_parts[0].astype(f32), 0.0)
-    for part in gate_parts[1:]:
-        sum_gate = sum_gate + part.astype(f32)
     inner = (small_sum(inner.T, ("row", "zl")) / width).T
     cube = inv_scale * inv_scale * inv_scale * inner
     dqkv = jnp.concatenate(
@@ -1613,12 +1583,14 @@
     )
     grad_qkv = matmul(x_full, dqkv, TN).astype(bf16)
 
+    qkv_full, *gate_parts = tie(qkv_full, *gate_parts)
+    sum_gate = jnp.where(same, gate_parts[0].astype(f32), 0.0)
+    for part in gate_parts[1:]:
+        sum_gate = sum_gate + part.astype(f32)
     dx = matmul(dqkv, qkv_full, NT).astype(bf16)
     here = lax.dynamic_slice_in_dim(dx, block_at * mine, mine, 0).astype(f32) + dh_tok
     dx = lax.dynamic_update_slice_in_dim(dx, here.astype(bf16), block_at * mine, 0)
-    dtokens, sum_qkv, sum_up, sum_down = last_sums(
-        dx, grad_qkv, [jnp.stack(up_sums), jnp.stack([down_one, down_two])]
-    )
+    dtokens, sum_down, sum_qkv, sum_up = last_sums(dx, grad_down_w, grad_qkv, jnp.stack(up_sums))
     sum_qkv = sum_qkv.reshape(qkv_first.shape)
 
     half_w = width // 2
@@ -1633,6 +1605,7 @@
         jnp.zeros((2, width), f32), grad_head, block_at * col_width, 1
     )
     small = jnp.concatenate([head_place, grad_gain_attn[None], grad_gain_mlp[None]], axis=0)
+    small, sum_down = tie(small, sum_down)
     small = small_sum(small, ("dp", "row", "zh", "zl"))
     col_at = g * tp + t
     sum_head = lax.dynamic_slice_in_dim(small[:2], col_at * col_width, col_width, 1)

time: 1380 us -> 1330 us (0.964)
  waiting for transfers between devices: 183 us -> 129 us
  Pallas kernels: 717 us -> 753 us
  local copies, waits for them, and re-layouts: 107 us -> 90.8 us
    reduce_scatter x4, waiting for transfers between devices: 0.08 us -> 64.1 us  [data_sums(): lax.psum_scatter(grad[i * half:(i + 1) * half], 'dp', scatter_dimension=0...]
    ppermute x21 -> x17, waiting for transfers between devices: 84.3 us -> 23.2 us  [swap_bit(): lax.ppermute(piece, axis, [(i, i ^ bit) for i in range(lax.axis_size(axis...]
    ppermute x6 -> x4, waiting for transfers between devices: 68.8 us -> 31.1 us  [swap(): return lax.ppermute(piece, axis, [(0, 1), (1, 0)])]
    ppermute x1, waiting for transfers between devices: 29.3 us -> 0.01 us  [owner_parts(): lax.ppermute(keep, axes, [(1, 0), (2, 3)])]
    pallas_call x1, Pallas kernels: 134 us -> 162 us  [first_gather(): pl.pallas_call(functools.partial(gather_kernel, chunks), in_specs=[anywhe...]
    ppermute x6 -> x4, starting transfers between devices: 26 us -> 3.77 us  [swap(): return lax.ppermute(piece, axis, [(0, 1), (1, 0)])]
    pallas_call x1, Pallas kernels: 195 us -> 212 us  [last_sums(): pl.pallas_call(functools.partial(last_kernel, chunks), in_specs=[anywhere...]
    ppermute x21 -> x17, starting transfers between devices: 29.2 us -> 43 us  [swap_bit(): lax.ppermute(piece, axis, [(i, i ^ bit) for i in range(lax.axis_size(axis...]
  transfers between devices with their start and end apart: 43 -> 37, of which waited for: 11 -> 10; matrix products, arithmetic and copies ran while one was open for 22% -> 23% of each run, Pallas kernels for 42% -> 47%
where the time goes in v3:
time: 1330 us; the launch traced here: 1320 us
  Pallas kernels  753 us (57%)
  matrix products  151 us (11%)
  waiting for transfers between devices  129 us (10%)
  other arithmetic  112 us (8%)
  local copies, waits for them, and re-layouts  90.8 us (7%)
  starting transfers between devices  72.2 us (5%)
  between operations  15 us (1%)
    pallas_call x3, Pallas kernels, tile_call(): pl.pallas_call(functools.partial(tile_kernel, job, tp, chunks), in_specs=...  299 us
    pallas_call x1, Pallas kernels, last_sums(): pl.pallas_call(functools.partial(last_kernel, chunks), in_specs=[anywhere...  212 us
    pallas_call x1, Pallas kernels, first_gather(): pl.pallas_call(functools.partial(gather_kernel, chunks), in_specs=[anywhe...  162 us
    dot_general x9, matrix products, matmul(): return lax.dot_general(left, right, dims, preferred_element_type=f32)  151 us
    reduce_scatter x4, waiting for transfers between devices, data_sums(): lax.psum_scatter(grad[i * half:(i + 1) * half], 'dp', scatter_dimension=0...  64.1 us
    ppermute x17, starting transfers between devices, swap_bit(): lax.ppermute(piece, axis, [(i, i ^ bit) for i in range(lax.axis_size(axis...  43 us
    ppermute x4, waiting for transfers between devices, swap(): return lax.ppermute(piece, axis, [(0, 1), (1, 0)])  31.1 us
    unnamed x123, local copies, waits for them, and re-layouts  30.6 us
  transfers between devices with their start and end apart: 37, of which 10 were waited for; matrix products, arithmetic and copies ran while one was open for 23% of the time, Pallas kernels for 47%

profile of v3, /device:TPU:0, one launch (start us, length us, event | category | flops | bytes accessed | tf_op | source)
XLA Modules:
  0.0 1323.5 jit_solution(434999818207566160)
XLA Ops:
  9.1 3.2 convert.8
  13.1 3.9 dynamic-slice_convert_fusion.1
  18.9 161.8 %first_gather.1 = (bf16[8,2048,256]{2,1,0:T(8,128)(2,1)}, bf16[2048,1536]{1,0:T(8,128)(2,1)}, f32[8,16,128]{2,1,0:T(8,128)}, bf16[256,1536]{1,0:T(8,128)(2,1)}, bf16[256,2048]{1,0:T(8,128)(2,1)}) custom-call(bf16[4096,256]{1,0:T(8,128)(2,1)} %tok_ref.1, bf16[1024,1536]{1,0:T(8,128)(2,1)} %pad_maximum_fusion.1.low_ref, f32[16,128]{1,0:T(8,128)} %bitcast.160, ...), custom_call_target="tpu_custom_call" | custom-call | bytes 25165824 | tf_op jit(solution)/shard_map/first_gather/pallas_call | solution.py:295
  182.8 8.5 copy.134
  191.3 15.7 %fusion.35.qkv_ref = f32[2048,1536]{1,0:T(8,128)S(1)} fusion(bf16[2048,2048]{1,0:T(8,128)(2,1)} %bitcast.122, bf16[2048,1536]{1,0:T(8,128)(2,1)S(1)} %bitcast.170), kind=kOutput, calls=%fused_computation.120 | convolution fusion | flops 12884901888 | bytes 27262976 | tf_op jit(solution)/shard_map/dot_general | solution.py:1406
  213.6 3.9 fusion.11
  224.1 12.7 collective-permute-done.3.refs_4_
  238.1 12.0 prepare.1
  259.0 2.9 collective-permute-start.5
  262.2 31.1 %collective-permute-done.refs_9_ = bf16[256,1024]{1,0:T(8,128)(2,1)S(1)} collective-permute-done((bf16[256,1024]{1,0:T(8,128)(2,1)S(1)}, bf16[256,1024]{1,0:T(8,128)(2,1)S(1)}, u32[]{:S(2)}, u32[]{:S(2)}) %collective-permute-start) | collective-permute-done | bytes 524320 | tf_op jit(solution)/shard_map/ppermute | solution.py:33
  295.7 23.5 %attend.1 = (bf16[2048,512]{1,0:T(8,128)(2,1)S(1)}, f32[4,1,2048]{2,1,0:T(1,128)S(1)}) custom-call(s32[4]{0:T(128)S(1)} %bitcast.117, bf16[2048,512]{1,0:T(8,128)(2,1)S(1)} %copy-done.8, bf16[2048,512]{1,0:T(8,128)(2,1)} %get-tuple-element.99.k_ref, bf16[512,2048]{1,0:T(8,128)(2,1)} %get-tuple-element.100.vt_ref), custom_call_target="tpu_custom_call" | custom-call | flops 4294967296 | bytes 8388608 | tf_op jit(solution)/shard_map/attend/pallas_call | solution.py:384
  319.3 2.7 copy.111
  322.0 4.5 all-to-all-start
  328.2 6.3 collective-permute-start.9
  334.5 2.7 dynamic-slice_convert_fusion
  337.6 6.2 convert_element_type.148.refs_1_
  343.8 6.3 convert_element_type.149.refs_8_
  350.1 2.6 convert_element_type.151.refs_1_
  354.2 9.2 all-to-all-done
  364.5 7.3 collective-permute-start.10
  374.0 8.2 collective-permute-start.11
  382.2 10.6 multiply_reduce_fusion.5
  392.8 3.6 all-to-all-start.2
  396.4 4.9 fusion.refs_0_
  401.4 3.8 collective-permute-done.11.refs_14_
  405.2 99.1 %gate_up.1 = (bf16[2048,2048]{1,0:T(8,128)(2,1)}, bf16[2048,2048]{1,0:T(8,128)(2,1)}, bf16[2048,2048]{1,0:T(8,128)(2,1)}, bf16[2048,2048]{1,0:T(8,128)(2,1)}, bf...) custom-call(bf16[512,2048]{1,0:T(8,128)(2,1)} %fusion.refs_0_, ...), custom_call_target="tpu_custom_call" | custom-call | flops 34359738368 | bytes 33554432 | tf_op jit(solution)/shard_map/gate_up/pallas_call | solution.py:1023
  504.3 65.3 %down.1 = (bf16[2048,2048]{1,0:T(8,128)(2,1)}, f32[512,2048]{1,0:T(8,128)}) custom-call(bf16[2048,2048]{1,0:T(8,128)(2,1)} %get-tuple-element.145.refs_0_, bf16[2048,1024]{1,0:T(8,128)(2,1)} %convert_element_type.151.refs_1_, bf16[2048,1024]{1,0:T(8,128)(2,1)} %get-tuple-element.119.refs_2_), custom_call_target="tpu_custom_call" | custom-call | flops 17179869184 | bytes 33554432 | tf_op jit(solution)/shard_map/down/pallas_call | solution.py:1023
  573.1 3.2 copy-done.17
  578.5 4.6 subtract_convert_fusion.3
  583.1 135.0 %feed_back.1 = (bf16[2048,2048]{1,0:T(8,128)(2,1)}, bf16[2048,2048]{1,0:T(8,128)(2,1)}, bf16[2048,2048]{1,0:T(8,128)(2,1)}, f32[512,2048]{1,0:T(8,128)}) custom-call(bf16[512,2048]{1,0:T(8,128)(2,1)} %get-tuple-element.266.refs_0_, bf16[2048,2048]{1,0:T(8,128)(2,1)} %get-tuple-element.125.refs_1_, bf16[2048,2048]{1,0:T(8,128)(2,1)} %get-tuple-element.126.refs_2_, ...), custom_call_target="tpu_custom_call" | custom-call | flops 51539607552 | bytes 33554432 | tf_op jit(solution)/shard_map/feed_back/pallas_call | solution.py:1023
  718.1 6.2 multiply_reduce_fusion.1
  726.3 8.9 convolution_convert_fusion.6
  736.7 3.6 all-to-all-start.3
  740.4 23.9 %convolution_convert_fusion.4 = bf16[2048,2048]{1,0:T(8,128)(2,1)} fusion(bf16[2048,2048]{1,0:T(8,128)(2,1)} %get-tuple-element.133, bf16[2048,2048]{1,0:T(8,128)(2,1)} %get-tuple-element.134), kind=kOutput, calls=%fused_computation.5 | convolution fusion | flops 17184063488 | bytes 25165824 | tf_op jit(solution)/shard_map/dot_general | solution.py:1406
  764.3 23.8 %convolution_convert_fusion.3 = bf16[2048,2048]{1,0:T(8,128)(2,1)} fusion(bf16[2048,2048]{1,0:T(8,128)(2,1)} %get-tuple-element.133, bf16[2048,2048]{1,0:T(8,128)(2,1)} %get-tuple-element.135), kind=kOutput, calls=%fused_computation.4 | convolution fusion | flops 17184063488 | bytes 25165824 | tf_op jit(solution)/shard_map/dot_general | solution.py:1406
  788.1 6.8 fusion.30
  795.6 6.2 fusion.29
  806.0 4.4 all-to-all-start.1
  810.4 6.8 convolution_convert_fusion
  817.3 3.0 constant_dynamic-slice_fusion.2
  822.4 24.2 %convolution_convert_fusion.1.down_ref = bf16[2048,2048]{1,0:T(8,128)(2,1)} fusion(bf16[2048,2048]{1,0:T(8,128)(2,1)} %get-tuple-element.145.refs_0_, bf16[2048,2048]{1,0:T(8,128)(2,1)} %get-tuple-element.146), kind=kOutput, calls=%fused_computation.2 | convolution fusion | flops 17184063488 | bytes 25165824 | tf_op jit(solution)/shard_map/dot_general | solution.py:1406
  846.7 30.4 %attend_back.1 = (f32[512,2048]{1,0:T(8,128)}, f32[2048,512]{1,0:T(8,128)}, bf16[2048,512]{1,0:T(8,128)(2,1)S(1)}) custom-call(s32[4]{0:T(128)S(1)} %bitcast.118, bf16[2048,512]{1,0:T(8,128)(2,1)S(1)} %copy-done.9, bf16[2048,512]{1,0:T(8,128)(2,1)} %get-tuple-element.99.k_ref, bf16[512,2048]{1,0:T(8,128)(2,1)} %get-tuple-element.121.kt_ref, ...), custom_call_target="tpu_custom_call" | custom-call | flops 10737418240 | bytes 20971520 | tf_op jit(solution)/shard_map/attend_back/pallas_call | solution.py:476
  877.1 14.4 %unturn.1 = (f32[2048,1024]{1,0:T(8,128)}, f32[2048,2]{1,0:T(8,128)S(1)}, f32[2,512]{1,0:T(2,128)S(1)}) custom-call(f32[512,2048]{1,0:T(8,128)} %get-tuple-element.138.dqt_ref, f32[2048,512]{1,0:T(8,128)} %get-tuple-element.139.dk_ref, f32[2048,1536]{1,0:T(8,128)} %copy-done.12, f32[2048,2]{1,0:T(8,128)S(1)} %copy-done.1, f32[2,512]{1,0:T(2,128)S(1)} %copy-done.6, ...), custom_call_target="tpu_custom_call" | custom-call | flops 20971520 | bytes 25165824 | tf_op jit(solution)/shard_map/unturn/pallas_call | solution.py:599
  894.4 5.7 add_convert_fusion
  909.7 9.7 subtract_convert_fusion.1
  919.4 2.9 broadcast_select_fusion
  924.0 6.0 collective-permute-start.17
  931.3 18.3 %convolution_convert_fusion.5.qkv_ref = bf16[2048,1536]{1,0:T(8,128)(2,1)} fusion(bf16[2048,2048]{1,0:T(8,128)(2,1)} %bitcast.125, bf16[2048,512]{1,0:T(8,128)(2,1)S(1)} %copy-done.11, bf16[2048,512]{1,0:T(8,128)(2,1)} %get-tuple-element.261, bf16[2048,512]{1,0:T(8,128)(2,1)S(1)} %copy-done.24), kind=kOutput, calls=%fused_computation.6 | convolution fusion | flops 12906921984 | bytes 20971520 | tf_op jit(solution)/shard_map/dot_general | solution.py:1406
  949.7 8.1 reduce-scatter.15.cloned.1.call-done
  957.7 56.0 %reduce-scatter.13.cloned.1.call-done = bf16[256,2048]{1,0:T(8,128)(2,1)} async-done(((bf16[1024,2048]{1,0:T(8,128)(2,1)}), bf16[256,2048]{1,0:T(8,128)(2,1)}) %reduce-scatter.13.cloned.1.call-update) | async-done | bytes 1048592 | tf_op jit(solution)/shard_map/reduce_scatter | solution.py:1557
  1013.7 3.1 pad_maximum_fusion.4.up_ref
  1016.8 18.9 %convolution_convert_fusion.2 = bf16[2048,2048]{1,0:T(8,128)(2,1)} fusion(bf16[2048,1536]{1,0:T(8,128)(2,1)} %get-tuple-element.144, bf16[2048,512]{1,0:T(8,128)(2,1)S(1)} %copy-done.11, bf16[2048,512]{1,0:T(8,128)(2,1)} %get-tuple-element.261, bf16[2048,512]{1,0:T(8,128)(2,1)} %get-tuple-element.260), kind=kOutput, calls=%fused_computation.3 | convolution fusion | flops 12907970560 | bytes 20971520 | tf_op jit(solution)/shard_map/dot_general | solution.py:1406
  1035.7 4.9 fusion.4.dx_ref
  1040.6 211.6 %last_sums.1 = (f32[4096,256]{1,0:T(8,128)}, f32[512,1024]{1,0:T(8,128)}, f32[256,1536]{1,0:T(8,128)}, f32[256,2048]{1,0:T(8,128)}) custom-call(bf16[2048,2048]{1,0:T(8,128)(2,1)} %fusion.4.dx_ref, bf16[2048,2048]{1,0:T(8,128)(2,1)} %convolution_convert_fusion.1.down_ref, bf16[2048,1536]{1,0:T(8,128)(2,1)} %convolution_convert_fusion.5.qkv_ref, ...), custom_call_target="tpu_custom_call" | custom-call | bytes 33554432 | tf_op jit(solution)/shard_map/last_sums/pallas_call | solution.py:1333
  1257.7 3.0 copy.122
  1260.7 3.0 copy.113
  1264.5 8.8 multiply_subtract_fusion.2
  1273.3 7.8 collective-permute-start.21
  1281.1 5.6 multiply_subtract_fusion.1
  1286.9 5.5 multiply_subtract_fusion
  1292.4 3.0 copy.123
  1297.1 4.8 multiply_subtract_fusion.3
  1301.9 3.2 copy.127
  1312.3 4.5 copy.149
  (249 shorter events, 85.9 us)
Async XLA Ops:
  7.2 175.5 %all-gather.8.cloned.1.call-start = ((), (), s32[]{:S(2)}) async-start(), calls=%async_computation.16 | async-start | bytes 1310720 | tf_op jit(solution)/shard_map/all_gather | solution.py:1464
  9.1 243.3 %all-gather.10.cloned.1.call-start = ((), (), s32[]{:S(2)}) async-start(), calls=%async_computation.17 | async-start | bytes 5242880 | tf_op jit(solution)/shard_map/all_gather | solution.py:1465
  18.9 162.7 %copy-start.23 = (bf16[256,2048]{1,0:T(8,128)(2,1)S(1)}, bf16[256,2048]{1,0:T(8,128)(2,1)}, u32[]{:S(2)}) copy-start(bf16[256,2048]{1,0:T(8,128)(2,1)} %get-tuple-element.286) | copy-start | bytes 3145732
  182.7 8.6 slice-start.2
  182.8 199.4 %all-gather.6.cloned.1.call-start = ((), (), s32[]{:S(2)}) async-start(), calls=%async_computation.10 | async-start | bytes 12582912 | tf_op jit(solution)/shard_map/all_gather | solution.py:1482
  182.8 8.5 slice-start.3
  207.0 10.6 copy-start.12
  207.7 9.8 collective-permute-start.1
  210.7 26.1 %collective-permute-start.3 = (bf16[256,1024]{1,0:T(8,128)(2,1)}, bf16[256,1024]{1,0:T(8,128)(2,1)}, u32[]{:S(2)}, u32[]{:S(2)}) collective-permute-start(bf16[256,1024]{1,0:T(8,128)(2,1)} %get-tuple-element.274.refs_2_), channel_id=1, source_target_pairs={{0,8},{8,0},{16,24},{24,16},{1,9},{9,1},{17,25},{25,17},{2,10},{10... | collective-permute-start | bytes 1572872 | tf_op jit(solution)/shard_map/ppermute | solution.py:42
  212.0 26.0 %collective-permute-start.4 = (bf16[256,1024]{1,0:T(8,128)(2,1)}, bf16[256,1024]{1,0:T(8,128)(2,1)}, u32[]{:S(2)}, u32[]{:S(2)}) collective-permute-start(bf16[256,1024]{1,0:T(8,128)(2,1)} %get-tuple-element.273.refs_3_), channel_id=1, source_target_pairs={{0,16},{8,24},{16,0},{24,8},{1,17},{9,25},{17,1},{25,9},{2,18},{10... | collective-permute-start | bytes 1572872 | tf_op jit(solution)/shard_map/ppermute | solution.py:42
  217.5 3.8 collective-permute-start.2
  218.2 31.8 %copy-start.2 = (f32[2048,128]{1,0:T(8,128)}, f32[2048,128]{1,0:T(8,128)S(1)}, u32[]{:S(2)}) copy-start(f32[2048,128]{1,0:T(8,128)S(1)} %get-tuple-element.288.cos_ref) | copy-start | bytes 3145732
  218.4 31.7 %copy-start.5 = (f32[2,512]{1,0:T(2,128)}, f32[2,512]{1,0:T(2,128)S(1)}, u32[]{:S(2)}) copy-start(f32[2,512]{1,0:T(2,128)S(1)} %reshape_squeeze.3.gains_ref) | copy-start | bytes 12292
  252.4 6.6 copy-start.37
  254.7 64.5 %collective-permute-start.6 = (bf16[512,1024]{1,0:T(8,128)(2,1)}, bf16[512,1024]{1,0:T(8,128)(2,1)}, u32[]{:S(2)}, u32[]{:S(2)}) collective-permute-start(bf16[512,1024]{1,0:T(8,128)(2,1)} %pad_maximum_fusion.7), channel_id=1, source_target_pairs={{0,16},{8,24},{16,0},{24,8},{1,17},{9,25},{17,1},{25,9},{2,18},{10... | collective-permute-start | bytes 3145736 | tf_op jit(solution)/shard_map/ppermute | solution.py:42
  258.7 60.6 %collective-permute-start.7 = (bf16[512,1024]{1,0:T(8,128)(2,1)}, bf16[512,1024]{1,0:T(8,128)(2,1)}, u32[]{:S(2)}, u32[]{:S(2)}) collective-permute-start(bf16[512,1024]{1,0:T(8,128)(2,1)} %pad_maximum_fusion.8), channel_id=1, source_target_pairs={{0,8},{8,0},{16,24},{24,16},{1,9},{9,1},{17,25},{25,17},{2,10},{10... | collective-permute-start | bytes 3145736 | tf_op jit(solution)/shard_map/ppermute | solution.py:42
  259.0 34.3 %collective-permute-start = (bf16[256,1024]{1,0:T(8,128)(2,1)S(1)}, bf16[256,1024]{1,0:T(8,128)(2,1)S(1)}, u32[]{:S(2)}, u32[]{:S(2)}) collective-permute-start(bf16[256,1024]{1,0:T(8,128)(2,1)S(1)} %copy-done.37), channel_id=1, source_target_pairs={{0,2},{2,0},{1,3},{3,1},{4,6},{6,4},{5,7},{7,5},{8,10},{10,8},{9,1... | collective-permute-start | bytes 1572872 | tf_op jit(solution)/shard_map/ppermute | solution.py:33
  259.0 60.2 %collective-permute-start.5 = (bf16[256,1024]{1,0:T(8,128)(2,1)}, bf16[256,1024]{1,0:T(8,128)(2,1)}, u32[]{:S(2)}, u32[]{:S(2)}) collective-permute-start(bf16[256,1024]{1,0:T(8,128)(2,1)} %get-tuple-element.102), channel_id=1, source_target_pairs={{0,2},{2,0},{1,3},{3,1},{4,6},{6,4},{5,7},{7,5},{8,10},{10,8},{9,1... | collective-permute-start | bytes 1572872 | tf_op jit(solution)/shard_map/ppermute | solution.py:33
  322.0 41.5 %all-to-all-start = ((bf16[4,512,512]{1,2,0:T(8,128)(2,1)}), bf16[4,512,512]{1,2,0:T(8,128)(2,1)}, u32[]{:S(2)}, u32[]{:S(2)}) async-start(bf16[4,512,512]{1,2,0:T(8,128)(2,1)} %copy.111), calls=%async_computation | async-start | bytes 4194304 | tf_op jit(solution)/shard_map/all_to_all | solution.py:1489
  326.4 27.8 %collective-permute-start.8 = (bf16[256,1024]{1,0:T(8,128)(2,1)}, bf16[256,1024]{1,0:T(8,128)(2,1)S(1)}, u32[]{:S(2)}, u32[]{:S(2)}) collective-permute-start(bf16[256,1024]{1,0:T(8,128)(2,1)} %copy-done.38), channel_id=1, source_target_pairs={{0,8},{8,0},{16,24},{24,16},{1,9},{9,1},{17,25},{25,17},{2,10},{10... | collective-permute-start | bytes 1572872 | tf_op jit(solution)/shard_map/ppermute | solution.py:42
  328.2 26.0 %collective-permute-start.9 = (bf16[256,1024]{1,0:T(8,128)(2,1)}, bf16[256,1024]{1,0:T(8,128)(2,1)S(1)}, u32[]{:S(2)}, u32[]{:S(2)}) collective-permute-start(bf16[256,1024]{1,0:T(8,128)(2,1)} %collective-permute-done.5.refs_10_), channel_id=1, source_target_pairs={{0,16},{8,24},{16,0},{24,8},{1,17},{9,25},{17,1},{25,9},{2,18},{10... | collective-permute-start | bytes 1572872 | tf_op jit(solution)/shard_map/ppermute | solution.py:42
  337.3 64.1 %collective-permute-start.12 = (bf16[512,1024]{1,0:T(8,128)(2,1)}, bf16[512,1024]{1,0:T(8,128)(2,1)}, u32[]{:S(2)}, u32[]{:S(2)}) collective-permute-start(bf16[512,1024]{1,0:T(8,128)(2,1)} %dynamic-slice_convert_fusion), channel_id=1, source_target_pairs={{0,2},{2,0},{1,3},{3,1},{4,6},{6,4},{5,7},{7,5},{8,10},{10,8},{9,1... | collective-permute-start | bytes 3145736 | tf_op jit(solution)/shard_map/ppermute | solution.py:33
  337.6 12.5 slice-start
  343.8 6.3 slice-start.1
  352.7 10.8 copy-start.39
  354.2 38.6 %copy-start.40 = (bf16[256,1024]{1,0:T(8,128)(2,1)}, bf16[256,1024]{1,0:T(8,128)(2,1)S(1)}, u32[]{:S(2)}) copy-start(bf16[256,1024]{1,0:T(8,128)(2,1)S(1)} %collective-permute-done.8.refs_11_) | copy-start | bytes 1572868
  354.2 38.6 %copy-start.41 = (bf16[256,1024]{1,0:T(8,128)(2,1)}, bf16[256,1024]{1,0:T(8,128)(2,1)S(1)}, u32[]{:S(2)}) copy-start(bf16[256,1024]{1,0:T(8,128)(2,1)S(1)} %collective-permute-done.9.refs_13_) | copy-start | bytes 1572868
  364.5 36.8 %collective-permute-start.10 = (bf16[512,1024]{1,0:T(8,128)(2,1)}, bf16[512,1024]{1,0:T(8,128)(2,1)}, u32[]{:S(2)}, u32[]{:S(2)}) collective-permute-start(bf16[512,1024]{1,0:T(8,128)(2,1)} %pad_maximum_fusion.9), channel_id=1, source_target_pairs={{0,16},{8,24},{16,0},{24,8},{1,17},{9,25},{17,1},{25,9},{2,18},{10... | collective-permute-start | bytes 3145736 | tf_op jit(solution)/shard_map/ppermute | solution.py:42
  374.0 31.2 %collective-permute-start.11 = (bf16[512,1024]{1,0:T(8,128)(2,1)}, bf16[512,1024]{1,0:T(8,128)(2,1)}, u32[]{:S(2)}, u32[]{:S(2)}) collective-permute-start(bf16[512,1024]{1,0:T(8,128)(2,1)} %pad_maximum_fusion.10), channel_id=1, source_target_pairs={{0,8},{8,0},{16,24},{24,16},{1,9},{9,1},{17,25},{25,17},{2,10},{10... | collective-permute-start | bytes 3145736 | tf_op jit(solution)/shard_map/ppermute | solution.py:42
  392.8 179.3 %all-to-all-start.2 = ((bf16[8,512,256]{2,1,0:T(8,128)(2,1)}), bf16[8,512,256]{2,1,0:T(8,128)(2,1)S(1)}, u32[]{:S(2)}, u32[]{:S(2)}) async-start(bf16[8,512,256]{2,1,0:T(8,128)(2,1)} %bitcast.131), calls=%async_computation.2 | async-start | bytes 4194304 | tf_op jit(solution)/shard_map/all_to_all | solution.py:1506
  718.1 6.3 copy-start.14
  726.3 8.9 copy-start.33
  736.7 51.3 %all-to-all-start.3 = ((bf16[4,512,512]{2,1,0:T(8,128)(2,1)}), bf16[4,512,512]{2,1,0:T(8,128)(2,1)S(1)}, u32[]{:S(2)}, u32[]{:S(2)}) async-start(bf16[4,512,512]{2,1,0:T(8,128)(2,1)} %bitcast.111), calls=%async_computation.3 | async-start | bytes 4194304 | tf_op jit(solution)/shard_map/all_to_all | solution.py:1494
  740.4 179.0 %reduce-scatter.11.cloned.1.call-start = ((), (), s32[]{:S(2)}) async-start(), calls=%async_computation.12 | async-start | bytes 5242880 | tf_op jit(solution)/shard_map/reduce_scatter | solution.py:1557
  788.1 6.8 copy-start.26
  794.9 124.5 %reduce-scatter.9.cloned.1.call-start = ((), (), s32[]{:S(2)}) async-start(), calls=%async_computation.11 | async-start | bytes 5242880 | tf_op jit(solution)/shard_map/reduce_scatter | solution.py:1557
  795.5 162.2 %reduce-scatter.15.cloned.1.call-start = ((), (), s32[]{:S(2)}) async-start(), calls=%async_computation.14 | async-start | bytes 5242880 | tf_op jit(solution)/shard_map/reduce_scatter | solution.py:1557
  801.8 211.9 %reduce-scatter.13.cloned.1.call-start = ((), (), s32[]{:S(2)}) async-start(), calls=%async_computation.13 | async-start | bytes 5242880 | tf_op jit(solution)/shard_map/reduce_scatter | solution.py:1557
  806.0 454.7 %all-to-all-start.1 = ((bf16[8,512,256]{2,1,0:T(8,128)(2,1)}), bf16[8,512,256]{2,1,0:T(8,128)(2,1)}, u32[]{:S(2)}, u32[]{:S(2)}) async-start(bf16[8,512,256]{2,1,0:T(8,128)(2,1)} %bitcast.130), calls=%async_computation.1 | async-start | bytes 4194304 | tf_op jit(solution)/shard_map/all_to_all | solution.py:1527
  810.4 453.4 %reduce-scatter.19.cloned.1.call-start = ((), (), s32[]{:S(2)}) async-start(), calls=%async_computation.18 | async-start | bytes 5242880
  821.9 72.5 %collective-permute-start.18 = (bf16[2048,1024]{1,0:T(8,128)(2,1)}, bf16[2048,1024]{1,0:T(8,128)(2,1)}, u32[]{:S(2)}, u32[]{:S(2)}) collective-permute-start(bf16[2048,1024]{1,0:T(8,128)(2,1)} %constant_dynamic-slice_fusion.2), channel_id=1, source_target_pairs={{0,4},{4,0},{1,5},{5,1},{2,6},{6,2},{3,7},{7,3},{8,12},{12,8},{9,1... | collective-permute-start | bytes 12582920 | tf_op jit(solution)/shard_map/ppermute | solution.py:33
  822.4 24.3 %copy-start.9 = (bf16[2048,512]{1,0:T(8,128)(2,1)S(1)}, bf16[2048,512]{1,0:T(8,128)(2,1)}, u32[]{:S(2)}) copy-start(bf16[2048,512]{1,0:T(8,128)(2,1)} %copy-done.7) | copy-start | bytes 6291460
  846.7 30.4 %copy-start.3 = (f32[2048,128]{1,0:T(8,128)S(1)}, f32[2048,128]{1,0:T(8,128)}, u32[]{:S(2)}) copy-start(f32[2048,128]{1,0:T(8,128)} %copy-done.2) | copy-start | bytes 3145732
  846.7 30.4 %copy-start.6 = (f32[2,512]{1,0:T(2,128)S(1)}, f32[2,512]{1,0:T(2,128)}, u32[]{:S(2)}) copy-start(f32[2,512]{1,0:T(2,128)} %copy-done.5) | copy-start | bytes 12292
  877.1 14.4 %copy-start.10 = (bf16[2048,512]{1,0:T(8,128)(2,1)}, bf16[2048,512]{1,0:T(8,128)(2,1)S(1)}, u32[]{:S(2)}) copy-start(bf16[2048,512]{1,0:T(8,128)(2,1)S(1)} %get-tuple-element.142) | copy-start | bytes 6291460
  891.8 1.2 collective-permute-start.13
  902.6 407.1 %reduce-scatter.17.cloned.1.call-start = ((), (), s32[]{:S(2)}) async-start(), calls=%async_computation.15 | async-start | bytes 1310720 | tf_op jit(solution)/shard_map/reduce_scatter | solution.py:1602
  904.3 3.8 collective-permute-start.14
  919.4 12.0 copy-start.11
  919.4 11.9 copy-start.24
  922.3 27.4 %copy-start.22 = (bf16[256,2048]{1,0:T(8,128)(2,1)}, bf16[256,2048]{1,0:T(8,128)(2,1)S(1)}, u32[]{:S(2)}) copy-start(bf16[256,2048]{1,0:T(8,128)(2,1)S(1)} %get-tuple-element.150) | copy-start | bytes 3145732
  922.3 94.5 %collective-permute-start.16 = (bf16[256,2048]{1,0:T(8,128)(2,1)}, bf16[256,2048]{1,0:T(8,128)(2,1)}, u32[]{:S(2)}, u32[]{:S(2)}) collective-permute-start(bf16[256,2048]{1,0:T(8,128)(2,1)} %get-tuple-element.271), channel_id=1, source_target_pairs={{2,4},{4,2},{3,5},{5,3},{10,12},{12,10},{11,13},{13,11},{18,20},{2... | collective-permute-start | bytes 3145736 | tf_op jit(solution)/shard_map/ppermute | solution.py:1568
  924.0 92.7 %collective-permute-start.17 = (bf16[256,2048]{1,0:T(8,128)(2,1)}, bf16[256,2048]{1,0:T(8,128)(2,1)}, u32[]{:S(2)}, u32[]{:S(2)}) collective-permute-start(bf16[256,2048]{1,0:T(8,128)(2,1)} %get-tuple-element.271), channel_id=1, source_target_pairs={{0,4},{6,2},{1,5},{7,3},{8,12},{14,10},{9,13},{15,11},{16,20},{22,... | collective-permute-start | bytes 3145736 | tf_op jit(solution)/shard_map/ppermute | solution.py:1569
  930.0 86.7 %collective-permute-start.15 = (bf16[256,2048]{1,0:T(8,128)(2,1)S(1)}, bf16[256,2048]{1,0:T(8,128)(2,1)}, u32[]{:S(2)}, u32[]{:S(2)}) collective-permute-start(bf16[256,2048]{1,0:T(8,128)(2,1)S(1)} %get-tuple-element.150), channel_id=1, source_target_pairs={{2,0},{4,6},{3,1},{5,7},{10,8},{12,14},{11,9},{13,15},{18,16},{20,... | collective-permute-start | bytes 3145736 | tf_op jit(solution)/shard_map/ppermute | solution.py:1567
  1252.2 11.6 collective-permute-start.19
  1263.8 17.2 %copy-start.27 = (f32[256,2048]{1,0:T(8,128)S(1)}, f32[256,2048]{1,0:T(8,128)}, u32[]{:S(2)}) copy-start(f32[256,2048]{1,0:T(8,128)} %param.41) | copy-start | bytes 6291460
  1263.8 17.2 %copy-start.28 = (f32[256,2048]{1,0:T(8,128)S(1)}, f32[256,2048]{1,0:T(8,128)}, u32[]{:S(2)}) copy-start(f32[256,2048]{1,0:T(8,128)} %param.40) | copy-start | bytes 6291460
  1263.8 17.2 %copy-start.32 = (f32[256,2048]{1,0:T(8,128)S(1)}, f32[256,2048]{1,0:T(8,128)}, u32[]{:S(2)}) copy-start(f32[256,2048]{1,0:T(8,128)} %get-tuple-element.154) | copy-start | bytes 6291460
  1263.9 9.4 collective-permute-start.20
  1273.3 13.5 %collective-permute-start.21 = (f32[4,2048]{1,0:T(4,128)S(1)}, f32[4,2048]{1,0:T(4,128)S(1)}, u32[]{:S(2)}, u32[]{:S(2)}) collective-permute-start(f32[4,2048]{1,0:T(4,128)S(1)} %add.295), channel_id=1, source_target_pairs={{0,4},{4,0},{1,5},{5,1},{2,6},{6,2},{3,7},{7,3},{8,12},{12,8},{9,1... | collective-permute-start | bytes 98312 | tf_op jit(solution)/shard_map/ppermute | solution.py:42
  1281.1 5.9 copy-start.29
  1281.1 5.9 copy-start.30
  1286.7 8.7 collective-permute-start.22
  1295.5 12.9 collective-permute-start.23
  (29 other events, 87.5 us)
Sparse Core Ops, SparseCore 0:
  10.2 55.2 all-gather.7
  182.9 62.8 all-gather.9
  252.5 17.7 all-gather.5
  795.0 51.2 reduce-scatter.10
  849.4 52.7 reduce-scatter.8
  905.0 52.6 reduce-scatter.14
  961.0 52.6 reduce-scatter.12
  1017.2 90.8 reduce-scatter.18
  1263.9 33.5 reduce-scatter.16

commit v4 on v3

--- a/solution.py
+++ b/solution.py
@@ -1120,7 +1120,8 @@
 def last_kernel(
     chunks, dx_ref, down_ref, qkv_ref, up_ref, out_ref, down_out, qkv_out, up_out,
     own, from_row, near, from_t, give, from_zh,
-    down_own, down_in, down_sum, down_late, qkv_own, qkv_in, qkv_sum, qkv_late, up_stay, up_late,
+    down_own, down_in, down_next, down_sum, down_late, qkv_own, qkv_in, qkv_next, qkv_sum, qkv_late,
+    up_stay, up_late,
     own_sem, row_send, row_recv, t_send, t_recv, zh_send, zh_recv,
     g_sem, d_send, d_recv, f_local, f_send, f_recv,
 ):
@@ -1144,14 +1145,13 @@
     zh_dev = (d, r, 1 - g, t)
     cross_dev = (d, 1 - r, 1 - g, t)
 
-    def dp_dev(k):
-        return (lax.rem(d + k, n_dp), r, g, t)
+    bits = (lax.rem(d, 2), d // 2)
+    near_devs = ((bits[1] * 2 + 1 - bits[0], r, g, t), ((1 - bits[1]) * 2 + bits[0], r, g, t))
 
     def t_dev(s):
         return (d, r, g, lax.rem(t + s, tp))
 
-    partners = [row_dev, zh_dev, cross_dev]
-    partners += [dp_dev(k) for k in range(1, n_dp)] + [t_dev(s) for s in range(1, tp)]
+    partners = [row_dev, zh_dev, cross_dev, *near_devs] + [t_dev(s) for s in range(1, tp)]
     barrier = pltpu.get_barrier_semaphore()
     for dev in partners:
         pl.semaphore_signal(barrier, inc=1, device_id=dev, device_id_type=pl.DeviceIdType.MESH)
@@ -1194,29 +1194,44 @@
     owner_start(2, up_ref, up_late)
 
     def down_piece(which, group):
-        rows, cols = down_own.shape[1:]
+        rows, cols = down_sum.shape[1:]
         return down_ref.at[
             pl.ds(pl.multiple_of(group * rows, rows), rows), pl.ds(pl.multiple_of(which * cols, cols), cols)
         ]
 
     def qkv_piece(which, group):
-        rows = qkv_own.shape[1]
+        rows = qkv_sum.shape[1]
         return qkv_ref.at[pl.ds(pl.multiple_of((which * n_dp + group) * rows, rows), rows)]
 
-    def group_copies(i, piece, mine, inbox):
-        loads = [pltpu.make_async_copy(piece(which, d), mine.at[which], g_sem.at[i, which]) for which in range(2)]
-        sends = [
-            remote(
-                piece(which, lax.rem(d + k, n_dp)), inbox.at[k - 1, which],
-                d_send.at[i, k, which], d_recv.at[i, k, which], dp_dev(k),
+    def group_at(which, first, second):
+        return second * 2 + first if which == 0 else first * 2 + second
+
+    def group_copies(i, piece, mine, inbox, following):
+        loads, sends, nexts = [], [], []
+        for which in range(2):
+            for other in range(2):
+                at = which * 2 + other
+                loads.append(
+                    pltpu.make_async_copy(
+                        piece(which, group_at(which, bits[which], other)), mine.at[at], g_sem.at[i, at]
+                    )
+                )
+                sends.append(
+                    remote(
+                        piece(which, group_at(which, 1 - bits[which], other)), inbox.at[at],
+                        d_send.at[i, at], d_recv.at[i, at], near_devs[which],
+                    )
+                )
+            nexts.append(
+                remote(
+                    mine.at[which * 2 + 1 - bits[1 - which]], following.at[which],
+                    d_send.at[i, 4 + which], d_recv.at[i, 4 + which], near_devs[1 - which],
+                )
             )
-            for which in range(2)
-            for k in range(1, n_dp)
-        ]
-        return loads, sends
-
-    down_copies = group_copies(0, down_piece, down_own, down_in)
-    qkv_copies = group_copies(1, qkv_piece, qkv_own, qkv_in)
+        return loads, sends, nexts
+
+    down_copies = group_copies(0, down_piece, down_own, down_in, down_next)
+    qkv_copies = group_copies(1, qkv_piece, qkv_own, qkv_in, qkv_next)
 
     def cols_at(which):
         return pl.ds(pl.multiple_of(which * half, half), half)
@@ -1230,7 +1245,7 @@
         cp = pltpu.make_async_copy(dx_ref.at[rows, cols_at(r)], own.at[c], own_sem.at[c])
         cp.start()
         own_copies.append(cp)
-    for loads, sends in (down_copies, qkv_copies):
+    for loads, sends, _ in (down_copies, qkv_copies):
         for cp in loads + sends:
             cp.start()
 
@@ -1270,33 +1285,44 @@
         zh_copies.append(cp)
         out_ref[pl.ds(pl.multiple_of(g * seq_len + c * step, step), step), :] = total_of(g)
 
-    def group_stage(copies, mine, inbox, total_ref):
-        for cp in copies[0]:
-            cp.wait()
-        for cp in copies[1]:
-            cp.wait_recv()
-        part = mine.shape[1]
-        block = min(64, part)
+    def group_first(copies, mine, inbox):
+        block = min(64, mine.shape[1])
+        for at in range(4):
+            copies[0][at].wait()
+            copies[1][at].wait_recv()
+
+            def add(i, carry, at=at):
+                span = pl.ds(pl.multiple_of(i * block, block), block)
+                mine[at, span, :] = (mine[at, span, :].astype(f32) + inbox[at, span, :].astype(f32)).astype(bf16)
+                return carry
+
+            lax.fori_loop(0, mine.shape[1] // block, add, 0)
+        for cp in copies[2]:
+            cp.start()
+
+    def group_second(copies, mine, following, total_ref):
+        block = min(64, mine.shape[1])
         for which in range(2):
+            copies[2][which].wait_recv()
 
             def add(i, carry, which=which):
-                at = pl.ds(pl.multiple_of(i * block, block), block)
-                total = mine[which, at, :].astype(f32)
-                for k in range(n_dp - 1):
-                    total = total + inbox[k, which, at, :].astype(f32)
-                total_ref[which, at, :] = total.astype(bf16)
+                span = pl.ds(pl.multiple_of(i * block, block), block)
+                kept = mine[which * 2 + bits[1 - which], span, :].astype(f32)
+                total_ref[which, span, :] = (kept + following[which, span, :].astype(f32)).astype(bf16)
                 return carry
 
-            lax.fori_loop(0, part // block, add, 0)
+            lax.fori_loop(0, mine.shape[1] // block, add, 0)
 
     for c in range(chunks):
         row_stage(c)
         if c >= 1:
             t_stage(c - 1)
     t_stage(chunks - 1)
-    group_stage(down_copies, down_own, down_in, down_sum)
+    group_first(down_copies, down_own, down_in)
+    group_first(qkv_copies, qkv_own, qkv_in)
+    group_second(down_copies, down_own, down_next, down_sum)
     owner_start(0, down_sum, down_late)
-    group_stage(qkv_copies, qkv_own, qkv_in, qkv_sum)
+    group_second(qkv_copies, qkv_own, qkv_next, qkv_sum)
     owner_start(1, qkv_sum, qkv_late)
     for c in range(chunks):
         zh_copies[c].wait_recv()
@@ -1305,7 +1331,9 @@
     owner_end(2, up_ref, up_late, up_stay, up_out)
     owner_end(0, down_sum, down_late, down_sum.at[r], down_out)
     owner_end(1, qkv_sum, qkv_late, qkv_sum.at[r], qkv_out)
-    for cp in rows_copies + down_copies[1] + qkv_copies[1] + list(t_copies.values()) + zh_copies:
+    for cp in down_copies[1] + qkv_copies[1] + down_copies[2] + qkv_copies[2]:
+        cp.wait_send()
+    for cp in rows_copies + list(t_copies.values()) + zh_copies:
         cp.wait_send()
 
 
@@ -1325,8 +1353,9 @@
     sums = []
     for shape in (down_shape, qkv_shape):
         sums += [
+            pltpu.VMEM((4, *shape), bf16),
+            pltpu.VMEM((4, *shape), bf16),
             pltpu.VMEM((2, *shape), bf16),
-            pltpu.VMEM((n_dp - 1, 2, *shape), bf16),
             pltpu.VMEM((2, *shape), bf16),
             pltpu.VMEM((2, *shape), bf16),
         ]
@@ -1357,9 +1386,9 @@
             dma((chunks, 2, tp)),
             dma((chunks,)),
             dma((chunks,)),
-            dma((2, 2)),
-            dma((2, n_dp, 2)),
-            dma((2, n_dp, 2)),
+            dma((2, 4)),
+            dma((2, 6)),
+            dma((2, 6)),
             dma(()),
             dma((3, 3)),
             dma((3, 3)),
@@ -1485,6 +1514,13 @@
     att, up_two, gate_pieces[3], gate_pieces[5] = tie(att, up_two, gate_pieces[3], gate_pieces[5])
     up_one_x, up_two_y = swap_bit(up_one, "dp", 1), swap_bit(up_two, "dp", 2)
 
+    def data_sums(grad):
+        half = grad.shape[0] // 2
+        return [
+            lax.psum_scatter(grad[i * half : (i + 1) * half], "dp", scatter_dimension=0, tiled=True)
+            for i in range(2)
+        ]
+
     def to_tokens(vals):
         got = lax.all_to_all(vals.reshape(group, mine, col_width), ("row", "zl"), 0, 0)
         return got.transpose(1, 0, 2).reshape(mine, width)
@@ -1545,19 +1581,14 @@
     grad_att = to_heads(datt)
     grad_gate_w = matmul(h_full, grad_gate, TN).astype(bf16)
     grad_up_w = matmul(h_full, grad_up, TN).astype(bf16)
-    grad_att, grad_gate_w, grad_up_w = tie(grad_att, grad_gate_w, grad_up_w)
+    gate_sums = data_sums(grad_gate_w)
+    grad_att, grad_up_w = tie(grad_att, grad_up_w)
+    up_sums = data_sums(grad_up_w)
     grad_down_w = matmul(hidden, dm_full, TN).astype(bf16)
     grad_out = matmul(att_tok, grad_a, TN).astype(bf16)
 
     dqt, dk, dv = attend_back(query, key, key_t, value, grad_att, att, log_total, ends)
     weighted, inner, grad_head = unturn(dqt, dk, qkv, inv_scale, gains, cos_two, sin_two)
-    def data_sums(grad):
-        half = grad.shape[0] // 2
-        return [
-            lax.psum_scatter(grad[i * half : (i + 1) * half], "dp", scatter_dimension=0, tiled=True)
-            for i in range(2)
-        ]
-
     def owner_parts(pieces):
         keep = jnp.where(r == 0, pieces[0], pieces[1])
         give = jnp.where(r == 0, pieces[1], pieces[0])
@@ -1569,8 +1600,7 @@
             lax.ppermute(give, axes, [(0, 2), (3, 1)]),
         ]
 
-    gate_parts = owner_parts(data_sums(grad_gate_w))
-    up_sums = data_sums(grad_up_w)
+    gate_parts = owner_parts(gate_sums)
     inner = (small_sum(inner.T, ("row", "zl")) / width).T
     cube = inv_scale * inv_scale * inv_scale * inner
     dqkv = jnp.concatenate(

time: 1330 us -> 1290 us (0.970)
  waiting for transfers between devices: 129 us -> 106 us
  starting transfers between devices: 72.2 us -> 49.9 us
    reduce_scatter x4, waiting for transfers between devices: 64.1 us -> 0.03 us  [data_sums(): lax.psum_scatter(grad[i * half:(i + 1) * half], 'dp', scatter_dimension=0...]
    ppermute x1, waiting for transfers between devices: 0.01 us -> 23.6 us  [owner_parts(): lax.ppermute(keep, axes, [(1, 0), (2, 3)])]
    ppermute x17, starting transfers between devices: 43 us -> 21.4 us  [swap_bit(): lax.ppermute(piece, axis, [(i, i ^ bit) for i in range(lax.axis_size(axis...]
  transfers between devices with their start and end apart: 37 -> 37, of which waited for: 10 -> 11; matrix products, arithmetic and copies ran while one was open for 23% -> 23% of each run, Pallas kernels for 47% -> 48%
where the time goes in v4:
time: 1290 us; the launch traced here: 1280 us
  Pallas kernels  753 us (58%)
  matrix products  151 us (12%)
  other arithmetic  114 us (9%)
  waiting for transfers between devices  106 us (8%)
  local copies, waits for them, and re-layouts  94.5 us (7%)
  starting transfers between devices  49.9 us (4%)
  between operations  15 us (1%)
    pallas_call x3, Pallas kernels, tile_call(): pl.pallas_call(functools.partial(tile_kernel, job, tp, chunks), in_specs=...  300 us
    pallas_call x1, Pallas kernels, last_sums(): pl.pallas_call(functools.partial(last_kernel, chunks), in_specs=[anywhere...  199 us
    pallas_call x1, Pallas kernels, first_gather(): pl.pallas_call(functools.partial(gather_kernel, chunks), in_specs=[anywhe...  160 us
    dot_general x9, matrix products, matmul(): return lax.dot_general(left, right, dims, preferred_element_type=f32)  151 us
    pallas_call x1, Pallas kernels, attend_back(): pl.pallas_call(functools.partial(attend_back_kernel, docs, block), grid_s...  37.4 us
    unnamed x123, local copies, waits for them, and re-layouts  35.7 us
    ppermute x4, waiting for transfers between devices, swap(): return lax.ppermute(piece, axis, [(0, 1), (1, 0)])  31.6 us
    pallas_call x1, Pallas kernels, attend(): pl.pallas_call(functools.partial(attend_kernel, docs, block), grid_spec=p...  29.9 us
  transfers between devices with their start and end apart: 37, of which 11 were waited for; matrix products, arithmetic and copies ran while one was open for 23% of the time, Pallas kernels for 48%

profile of v4, /device:TPU:0, one launch (start us, length us, event | category | flops | bytes accessed | tf_op | source)
XLA Modules:
  0.0 1283.4 jit_solution(9005647764755504272)
XLA Ops:
  9.1 4.9 convert.8
  14.7 3.6 dynamic-slice_convert_fusion.1
  20.3 160.4 %first_gather.1 = (bf16[8,2048,256]{2,1,0:T(8,128)(2,1)}, bf16[2048,1536]{1,0:T(8,128)(2,1)}, f32[8,16,128]{2,1,0:T(8,128)}, bf16[256,1536]{1,0:T(8,128)(2,1)}, bf16[256,2048]{1,0:T(8,128)(2,1)}) custom-call(bf16[4096,256]{1,0:T(8,128)(2,1)} %tok_ref.1, bf16[1024,1536]{1,0:T(8,128)(2,1)} %pad_maximum_fusion.1.low_ref, f32[16,128]{1,0:T(8,128)} %bitcast.160, ...), custom_call_target="tpu_custom_call" | custom-call | bytes 25165824 | tf_op jit(solution)/shard_map/first_gather/pallas_call | solution.py:295
  182.8 8.4 copy.134
  191.2 17.5 %fusion.35.qkv_ref = f32[2048,1536]{1,0:T(8,128)S(1)} fusion(bf16[2048,2048]{1,0:T(8,128)(2,1)} %bitcast.122, bf16[2048,1536]{1,0:T(8,128)(2,1)} %get-tuple-element.142), kind=kOutput, calls=%fused_computation.120 | convolution fusion | flops 12884901888 | bytes 27262976 | tf_op jit(solution)/shard_map/dot_general | solution.py:1435
  215.3 3.9 fusion.11
  220.5 2.6 collective-permute-done.2
  225.8 12.8 %collective-permute-done.3.refs_4_ = bf16[256,1024]{1,0:T(8,128)(2,1)} collective-permute-done((bf16[256,1024]{1,0:T(8,128)(2,1)}, bf16[256,1024]{1,0:T(8,128)(2,1)}, u32[]{:S(2)}, u32[]{:S(2)}) %collective-permute-start.3) | collective-permute-done | bytes 524320 | tf_op jit(solution)/shard_map/ppermute | solution.py:42
  239.9 12.1 prepare.1
  260.8 2.9 collective-permute-start.5
  264.0 31.6 %collective-permute-done.refs_9_ = bf16[256,1024]{1,0:T(8,128)(2,1)S(1)} collective-permute-done((bf16[256,1024]{1,0:T(8,128)(2,1)S(1)}, bf16[256,1024]{1,0:T(8,128)(2,1)S(1)}, u32[]{:S(2)}, u32[]{:S(2)}) %collective-permute-start) | collective-permute-done | bytes 524320 | tf_op jit(solution)/shard_map/ppermute | solution.py:33
  298.0 29.9 %attend.1 = (bf16[2048,512]{1,0:T(8,128)(2,1)S(1)}, f32[4,1,2048]{2,1,0:T(1,128)S(1)}) custom-call(s32[4]{0:T(128)S(1)} %bitcast.117, bf16[2048,512]{1,0:T(8,128)(2,1)S(1)} %copy-done.8, bf16[2048,512]{1,0:T(8,128)(2,1)} %get-tuple-element.98.k_ref, bf16[512,2048]{1,0:T(8,128)(2,1)} %get-tuple-element.99.vt_ref), custom_call_target="tpu_custom_call" | custom-call | flops 4294967296 | bytes 8388608 | tf_op jit(solution)/shard_map/attend/pallas_call | solution.py:384
  327.9 2.6 copy.111
  330.5 4.5 all-to-all-start
  337.1 2.7 dynamic-slice_convert_fusion
  339.8 6.2 convert_element_type.148.refs_1_
  346.0 6.3 convert_element_type.149.refs_8_
  352.4 2.6 convert_element_type.151.refs_1_
  356.5 21.8 %all-to-all-done = bf16[4,512,512]{1,2,0:T(8,128)(2,1)} async-done(((bf16[4,512,512]{1,2,0:T(8,128)(2,1)}), bf16[4,512,512]{1,2,0:T(8,128)(2,1)}, u32[]{:S(2)}, u32[]{:S(2)}) %all-to-all-start) | async-done | bytes 2097184 | tf_op jit(solution)/shard_map/all_to_all | solution.py:1525
  381.5 10.6 multiply_reduce_fusion.5
  392.1 3.6 all-to-all-start.2
  395.8 4.9 fusion.refs_0_
  400.7 3.7 collective-permute-done.10.refs_12_
  406.5 99.1 %gate_up.1 = (bf16[2048,2048]{1,0:T(8,128)(2,1)}, bf16[2048,2048]{1,0:T(8,128)(2,1)}, bf16[2048,2048]{1,0:T(8,128)(2,1)}, bf16[2048,2048]{1,0:T(8,128)(2,1)}, bf...) custom-call(bf16[512,2048]{1,0:T(8,128)(2,1)} %fusion.refs_0_, ...), custom_call_target="tpu_custom_call" | custom-call | flops 34359738368 | bytes 33554432 | tf_op jit(solution)/shard_map/gate_up/pallas_call | solution.py:1023
  505.6 65.3 %down.1 = (bf16[2048,2048]{1,0:T(8,128)(2,1)}, f32[512,2048]{1,0:T(8,128)}) custom-call(bf16[2048,2048]{1,0:T(8,128)(2,1)} %get-tuple-element.143.refs_0_, bf16[2048,1024]{1,0:T(8,128)(2,1)} %convert_element_type.151.refs_1_, bf16[2048,1024]{1,0:T(8,128)(2,1)} %get-tuple-element.118.refs_2_), custom_call_target="tpu_custom_call" | custom-call | flops 17179869184 | bytes 33554432 | tf_op jit(solution)/shard_map/down/pallas_call | solution.py:1023
  570.9 2.5 multiply_reduce_fusion.4
  574.4 3.2 copy-done.17
  579.8 4.6 subtract_convert_fusion.3
  584.3 135.3 %feed_back.1 = (bf16[2048,2048]{1,0:T(8,128)(2,1)}, bf16[2048,2048]{1,0:T(8,128)(2,1)}, bf16[2048,2048]{1,0:T(8,128)(2,1)}, f32[512,2048]{1,0:T(8,128)}) custom-call(bf16[512,2048]{1,0:T(8,128)(2,1)} %get-tuple-element.264.refs_0_, bf16[2048,2048]{1,0:T(8,128)(2,1)} %get-tuple-element.124.refs_1_, bf16[2048,2048]{1,0:T(8,128)(2,1)} %get-tuple-element.125.refs_2_, ...), custom_call_target="tpu_custom_call" | custom-call | flops 51539607552 | bytes 33554432 | tf_op jit(solution)/shard_map/feed_back/pallas_call | solution.py:1023
  719.7 6.2 multiply_reduce_fusion.1
  728.0 9.5 convolution_convert_fusion.6
  737.6 20.1 %convolution_convert_fusion.3 = bf16[2048,2048]{1,0:T(8,128)(2,1)S(1)} fusion(bf16[2048,2048]{1,0:T(8,128)(2,1)S(1)} %bitcast.170, bf16[2048,2048]{1,0:T(8,128)(2,1)} %get-tuple-element.141), kind=kOutput, calls=%fused_computation.4 | convolution fusion | flops 17184063488 | bytes 25165824 | tf_op jit(solution)/shard_map/dot_general | solution.py:1435
  757.7 3.7 fusion.30
  763.5 3.7 all-to-all-start.3
  767.3 23.8 %convolution_convert_fusion.4 = bf16[2048,2048]{1,0:T(8,128)(2,1)} fusion(bf16[2048,2048]{1,0:T(8,128)(2,1)} %get-tuple-element.132, bf16[2048,2048]{1,0:T(8,128)(2,1)} %get-tuple-element.133), kind=kOutput, calls=%fused_computation.5 | convolution fusion | flops 17184063488 | bytes 25165824 | tf_op jit(solution)/shard_map/dot_general | solution.py:1435
  792.9 7.0 fusion.29
  804.2 4.4 all-to-all-start.1
  808.6 6.8 convolution_convert_fusion
  815.4 3.1 constant_dynamic-slice_fusion.2
  820.3 25.0 %convolution_convert_fusion.1.down_ref = bf16[2048,2048]{1,0:T(8,128)(2,1)} fusion(bf16[2048,2048]{1,0:T(8,128)(2,1)} %get-tuple-element.143.refs_0_, bf16[2048,2048]{1,0:T(8,128)(2,1)} %get-tuple-element.144), kind=kOutput, calls=%fused_computation.2 | convolution fusion | flops 17184063488 | bytes 25165824 | tf_op jit(solution)/shard_map/dot_general | solution.py:1435
  845.3 37.4 %attend_back.1 = (f32[512,2048]{1,0:T(8,128)}, f32[2048,512]{1,0:T(8,128)}, bf16[2048,512]{1,0:T(8,128)(2,1)S(1)}) custom-call(s32[4]{0:T(128)S(1)} %bitcast.118, bf16[2048,512]{1,0:T(8,128)(2,1)S(1)} %copy-done.9, bf16[2048,512]{1,0:T(8,128)(2,1)} %get-tuple-element.98.k_ref, bf16[512,2048]{1,0:T(8,128)(2,1)} %get-tuple-element.120.kt_ref, ...), custom_call_target="tpu_custom_call" | custom-call | flops 10737418240 | bytes 20971520 | tf_op jit(solution)/shard_map/attend_back/pallas_call | solution.py:476
  882.7 14.3 %unturn.1 = (f32[2048,1024]{1,0:T(8,128)}, f32[2048,2]{1,0:T(8,128)S(1)}, f32[2,512]{1,0:T(2,128)S(1)}) custom-call(f32[512,2048]{1,0:T(8,128)} %get-tuple-element.136.dqt_ref, f32[2048,512]{1,0:T(8,128)} %get-tuple-element.137.dk_ref, f32[2048,1536]{1,0:T(8,128)} %copy-done.12, f32[2048,2]{1,0:T(8,128)S(1)} %copy-done.1, f32[2,512]{1,0:T(2,128)S(1)} %copy-done.6, ...), custom_call_target="tpu_custom_call" | custom-call | flops 20971520 | bytes 25165824 | tf_op jit(solution)/shard_map/unturn/pallas_call | solution.py:599
  908.2 5.6 add_convert_fusion
  917.4 8.7 subtract_convert_fusion.1
  929.7 5.9 collective-permute-start.17
  936.9 18.6 %convolution_convert_fusion.5.qkv_ref = bf16[2048,1536]{1,0:T(8,128)(2,1)} fusion(bf16[2048,2048]{1,0:T(8,128)(2,1)} %bitcast.125, bf16[2048,512]{1,0:T(8,128)(2,1)S(1)} %copy-done.11, bf16[2048,512]{1,0:T(8,128)(2,1)} %get-tuple-element.259, bf16[2048,512]{1,0:T(8,128)(2,1)S(1)} %copy-done.25), kind=kOutput, calls=%fused_computation.6 | convolution fusion | flops 12906921984 | bytes 20971520 | tf_op jit(solution)/shard_map/dot_general | solution.py:1435
  955.5 23.6 %collective-permute-done.15 = bf16[256,2048]{1,0:T(8,128)(2,1)S(1)} collective-permute-done((bf16[256,2048]{1,0:T(8,128)(2,1)S(1)}, bf16[256,2048]{1,0:T(8,128)(2,1)S(1)}, u32[]{:S(2)}, u32[]{:S(2)}) %collective-permute-start.15) | collective-permute-done | bytes 1048608 | tf_op jit(solution)/shard_map/ppermute | solution.py:1598
  980.0 19.2 %convolution_convert_fusion.2 = bf16[2048,2048]{1,0:T(8,128)(2,1)} fusion(bf16[2048,1536]{1,0:T(8,128)(2,1)} %get-tuple-element.142, bf16[2048,512]{1,0:T(8,128)(2,1)S(1)} %copy-done.11, bf16[2048,512]{1,0:T(8,128)(2,1)} %get-tuple-element.259, bf16[2048,512]{1,0:T(8,128)(2,1)} %get-tuple-element.258), kind=kOutput, calls=%fused_computation.3 | convolution fusion | flops 12907970560 | bytes 20971520 | tf_op jit(solution)/shard_map/dot_general | solution.py:1435
  999.2 5.1 fusion.4.dx_ref
  1004.3 3.1 pad_maximum_fusion.4.up_ref
  1007.4 199.4 %last_sums.1 = (f32[4096,256]{1,0:T(8,128)}, f32[512,1024]{1,0:T(8,128)}, f32[256,1536]{1,0:T(8,128)}, f32[256,2048]{1,0:T(8,128)}) custom-call(bf16[2048,2048]{1,0:T(8,128)(2,1)} %fusion.4.dx_ref, bf16[2048,2048]{1,0:T(8,128)(2,1)} %convolution_convert_fusion.1.down_ref, bf16[2048,1536]{1,0:T(8,128)(2,1)} %convolution_convert_fusion.5.qkv_ref, ...), custom_call_target="tpu_custom_call" | custom-call | bytes 33554432 | tf_op jit(solution)/shard_map/last_sums/pallas_call | solution.py:1362
  1210.7 3.0 copy.124
  1213.7 3.2 copy.122
  1216.9 3.2 copy.113
  1221.8 6.5 multiply_subtract_fusion.2
  1228.4 7.7 collective-permute-start.21
  1236.1 7.6 multiply_subtract_fusion.1
  1244.0 5.9 multiply_subtract_fusion
  1249.9 3.2 copy.123
  1255.0 5.4 multiply_subtract_fusion.3
  1260.4 3.2 copy.127
  1263.6 3.1 copy.128
  1269.7 2.5 multiply_subtract_fusion.4
  1272.2 4.5 copy.149
  (249 shorter events, 85.3 us)
Async XLA Ops:
  7.2 175.5 %all-gather.8.cloned.1.call-start = ((), (), s32[]{:S(2)}) async-start(), calls=%async_computation.16 | async-start | bytes 1310720 | tf_op jit(solution)/shard_map/all_gather | solution.py:1493
  9.1 245.1 %all-gather.10.cloned.1.call-start = ((), (), s32[]{:S(2)}) async-start(), calls=%async_computation.17 | async-start | bytes 5242880 | tf_op jit(solution)/shard_map/all_gather | solution.py:1494
  182.8 198.8 %all-gather.6.cloned.1.call-start = ((), (), s32[]{:S(2)}) async-start(), calls=%async_computation.10 | async-start | bytes 12582912 | tf_op jit(solution)/shard_map/all_gather | solution.py:1511
  208.7 10.7 copy-start.12
  209.4 9.9 collective-permute-start.1
  212.5 26.1 %collective-permute-start.3 = (bf16[256,1024]{1,0:T(8,128)(2,1)}, bf16[256,1024]{1,0:T(8,128)(2,1)}, u32[]{:S(2)}, u32[]{:S(2)}) collective-permute-start(bf16[256,1024]{1,0:T(8,128)(2,1)} %get-tuple-element.272.refs_2_), channel_id=1, source_target_pairs={{0,8},{8,0},{16,24},{24,16},{1,9},{9,1},{17,25},{25,17},{2,10},{10... | collective-permute-start | bytes 1572872 | tf_op jit(solution)/shard_map/ppermute | solution.py:42
  213.8 26.1 %collective-permute-start.4 = (bf16[256,1024]{1,0:T(8,128)(2,1)}, bf16[256,1024]{1,0:T(8,128)(2,1)}, u32[]{:S(2)}, u32[]{:S(2)}) collective-permute-start(bf16[256,1024]{1,0:T(8,128)(2,1)} %get-tuple-element.271.refs_3_), channel_id=1, source_target_pairs={{0,16},{8,24},{16,0},{24,8},{1,17},{9,25},{17,1},{25,9},{2,18},{10... | collective-permute-start | bytes 1572872 | tf_op jit(solution)/shard_map/ppermute | solution.py:42
  219.3 3.8 collective-permute-start.2
  220.0 31.9 %copy-start.2 = (f32[2048,128]{1,0:T(8,128)}, f32[2048,128]{1,0:T(8,128)S(1)}, u32[]{:S(2)}) copy-start(f32[2048,128]{1,0:T(8,128)S(1)} %get-tuple-element.286.cos_ref) | copy-start | bytes 3145732
  220.1 31.8 %copy-start.5 = (f32[2,512]{1,0:T(2,128)}, f32[2,512]{1,0:T(2,128)S(1)}, u32[]{:S(2)}) copy-start(f32[2,512]{1,0:T(2,128)S(1)} %reshape_squeeze.3.gains_ref) | copy-start | bytes 12292
  254.3 6.6 copy-start.37
  256.6 71.3 %collective-permute-start.6 = (bf16[512,1024]{1,0:T(8,128)(2,1)}, bf16[512,1024]{1,0:T(8,128)(2,1)}, u32[]{:S(2)}, u32[]{:S(2)}) collective-permute-start(bf16[512,1024]{1,0:T(8,128)(2,1)} %pad_maximum_fusion.7), channel_id=1, source_target_pairs={{0,16},{8,24},{16,0},{24,8},{1,17},{9,25},{17,1},{25,9},{2,18},{10... | collective-permute-start | bytes 3145736 | tf_op jit(solution)/shard_map/ppermute | solution.py:42
  260.5 67.4 %collective-permute-start.7 = (bf16[512,1024]{1,0:T(8,128)(2,1)}, bf16[512,1024]{1,0:T(8,128)(2,1)}, u32[]{:S(2)}, u32[]{:S(2)}) collective-permute-start(bf16[512,1024]{1,0:T(8,128)(2,1)} %pad_maximum_fusion.8), channel_id=1, source_target_pairs={{0,8},{8,0},{16,24},{24,16},{1,9},{9,1},{17,25},{25,17},{2,10},{10... | collective-permute-start | bytes 3145736 | tf_op jit(solution)/shard_map/ppermute | solution.py:42
  260.8 34.8 %collective-permute-start = (bf16[256,1024]{1,0:T(8,128)(2,1)S(1)}, bf16[256,1024]{1,0:T(8,128)(2,1)S(1)}, u32[]{:S(2)}, u32[]{:S(2)}) collective-permute-start(bf16[256,1024]{1,0:T(8,128)(2,1)S(1)} %copy-done.37), channel_id=1, source_target_pairs={{0,2},{2,0},{1,3},{3,1},{4,6},{6,4},{5,7},{7,5},{8,10},{10,8},{9,1... | collective-permute-start | bytes 1572872 | tf_op jit(solution)/shard_map/ppermute | solution.py:33
  260.8 67.0 %collective-permute-start.5 = (bf16[256,1024]{1,0:T(8,128)(2,1)}, bf16[256,1024]{1,0:T(8,128)(2,1)}, u32[]{:S(2)}, u32[]{:S(2)}) collective-permute-start(bf16[256,1024]{1,0:T(8,128)(2,1)} %get-tuple-element.101), channel_id=1, source_target_pairs={{0,2},{2,0},{1,3},{3,1},{4,6},{6,4},{5,7},{7,5},{8,10},{10,8},{9,1... | collective-permute-start | bytes 1572872 | tf_op jit(solution)/shard_map/ppermute | solution.py:33
  330.5 47.8 %all-to-all-start = ((bf16[4,512,512]{1,2,0:T(8,128)(2,1)}), bf16[4,512,512]{1,2,0:T(8,128)(2,1)}, u32[]{:S(2)}, u32[]{:S(2)}) async-start(bf16[4,512,512]{1,2,0:T(8,128)(2,1)} %copy.111), calls=%async_computation | async-start | bytes 4194304 | tf_op jit(solution)/shard_map/all_to_all | solution.py:1525
  335.0 21.5 %collective-permute-start.8 = (bf16[256,1024]{1,0:T(8,128)(2,1)}, bf16[256,1024]{1,0:T(8,128)(2,1)S(1)}, u32[]{:S(2)}, u32[]{:S(2)}) collective-permute-start(bf16[256,1024]{1,0:T(8,128)(2,1)} %copy-done.38), channel_id=1, source_target_pairs={{0,8},{8,0},{16,24},{24,16},{1,9},{9,1},{17,25},{25,17},{2,10},{10... | collective-permute-start | bytes 1572872 | tf_op jit(solution)/shard_map/ppermute | solution.py:42
  335.1 21.4 %collective-permute-start.9 = (bf16[256,1024]{1,0:T(8,128)(2,1)}, bf16[256,1024]{1,0:T(8,128)(2,1)S(1)}, u32[]{:S(2)}, u32[]{:S(2)}) collective-permute-start(bf16[256,1024]{1,0:T(8,128)(2,1)} %collective-permute-done.5.refs_10_), channel_id=1, source_target_pairs={{0,16},{8,24},{16,0},{24,8},{1,17},{9,25},{17,1},{25,9},{2,18},{10... | collective-permute-start | bytes 1572872 | tf_op jit(solution)/shard_map/ppermute | solution.py:42
  339.8 60.9 %collective-permute-start.12 = (bf16[512,1024]{1,0:T(8,128)(2,1)}, bf16[512,1024]{1,0:T(8,128)(2,1)}, u32[]{:S(2)}, u32[]{:S(2)}) collective-permute-start(bf16[512,1024]{1,0:T(8,128)(2,1)} %dynamic-slice_convert_fusion), channel_id=1, source_target_pairs={{0,2},{2,0},{1,3},{3,1},{4,6},{6,4},{5,7},{7,5},{8,10},{10,8},{9,1... | collective-permute-start | bytes 3145736 | tf_op jit(solution)/shard_map/ppermute | solution.py:33
  339.8 12.5 slice-start
  346.0 6.3 slice-start.1
  355.0 23.3 %copy-start.39 = (bf16[256,1024]{1,0:T(8,128)(2,1)S(1)}, bf16[256,1024]{1,0:T(8,128)(2,1)}, u32[]{:S(2)}) copy-start(bf16[256,1024]{1,0:T(8,128)(2,1)} %copy-done.38) | copy-start | bytes 1572868
  356.5 35.6 %copy-start.40 = (bf16[256,1024]{1,0:T(8,128)(2,1)}, bf16[256,1024]{1,0:T(8,128)(2,1)S(1)}, u32[]{:S(2)}) copy-start(bf16[256,1024]{1,0:T(8,128)(2,1)S(1)} %collective-permute-done.8.refs_11_) | copy-start | bytes 1572868
  356.5 35.6 %copy-start.41 = (bf16[256,1024]{1,0:T(8,128)(2,1)}, bf16[256,1024]{1,0:T(8,128)(2,1)S(1)}, u32[]{:S(2)}) copy-start(bf16[256,1024]{1,0:T(8,128)(2,1)S(1)} %collective-permute-done.9.refs_13_) | copy-start | bytes 1572868
  379.3 25.0 %collective-permute-start.10 = (bf16[512,1024]{1,0:T(8,128)(2,1)}, bf16[512,1024]{1,0:T(8,128)(2,1)}, u32[]{:S(2)}, u32[]{:S(2)}) collective-permute-start(bf16[512,1024]{1,0:T(8,128)(2,1)} %pad_maximum_fusion.9), channel_id=1, source_target_pairs={{0,16},{8,24},{16,0},{24,8},{1,17},{9,25},{17,1},{25,9},{2,18},{10... | collective-permute-start | bytes 3145736 | tf_op jit(solution)/shard_map/ppermute | solution.py:42
  381.5 25.0 %collective-permute-start.11 = (bf16[512,1024]{1,0:T(8,128)(2,1)}, bf16[512,1024]{1,0:T(8,128)(2,1)}, u32[]{:S(2)}, u32[]{:S(2)}) collective-permute-start(bf16[512,1024]{1,0:T(8,128)(2,1)} %pad_maximum_fusion.10), channel_id=1, source_target_pairs={{0,8},{8,0},{16,24},{24,16},{1,9},{9,1},{17,25},{25,17},{2,10},{10... | collective-permute-start | bytes 3145736 | tf_op jit(solution)/shard_map/ppermute | solution.py:42
  392.1 181.4 %all-to-all-start.2 = ((bf16[8,512,256]{2,1,0:T(8,128)(2,1)}), bf16[8,512,256]{2,1,0:T(8,128)(2,1)S(1)}, u32[]{:S(2)}, u32[]{:S(2)}) async-start(bf16[8,512,256]{2,1,0:T(8,128)(2,1)} %bitcast.131), calls=%async_computation.2 | async-start | bytes 4194304 | tf_op jit(solution)/shard_map/all_to_all | solution.py:1542
  395.7 530.4 %reduce-scatter.11.cloned.1.call-start = ((), (), s32[]{:S(2)}) async-start(), calls=%async_computation.12 | async-start | bytes 5242880 | tf_op jit(solution)/shard_map/reduce_scatter | solution.py:1520
  719.7 6.2 copy-start.14
  725.9 11.7 slice-start.2
  728.0 9.6 copy-start.31
  728.0 9.6 slice-start.3
  761.4 164.7 %reduce-scatter.9.cloned.1.call-start = ((), (), s32[]{:S(2)}) async-start(), calls=%async_computation.11 | async-start | bytes 5242880 | tf_op jit(solution)/shard_map/reduce_scatter | solution.py:1520
  763.5 29.3 %all-to-all-start.3 = ((bf16[4,512,512]{2,1,0:T(8,128)(2,1)}), bf16[4,512,512]{2,1,0:T(8,128)(2,1)S(1)}, u32[]{:S(2)}, u32[]{:S(2)}) async-start(bf16[4,512,512]{2,1,0:T(8,128)(2,1)} %bitcast.111), calls=%async_computation.3 | async-start | bytes 4194304 | tf_op jit(solution)/shard_map/all_to_all | solution.py:1530
  767.2 237.1 %reduce-scatter.15.cloned.1.call-start = ((), (), s32[]{:S(2)}) async-start(), calls=%async_computation.14 | async-start | bytes 5242880 | tf_op jit(solution)/shard_map/reduce_scatter | solution.py:1520
  792.9 7.0 copy-start.27
  799.9 204.4 %reduce-scatter.13.cloned.1.call-start = ((), (), s32[]{:S(2)}) async-start(), calls=%async_computation.13 | async-start | bytes 5242880 | tf_op jit(solution)/shard_map/reduce_scatter | solution.py:1520
  804.2 412.7 %all-to-all-start.1 = ((bf16[8,512,256]{2,1,0:T(8,128)(2,1)}), bf16[8,512,256]{2,1,0:T(8,128)(2,1)}, u32[]{:S(2)}, u32[]{:S(2)}) async-start(bf16[8,512,256]{2,1,0:T(8,128)(2,1)} %bitcast.130), calls=%async_computation.1 | async-start | bytes 4194304 | tf_op jit(solution)/shard_map/all_to_all | solution.py:1563
  808.5 427.5 %reduce-scatter.19.cloned.1.call-start = ((), (), s32[]{:S(2)}) async-start(), calls=%async_computation.18 | async-start | bytes 5242880
  820.0 88.3 %collective-permute-start.18 = (bf16[2048,1024]{1,0:T(8,128)(2,1)}, bf16[2048,1024]{1,0:T(8,128)(2,1)}, u32[]{:S(2)}, u32[]{:S(2)}) collective-permute-start(bf16[2048,1024]{1,0:T(8,128)(2,1)} %constant_dynamic-slice_fusion.2), channel_id=1, source_target_pairs={{0,4},{4,0},{1,5},{5,1},{2,6},{6,2},{3,7},{7,3},{8,12},{12,8},{9,1... | collective-permute-start | bytes 12582920 | tf_op jit(solution)/shard_map/ppermute | solution.py:33
  820.3 25.0 %copy-start.9 = (bf16[2048,512]{1,0:T(8,128)(2,1)S(1)}, bf16[2048,512]{1,0:T(8,128)(2,1)}, u32[]{:S(2)}) copy-start(bf16[2048,512]{1,0:T(8,128)(2,1)} %copy-done.7) | copy-start | bytes 6291460
  845.3 37.4 %copy-start.3 = (f32[2048,128]{1,0:T(8,128)S(1)}, f32[2048,128]{1,0:T(8,128)}, u32[]{:S(2)}) copy-start(f32[2048,128]{1,0:T(8,128)} %copy-done.2) | copy-start | bytes 3145732
  845.3 37.4 %copy-start.6 = (f32[2,512]{1,0:T(2,128)S(1)}, f32[2,512]{1,0:T(2,128)}, u32[]{:S(2)}) copy-start(f32[2,512]{1,0:T(2,128)} %copy-done.5) | copy-start | bytes 12292
  882.7 14.3 %copy-start.10 = (bf16[2048,512]{1,0:T(8,128)(2,1)}, bf16[2048,512]{1,0:T(8,128)(2,1)S(1)}, u32[]{:S(2)}) copy-start(bf16[2048,512]{1,0:T(8,128)(2,1)S(1)} %get-tuple-element.140) | copy-start | bytes 6291460
  897.0 6.3 copy-start.42
  897.3 1.2 collective-permute-start.13
  901.6 3.8 collective-permute-start.14
  916.4 353.3 %reduce-scatter.17.cloned.1.call-start = ((), (), s32[]{:S(2)}) async-start(), calls=%async_computation.15 | async-start | bytes 1310720 | tf_op jit(solution)/shard_map/reduce_scatter | solution.py:1632
  926.1 10.8 copy-start.11
  926.2 10.7 copy-start.25
  928.0 52.0 %collective-permute-start.16 = (bf16[256,2048]{1,0:T(8,128)(2,1)S(1)}, bf16[256,2048]{1,0:T(8,128)(2,1)}, u32[]{:S(2)}, u32[]{:S(2)}) collective-permute-start(bf16[256,2048]{1,0:T(8,128)(2,1)S(1)} %get-tuple-element.269), channel_id=1, source_target_pairs={{2,4},{4,2},{3,5},{5,3},{10,12},{12,10},{11,13},{13,11},{18,20},{2... | collective-permute-start | bytes 3145736 | tf_op jit(solution)/shard_map/ppermute | solution.py:1599
  929.7 50.4 %collective-permute-start.17 = (bf16[256,2048]{1,0:T(8,128)(2,1)S(1)}, bf16[256,2048]{1,0:T(8,128)(2,1)}, u32[]{:S(2)}, u32[]{:S(2)}) collective-permute-start(bf16[256,2048]{1,0:T(8,128)(2,1)S(1)} %get-tuple-element.269), channel_id=1, source_target_pairs={{0,4},{6,2},{1,5},{7,3},{8,12},{14,10},{9,13},{15,11},{16,20},{22,... | collective-permute-start | bytes 3145736 | tf_op jit(solution)/shard_map/ppermute | solution.py:1600
  935.6 43.5 %collective-permute-start.15 = (bf16[256,2048]{1,0:T(8,128)(2,1)S(1)}, bf16[256,2048]{1,0:T(8,128)(2,1)S(1)}, u32[]{:S(2)}, u32[]{:S(2)}) collective-permute-start(bf16[256,2048]{1,0:T(8,128)(2,1)S(1)} %get-tuple-element.148), channel_id=1, source_target_pairs={{2,0},{4,6},{3,1},{5,7},{10,8},{12,14},{11,9},{13,15},{18,16},{20,... | collective-permute-start | bytes 3145736 | tf_op jit(solution)/shard_map/ppermute | solution.py:1598
  1206.8 13.3 %collective-permute-start.19 = (f32[4,2048]{1,0:T(4,128)S(1)}, f32[4,2048]{1,0:T(4,128)S(1)}, u32[]{:S(2)}, u32[]{:S(2)}) collective-permute-start(f32[4,2048]{1,0:T(4,128)S(1)} %pad_maximum_fusion.11), channel_id=1, source_target_pairs={{0,8},{8,0},{16,24},{24,16},{1,9},{9,1},{17,25},{25,17},{2,10},{10... | collective-permute-start | bytes 98312 | tf_op jit(solution)/shard_map/ppermute | solution.py:42
  1213.7 8.1 copy-start.23
  1220.1 8.2 collective-permute-start.20
  1228.4 15.4 %collective-permute-start.21 = (f32[4,2048]{1,0:T(4,128)S(1)}, f32[4,2048]{1,0:T(4,128)S(1)}, u32[]{:S(2)}, u32[]{:S(2)}) collective-permute-start(f32[4,2048]{1,0:T(4,128)S(1)} %add.295), channel_id=1, source_target_pairs={{0,4},{4,0},{1,5},{5,1},{2,6},{6,2},{3,7},{7,3},{8,12},{12,8},{9,1... | collective-permute-start | bytes 98312 | tf_op jit(solution)/shard_map/ppermute | solution.py:42
  1236.1 7.9 copy-start.28
  1236.1 7.9 copy-start.29
  1236.1 7.9 copy-start.30
  1243.8 9.3 collective-permute-start.22
  1253.1 15.2 %collective-permute-start.23 = (f32[4,2048]{1,0:T(4,128)S(1)}, f32[4,2048]{1,0:T(4,128)S(1)}, u32[]{:S(2)}, u32[]{:S(2)}) collective-permute-start(f32[4,2048]{1,0:T(4,128)S(1)} %add.297), channel_id=1, source_target_pairs={{0,1},{1,0},{2,3},{3,2},{4,5},{5,4},{6,7},{7,6},{8,9},{9,8},{10,11... | collective-permute-start | bytes 98312 | tf_op jit(solution)/shard_map/ppermute | solution.py:42
  1260.4 6.3 copy-start.22
  1263.6 6.1 copy-start.35
  (29 other events, 103.7 us)
Sparse Core Ops, SparseCore 0:
  10.2 54.5 all-gather.7
  182.9 62.8 all-gather.9
  254.4 18.0 all-gather.5
  761.6 50.1 reduce-scatter.10
  814.8 52.6 reduce-scatter.8
  870.3 52.7 reduce-scatter.14
  926.4 52.6 reduce-scatter.12
  982.6 71.7 reduce-scatter.18
  1236.2 26.4 reduce-scatter.16
